TPU v7x, 32 devices: a whole 2x2x4 slice. The times are simulated.
32 devices in a mesh: member: 2 (over x), band: 16 (over z, y, core).
Axes of the slice: x: 2, y: 2, z: 4, core: 2. Of those that a mesh axis runs over, the one named last changes fastest.
Arguments:
- state: float32 [14, 6, 2048, 1024], P('member', None, 'band'), parts along dimension 0, may hold values from -6 to 6
- courant_lon: float32 [4096, 1024], P(('member', 'band')), parts along dimension 0, may hold values from 0.05 to 0.45
- courant_lat: float32 [4096, 1024], P(('member', 'band')), parts along dimension 0, may hold values from 0.05 to 0.45
- reference_field: float32 [12, 2048, 1024], P('member', 'band'), parts along dimension 0, may hold values from -6 to 6
- nudge_rate: float32 [512], replicated, may hold values from 0.05 to 1
Outputs:
- new_state: float32 [14, 6, 2048, 1024], P('member', None, 'band'), parts along dimension 0
There are 2 independent parts, one for each index of `member`. A program takes and returns all parts, laid end to end along the dimension named above; an argument that names none is the same for every part. Nothing has to cross between parts.
All inputs are finite; a program needn't handle non-finite values.
Results may differ from a plain program's by a relative error of at most 0.0003.
Values sent between devices are 32-bit elements; how exact they have to be, the bound alone decides.
No kernel may reach another device: no remote copies, remote signals or barrier semaphores. Data moves between devices by JAX's collectives and lax.ppermute only.
A program may use at most 256 MiB of HBM per device.

v0:
```python
import math

import jax
import jax.numpy as jnp
from jax import lax
from jax.sharding import PartitionSpec as P

STEPS = 2


highest = lax.Precision.HIGHEST


def passed_along(value, axis, by):
    peers = lax.axis_size(axis)
    return lax.ppermute(value, axis, [(i, (i + by) % peers) for i in range(peers)])


def latitude_terms(lat_total):
    centres = (jnp.arange(lat_total).astype(jnp.float32) + 0.5) * (math.pi / lat_total)
    return (jnp.cos(centres), jnp.log(jnp.sin(centres)), jnp.sin(centres) * (math.pi / lat_total))


def norm_table(wave_total):
    orders = jnp.arange(1, wave_total).astype(jnp.float32)
    terms = jnp.log((2.0 * orders + 1.0) / (2.0 * orders))
    return jnp.concatenate([jnp.zeros((1,), jnp.float32), jnp.cumsum(terms)])


def start_value(wave_ids, log_sin, norms):
    matches = wave_ids[:, None] == jnp.arange(norms.shape[0])[None, :]
    log_norm = jnp.sum(jnp.where(matches, norms[None, :], 0.0), axis=1)
    orders = wave_ids.astype(jnp.float32)
    return 0.5 * log_norm[:, None] + orders[:, None] * log_sin[None, :] - 0.5 * math.log(2.0)


def legendre_table(wave_rows, offset_rows, upper_rows, starts, cosines):

    def advance(carry, inputs):
        earlier, latest, deficit = carry
        wave_now, offset_now, upper_now = inputs
        orders = wave_now.astype(jnp.float32)[:, None]
        degree = (wave_now + offset_now).astype(jnp.float32)[:, None]
        factor_now = jnp.sqrt(
            (4.0 * degree * degree - 1.0) / jnp.maximum(degree * degree - orders * orders, 1.0)
        )
        below = degree - 1.0
        older_sq = jnp.where(
            offset_now[:, None] >= 2,
            (4.0 * below * below - 1.0) / jnp.maximum(below * below - orders * orders, 1.0),
            1.0,
        )
        factor_old = jnp.where(offset_now[:, None] >= 2, factor_now / jnp.sqrt(older_sq), 0.0)
        log_start = jnp.where(upper_now[:, None] == 1, starts[:, 1], starts[:, 0])
        clamped = jnp.maximum(log_start, -80.0)
        fresh = offset_now[:, None] == 0
        recurred = factor_now * cosines[None, :] * latest - factor_old * earlier
        largest = jnp.maximum(jnp.abs(recurred), jnp.abs(latest))
        absorb = jnp.maximum(deficit, -jnp.log(jnp.maximum(largest, 1.0)))
        rescale = jnp.exp(absorb)
        next_latest = jnp.where(fresh, jnp.exp(clamped), recurred * rescale)
        next_earlier = jnp.where(fresh, jnp.zeros_like(latest), latest * rescale)
        next_deficit = jnp.where(fresh, log_start - clamped, deficit - absorb)
        result_row = next_latest * jnp.exp(next_deficit)
        return ((next_earlier, next_latest, next_deficit), result_row)

    zero_row = jnp.zeros_like(starts[:, 0])
    final_carry, rows = lax.scan(
        advance,
        (zero_row, zero_row, zero_row),
        (wave_rows.T, offset_rows.T, upper_rows.T),
        unroll=16,
    )
    return jnp.transpose(rows, (1, 0, 2))


def rate_lookup(degrees, rate_table):
    matches = degrees[..., None] == jnp.arange(rate_table.shape[0])
    return jnp.sum(jnp.where(matches, rate_table, 0.0), axis=-1)


def advect(cells, west_edge, lon_courant, lat_courant):
    west_cells = jnp.concatenate([west_edge, cells[:, :, :-1]], axis=2)
    south_cells = jnp.concatenate([jnp.zeros_like(cells[:, :, :, :1]), cells[:, :, :, :-1]], axis=3)
    return cells - lon_courant * (cells - west_cells) - lat_courant * (cells - south_cells)


def body(state, courant_lon, courant_lat, reference_field, nudge_rate):
    level_count = state.shape[1]
    lon_local = state.shape[2]
    lat_total = state.shape[3]
    band_count = lax.axis_size("band")
    band_place = lax.axis_index("band")
    lon_total = lon_local * band_count
    wave_total = nudge_rate.shape[0]
    wave_local = wave_total // band_count
    advected = state
    for turn_index in range(STEPS):
        west_column = passed_along(advected[:, :, -1:], "band", 1)
        advected = advect(advected, west_column, courant_lon, courant_lat)
    anomaly = reference_field - advected[0]
    lon_iota = jnp.arange(lon_total)
    wave_iota = jnp.arange(wave_total)
    phase = (lon_iota[:, None] * wave_iota[None, :] % lon_total).astype(jnp.float32) * (
        2.0 * math.pi / lon_total
    )
    cos_table = jnp.cos(phase)
    sin_table = jnp.sin(phase)
    forward = jnp.concatenate([cos_table, -sin_table], axis=1) / lon_total
    doubling = jnp.where(wave_iota == 0, 1.0, 2.0)[:, None]
    inverse = jnp.concatenate([cos_table.T * doubling, -sin_table.T * doubling], axis=0)
    fourier = jnp.einsum(
        "lij,ik->klj",
        lax.all_to_all(anomaly, "band", split_axis=2, concat_axis=1, tiled=True),
        forward,
        precision=highest,
    )
    spectrum = fourier.reshape(2, wave_total, level_count, fourier.shape[2])
    lat_local = spectrum.shape[3]
    cosines, log_sin, quad_weights = latitude_terms(lat_total)
    norms = norm_table(wave_total)
    wave_ids = band_place * wave_local + jnp.arange(wave_local)
    wave_rows = jnp.broadcast_to(wave_ids[:, None], (wave_local, wave_total))
    offset_rows = jnp.broadcast_to(jnp.arange(wave_total)[None, :], (wave_local, wave_total))
    initial = start_value(wave_ids, log_sin, norms)
    legendre = legendre_table(
        wave_rows, offset_rows, jnp.zeros_like(wave_rows), jnp.stack([initial, initial], 1), cosines
    )
    rate_rows = rate_lookup(wave_rows + offset_rows, nudge_rate)
    weighted = (
        lax.all_to_all(spectrum, "band", split_axis=1, concat_axis=3, tiled=True) * quad_weights
    )
    analysed = jnp.einsum("skj,cslj->skcl", legendre, weighted, precision=highest)
    scaled = analysed * rate_rows[:, :, None, None]
    waves_out = jnp.einsum("skj,skcl->cslj", legendre, scaled, precision=highest)
    gathered = lax.all_to_all(waves_out, "band", split_axis=3, concat_axis=1, tiled=True)
    level_part = gathered.shape[2]
    flattened = gathered.reshape(2 * wave_total, level_part, lat_local)
    band_increment = jnp.einsum("klj,ki->lij", flattened, inverse, precision=highest)
    increment = lax.all_to_all(band_increment, "band", split_axis=1, concat_axis=2, tiled=True)
    nudged = advected[0] + increment
    return jnp.concatenate([nudged[None], advected[1:]], axis=0)


def solution(mesh):
    placed = (
        P("member", None, "band", None),
        P(("member", "band"), None),
        P(("member", "band"), None),
        P("member", "band", None),
        P(),
    )
    return jax.shard_map(
        body, mesh=mesh, in_specs=placed, out_specs=P("member", None, "band", None), check_vma=False
    )
```

profile of v0, /device:TPU:15, one launch (start us, length us, event | category | flops | bytes accessed | tf_op | source)
XLA Modules:
  0.0 927.3 jit_solution(11728541990109933526)
XLA Ops:
  3.4 21.6 %copy.111 = f32[7,6,128,1024]{2,3,1,0:T(8,128)} copy(f32[7,6,128,1024]{3,2,1,0:T(8,128)} %param.7) | data formatting | bytes 44040192 | tf_op args[0]
  25.4 10.5 %copy.109 = f32[7,6,1,1024]{2,3,1,0:T(8,128)} copy(f32[7,6,1,1024]{3,2,1,0:T(1,128)S(1)} %collective-permute-done) | data formatting | bytes 344064 | tf_op jit(solution)/shard_map/ppermute | solution.py:16
  35.9 36.4 %fusion.157 = f32[7,6,128,1024]{2,3,1,0:T(8,128)} fusion(f32[7,6,128,1024]{2,3,1,0:T(8,128)} %copy.111, f32[7,6,127,1024]{2,3,1,0:T(8,128)} %bitcast.695, f32[7,6,1,1024]{2,3,1,0:T(8,128)} %copy.109, f32[7,6,128,1023]{2,3,1,0:T(8,128)} %bitcast.696, f32[128,1024]{0,1:T(8,128)S(1)} %copy.112, f32[128,1024]{0,1:T(8,128)S(1)} %copy.107), kind=kLoop, calls=%fused_computation.404 | loop fusion | flops 38535168 | bytes 89107456 | tf_op jit(solution)/shard_map/sub | solution.py:85
  72.3 18.3 %slice.384 = f32[7,6,1,1024]{2,3,1,0:T(8,128)} slice(f32[7,6,128,1024]{2,3,1,0:T(8,128)} %fusion.157), slice={[0:7], [0:6], [127:128], [0:1024]} | slice | bytes 344064 | tf_op jit(solution)/shard_map/slice | solution.py:99
  90.5 11.8 %copy.115 = f32[7,6,1,1024]{3,2,1,0:T(1,128)S(1)} copy(f32[7,6,1,1024]{2,3,1,0:T(8,128)} %slice.384) | data formatting | bytes 344064 | tf_op jit(solution)/shard_map/slice | solution.py:99
  104.8 10.5 %copy.116 = f32[7,6,1,1024]{2,3,1,0:T(8,128)} copy(f32[7,6,1,1024]{3,2,1,0:T(1,128)S(1)} %collective-permute-done.1) | data formatting | bytes 344064 | tf_op jit(solution)/shard_map/ppermute | solution.py:16
  115.3 37.1 %fusion.160 = f32[7,6,128,1024]{2,3,1,0:T(8,128)} fusion(f32[7,6,128,1024]{2,3,1,0:T(8,128)} %fusion.157, f32[7,6,127,1024]{2,3,1,0:T(8,128)} %bitcast.693, f32[7,6,1,1024]{2,3,1,0:T(8,128)} %copy.116, f32[7,6,128,1023]{2,3,1,0:T(8,128)} %bitcast.694, f32[128,1024]{0,1:T(8,128)} %copy-done.1, f32[128,1024]{0,1:T(8,128)} %copy-done), kind=kLoop, calls=%fused_computation.408 | loop fusion | flops 38535168 | bytes 89107456 | tf_op jit(solution)/shard_map/sub | solution.py:85
  158.5 9.0 all-to-all-start
  169.1 16.4 %sine_negate_fusion = (f32[2048,512]{0,1:T(8,128)S(1)}, f32[2048,512]{0,1:T(8,128)S(1)}) fusion(), kind=kLoop, calls=%fused_computation.427 | loop fusion | flops 15728640 | bytes 8388608 | tf_op jit(solution)/shard_map/neg | solution.py:109
  189.7 70.2 %all-to-all-done = f32[6,128,1024]{1,0,2:T(8,128)} async-done(((f32[6,128,1024]{1,0,2:T(8,128)}), f32[6,128,1024]{1,0,2:T(8,128)}, u32[]{:S(2)}, u32[]{:S(2)}) %all-to-all-start) | async-done | bytes 3145760 | tf_op jit(solution)/shard_map/all_to_all | solution.py:114
  266.4 14.5 %fusion.241 = f32[2,512,6,64]{1,3,2,0:T(8,128)} fusion(f32[2,512,2048,1]{2,1,3,0:T(8,128)} %bitcast.697, f32[6,2048,64,1]{1,2,0,3:T(8,128)} %reshape.1941), kind=kOutput, calls=%fused_computation.462 | convolution fusion | flops 9663676416 | bytes 13107200 | tf_op jit(solution)/shard_map/lij,ik->klj/dot_general | solution.py:112
  295.4 173.3 %while.21 = (s32[]{:T(128)}, f32[32,1024]{1,0:T(8,128)S(1)}, f32[32,1024]{1,0:T(8,128)S(1)}, f32[32,1024]{1,0:T(8,128)S(1)}, f32[32,16,32,1024]{3,2,1,0:T(8,128)...) while((s32[]{:T(128)}, f32[32,1024]{1,0:T(8,128)S(1)}, ...), condition=%wide.region_4.5_spmd.clone.clone, body=%wide.region_3.4_spmd.clone.clone.sunk | while | flops 15023121 | bytes 23396332 | solution.py:68
  468.8 6.4 select_reduce_fusion
  475.8 6.1 reduce.2
  491.3 107.1 %fusion.182 = f32[32,512,2,6]{1,3,2,0:T(8,128)S(1)} fusion(f32[2,32,6,1024]{3,1,2,0:T(8,128)S(1)} %broadcast_multiply_fusion, f32[512,32,1024]{2,1,0:T(8,128)} %bitcast.2, f32[32,512]{1,0:T(8,128)S(1)} %select_reduce_fusion), kind=kOutput, calls=%fused_computation.441 | convolution fusion | flops 2416115712 | bytes 69533696 | tf_op jit(solution)/shard_map/skj,cslj->skcl/dot_general | solution.py:133
  598.4 85.2 %fusion.179 = f32[2,32,6,1024]{3,2,0,1:T(8,128)S(1)} fusion(f32[32,512,2,6]{1,3,2,0:T(8,128)S(1)} %fusion.182, f32[512,32,1024]{2,1,0:T(8,128)} %bitcast.2), kind=kOutput, calls=%fused_computation.440 | convolution fusion | flops 2415919104 | bytes 69468160 | tf_op jit(solution)/shard_map/skj,skcl->cslj/dot_general | solution.py:135
  683.7 5.2 copy.126
  688.8 8.8 reshape.1949
  697.6 6.0 all-to-all-start.2
  703.7 18.1 %cosine_multiply_fusion = (f32[512,2048]{1,0:T(8,128)}, f32[512,2048]{1,0:T(8,128)}) fusion(f32[512]{0:T(512)S(1)} %fusion.190), kind=kLoop, calls=%fused_computation.431 | loop fusion | flops 17825792 | bytes 8390656 | tf_op jit(solution)/shard_map/mul | solution.py:111
  721.7 18.1 %all-to-all-done.2 = f32[16,1,24576]{2,1,0:T(1,128)S(1)} async-done(((f32[16,1,24576]{2,1,0:T(1,128)}), f32[16,1,24576]{2,1,0:T(1,128)S(1)}, u32[]{:S(2)}, u32[]{:S(2)}) %all-to-all-start.2) | async-done | bytes 1572896 | tf_op jit(solution)/shard_map/all_to_all | solution.py:136
  744.2 7.0 reshape.1950
  751.2 7.8 copy.138
  761.1 13.1 %fusion.161 = f32[2048,384]{0,1:S(1)} fusion(f32[1024,384]{0,1:T(8,128)} %bitcast.707, f32[512,2048]{1,0:T(8,128)} %get-tuple-element.510, f32[512,2048]{1,0:T(8,128)} %get-tuple-element.509), kind=kOutput, calls=%fused_computation.410 | convolution fusion | flops 9665773568 | bytes 13107200
  779.0 12.5 %reshape.1951 = f32[16,1,49152]{2,1,0:T(1,128)} reshape(f32[2048,6,64]{2,1,0:T(8,128)} %bitcast.698) | data formatting | bytes 6291456
  791.5 5.2 all-to-all-start.3
  796.7 14.4 %slice.388 = f32[6,6,128,1024]{2,3,1,0:T(8,128)} slice(f32[7,6,128,1024]{2,3,1,0:T(8,128)} %fusion.160), slice={[1:7], [0:6], [0:128], [0:1024]} | slice | bytes 37748736 | tf_op jit(solution)/shard_map/slice | solution.py:142
  811.0 55.4 %all-to-all-done.3 = f32[16,1,49152]{2,1,0:T(1,128)S(1)} async-done(((f32[16,1,49152]{2,1,0:T(1,128)}), f32[16,1,49152]{2,1,0:T(1,128)S(1)}, u32[]{:S(2)}, u32[]{:S(2)}) %all-to-all-start.3) | async-done | bytes 3145760 | tf_op jit(solution)/shard_map/all_to_all | solution.py:140
  866.5 10.8 %reduce.4 = f32[16,49152]{1,0:T(8,128)} reduce(f32[16,1,49152]{2,1,0:T(1,128)S(1)} %all-to-all-done.3, f32[]{:T(128)} %broadcast.2552), dimensions={1}, to_apply=%all_to_all.61.reduce_sub_computation | reduce | bytes 6291460 | tf_op jit(solution)/shard_map/all_to_all | solution.py:140
  877.3 6.5 reshape.1952
  891.1 14.3 %pad_maximum_fusion = f32[7,6,128,1024]{2,3,1,0:T(8,128)} fusion(f32[6,6,128,1024]{2,3,1,0:T(8,128)} %slice.388, f32[1,6,128,1024]{2,3,1,0:T(8,128)S(1)} %bitcast_add_fusion.16), kind=kLoop, calls=%fused_computation.409 | loop fusion | flops 5505024 | bytes 44040192 | tf_op jit(solution)/shard_map/concatenate | solution.py:142
  905.4 21.7 %copy.133 = f32[7,6,128,1024]{3,2,1,0:T(8,128)} copy(f32[7,6,128,1024]{2,3,1,0:T(8,128)} %pad_maximum_fusion) | data formatting | bytes 44040192 | tf_op jit(solution)/shard_map/concatenate | solution.py:142
  (802 shorter events, 237.0 us)
Async XLA Ops:
  1.5 23.5 %copy-start.2 = (f32[128,1024]{1,0:T(8,128)S(1)}, f32[128,1024]{1,0:T(8,128)}, u32[]{:S(2)}) copy-start(f32[128,1024]{1,0:T(8,128)} %param.8) | copy-start | bytes 1572868
  1.5 23.7 %copy-start.3 = (f32[128,1024]{1,0:T(8,128)S(1)}, f32[128,1024]{1,0:T(8,128)}, u32[]{:S(2)}) copy-start(f32[128,1024]{1,0:T(8,128)} %param.9) | copy-start | bytes 1572868
  1.5 23.9 %collective-permute-start = (f32[7,6,1,1024]{3,2,1,0:T(1,128)S(1)}, f32[7,6,1,1024]{3,2,1,0:T(1,128)S(1)}, u32[]{:S(2)}, u32[]{:S(2)}) collective-permute-start(f32[7,6,1,1024]{3,2,1,0:T(1,128)S(1)} %slice.307), channel_id=1, source_target_pairs={{0,1},{1,2},{2,3},{3,4},{4,5},{5,6},{6,7},{7,8},{8,9},{9,10},{10,1... | collective-permute-start | bytes 516104 | tf_op jit(solution)/shard_map/ppermute | solution.py:16
  25.2 10.7 %copy-start = (f32[128,1024]{0,1:T(8,128)}, f32[128,1024]{0,1:T(8,128)S(1)}, u32[]{:S(2)}) copy-start(f32[128,1024]{0,1:T(8,128)S(1)} %copy.107) | copy-start | bytes 1572868
  25.4 10.5 %copy-start.1 = (f32[128,1024]{0,1:T(8,128)}, f32[128,1024]{0,1:T(8,128)S(1)}, u32[]{:S(2)}) copy-start(f32[128,1024]{0,1:T(8,128)S(1)} %copy.112) | copy-start | bytes 1572868
  102.3 2.5 collective-permute-start.1
  158.5 101.3 %all-to-all-start = ((f32[6,128,1024]{1,0,2:T(8,128)}), f32[6,128,1024]{1,0,2:T(8,128)}, u32[]{:S(2)}, u32[]{:S(2)}) async-start(f32[6,128,1024]{1,0,2:T(8,128)} %copy.119), calls=%async_computation | async-start | bytes 8388608 | tf_op jit(solution)/shard_map/all_to_all | solution.py:114
  168.0 17.6 %copy-start.4 = (s32[32]{0:T(128)}, s32[32]{0:T(128)S(1)}, u32[]{:S(2)}) copy-start(s32[32]{0:T(128)S(1)} %get-tuple-element.513) | copy-start | bytes 388
  285.1 9.4 %copy-start.5 = (s32[32]{0:T(128)S(1)}, s32[32]{0:T(128)}, u32[]{:S(2)}) copy-start(s32[32]{0:T(128)} %copy-done.4) | copy-start | bytes 388
  289.4 185.9 %all-to-all-start.1 = ((f32[16,1,24576]{2,1,0:T(1,128)}), f32[16,1,24576]{2,1,0:T(1,128)S(1)}, u32[]{:S(2)}, u32[]{:S(2)}) async-start(f32[16,1,24576]{2,1,0:T(1,128)} %reshape.1947), calls=%async_computation.1 | async-start | bytes 3145728 | tf_op jit(solution)/shard_map/all_to_all | solution.py:131
  295.4 173.3 %copy-start.6 = (s32[32]{0:T(128)S(1)}, s32[32]{0:T(128)}, u32[]{:S(2)}) copy-start(s32[32]{0:T(128)} %copy-done.4) | copy-start | bytes 388
  295.4 173.4 %copy-start.7 = (f32[512]{0:T(512)S(1)}, f32[512]{0:T(512)}, u32[]{:S(2)}) copy-start(f32[512]{0:T(512)} %param.11) | copy-start | bytes 6148
  697.6 42.2 %all-to-all-start.2 = ((f32[16,1,24576]{2,1,0:T(1,128)}), f32[16,1,24576]{2,1,0:T(1,128)S(1)}, u32[]{:S(2)}, u32[]{:S(2)}) async-start(f32[16,1,24576]{2,1,0:T(1,128)} %reshape.1949), calls=%async_computation.2 | async-start | bytes 3145728 | tf_op jit(solution)/shard_map/all_to_all | solution.py:136
  791.5 75.0 %all-to-all-start.3 = ((f32[16,1,49152]{2,1,0:T(1,128)}), f32[16,1,49152]{2,1,0:T(1,128)S(1)}, u32[]{:S(2)}, u32[]{:S(2)}) async-start(f32[16,1,49152]{2,1,0:T(1,128)} %reshape.1951), calls=%async_computation.3 | async-start | bytes 6291456 | tf_op jit(solution)/shard_map/all_to_all | solution.py:140
where the time goes:
time: 936 us; the launch traced here: 927 us
  other arithmetic  284 us (30%)
  local copies, waits for them, and re-layouts  248 us (26%)
  matrix products  220 us (24%)
  waiting for transfers between devices  144 us (15%)
  starting transfers between devices  27.3 us (3%)
    dot_general x1, matrix products, body(): jnp.einsum('skj,cslj->skcl', legendre, weighted, precision=highest)  107 us
    while x480, other arithmetic  101 us
    dot_general x1, matrix products, body(): jnp.einsum('skj,skcl->cslj', legendre, scaled, precision=highest)  85.2 us
    sub x2, other arithmetic, advect(): cells - lon_courant * (cells - west_cells)  73.5 us
    all_to_all x1, waiting for transfers between devices, body(): lax.all_to_all(anomaly, 'band', split_axis=2, concat_axis=1, tiled=True)  70.2 us
    unnamed x26, local copies, waits for them, and re-layouts  66.9 us
    all_to_all x1, waiting for transfers between devices, body(): lax.all_to_all(band_increment, 'band', split_axis=1, concat_axis=2, tiled...  55.4 us
    dynamic_update_slice x32, local copies, waits for them, and re-layouts, legendre_table(): lax.scan(advance, (zero_row, zero_row, zero_row), (wave_rows.T, offset_ro...  47.4 us
  transfers between devices with their start and end apart: 6, of which 3 were waited for; matrix products, arithmetic and copies ran while one was open for 28% of the time, Pallas kernels for 0%

commit v1 on v0

v1 whole, which is shorter than its diff:
```python
import functools
import math

import jax
import jax.numpy as jnp
import ml_dtypes
import numpy as np
from jax import lax
from jax.experimental import pallas as pl
from jax.experimental.pallas import tpu as pltpu
from jax.sharding import PartitionSpec as P

STEPS = 2
GROUP = 8
STRIPS = 16
UNIT = 2
ROWS = 64
QUADS = ROWS // 32
SHIFT = 100
DROP = 120
TOP = 20
CHUNKS = 4
F32 = jnp.float32
BF16 = jnp.bfloat16


def split_np(values):
    high = values.astype(ml_dtypes.bfloat16)
    low = (values - high.astype(np.float64)).astype(ml_dtypes.bfloat16)
    return high, low


def split(values):
    high = values.astype(BF16)
    return high, (values - high.astype(F32)).astype(BF16)


def dot(left, right):
    return jnp.dot(left, right, preferred_element_type=F32)


class Layout:
    def __init__(self, wave_total, lat_total, lon_total, band_count):
        self.waves, self.lats, self.lons, self.band = wave_total, lat_total, lon_total, band_count
        self.half = lat_total // 2
        self.groups = wave_total // (2 * GROUP)
        self.blocks = [-(-(wave_total - 2 * GROUP * t) // ROWS) for t in range(self.groups)]
        shares = [0] * CHUNKS
        self.chunks = [[] for _ in range(CHUNKS)]
        for t in sorted(range(self.groups), key=lambda t: -self.blocks[t]):
            q = int(np.argmin(shares))
            self.chunks[q].append(t)
            shares[q] += self.blocks[t]
        self.chunks = [chunk for chunk in self.chunks if chunk]
        self.order = [t for chunk in self.chunks for t in chunk]
        ends = np.cumsum([0] + [2 * GROUP * len(chunk) for chunk in self.chunks])
        self.cuts = [(int(b), int(e)) for b, e in zip(ends[:-1], ends[1:])]

    def wave_ids(self, core):
        ids = []
        for t in self.order:
            ids.append(GROUP * (2 * t + core) + np.arange(GROUP))
        return np.stack(ids)

    def items(self, chunk):
        items = [(local, b) for local, t in enumerate(chunk) for b in range(self.blocks[t])]
        while len(items) % (2 * UNIT):
            items.append((len(chunk) - 1, -1))
        return items

    @functools.cached_property
    def angles(self):
        return math.pi * (np.arange(self.half) + 0.5) / self.lats

    @functools.cached_property
    def recurrence(self):
        depth = self.waves + 2 * ROWS
        m = np.arange(self.waves, dtype=np.float64)[:, None]
        k = np.arange(depth, dtype=np.float64)[None, :]
        n = m + k
        a = np.ones((self.waves, depth))
        a[:, 1:] = np.sqrt((4 * n * n - 1)[:, 1:] / (n * n - m * m)[:, 1:])
        c = np.ones_like(a)
        c[:, 1] = a[:, 1]
        for i in range(2, depth):
            c[:, i] = a[:, i] / a[:, i - 1] * c[:, i - 2]
        alpha = np.zeros_like(a)
        alpha[:, 1:] = a[:, 1:] * c[:, :-1] / c[:, 1:]
        return alpha, c

    @functools.cached_property
    def starts(self):
        orders = np.arange(1, self.waves)
        norms = np.concatenate([[0.0], np.cumsum(np.log((2.0 * orders + 1) / (2.0 * orders)))])
        m = np.arange(self.waves)[:, None]
        logs = 0.5 * norms[:, None] + m * np.log(np.sin(self.angles))[None, :] - 0.5 * math.log(2.0)
        exps = logs / math.log(2.0) + SHIFT
        deficit = np.where(exps < -SHIFT, np.ceil((-SHIFT - exps) / DROP), 0.0)
        return np.exp2(exps + DROP * deficit), deficit

    def tables(self, chunk):
        alpha, c = self.recurrence
        mant, deficit = self.starts
        items = self.items(chunk)
        out_alpha = np.zeros((2, len(items), GROUP, 128), np.float32)
        out_c = np.zeros((2, len(items), ROWS, 128), np.float32)
        shape = (2, len(chunk) * GROUP, self.half)
        out_start, out_deficit = np.zeros(shape, np.float32), np.zeros(shape, np.float32)
        rows = np.concatenate([np.arange(0, ROWS, 2), np.arange(1, ROWS, 2)])
        for core in range(2):
            for local, t in enumerate(chunk):
                waves = GROUP * (2 * t + core) + np.arange(GROUP)
                place = slice(GROUP * local, GROUP * (local + 1))
                out_start[core, place], out_deficit[core, place] = -mant[waves], deficit[waves]
            for i, (local, b) in enumerate(items):
                if b < 0:
                    continue
                waves = GROUP * (2 * chunk[local] + core) + np.arange(GROUP)
                out_alpha[core, i, :, :ROWS] = alpha[waves, ROWS * b : ROWS * (b + 1)]
                squares = c[waves][:, ROWS * b + rows] ** 2 * 2.0**-SHIFT
                out_c[core, i] = np.tile(squares.T, (1, 128 // GROUP))
        return out_alpha, out_start, out_deficit, out_c

    def fourier_tables(self):
        local = self.lons // self.band
        forward = np.zeros((self.band, self.waves, 2 * local))
        inverse = np.zeros((self.band, 2 * local, self.waves))
        for place in range(self.band):
            waves = self.wave_ids(place % 2)
            lons = np.concatenate([local * place + np.arange(local), local * (place ^ 1) + np.arange(local)])
            phase = (waves[:, :, None] * lons % self.lons) * (2 * math.pi / self.lons)
            both = np.stack([np.cos(phase), -np.sin(phase)], axis=1).reshape(self.waves, 2 * local)
            double = np.where(waves == 0, 1.0, 2.0)
            double = np.stack([double, double], axis=1).reshape(self.waves)
            forward[place] = both / self.lons
            inverse[place] = (both * double[:, None]).T
        return [np.concatenate(split_np(t), axis=1) for t in (forward, inverse)]


def south_of(cells, lane_ids):
    return jnp.where(lane_ids == 0, 0.0, pltpu.roll(cells, 1, 1))


def two_steps(cells, edge, lon, lat, lon_edge, lat_edge, store):
    shape = (8, cells.shape[1])
    row_ids = lax.broadcasted_iota(jnp.int32, shape, 0)
    lane_ids = lax.broadcasted_iota(jnp.int32, shape, 1)
    outer = jnp.broadcast_to(edge[0:1], shape)
    inner = jnp.broadcast_to(edge[1:2], shape)
    inner_once = (
        inner - lon_edge * (inner - outer) - lat_edge * (inner - south_of(inner, lane_ids))
    )

    def strip(i, carry):
        before, before_once = carry
        rows = pl.ds(pl.multiple_of(8 * i, 8), 8)
        now, east, north = cells[rows, :], lon[rows, :], lat[rows, :]
        turned = pltpu.roll(now, 1, 0)
        west = jnp.where(row_ids == 0, before, turned)
        once = now - east * (now - west) - north * (now - south_of(now, lane_ids))
        turned_once = pltpu.roll(once, 1, 0)
        west = jnp.where(row_ids == 0, before_once, turned_once)
        store(rows, once - east * (once - west) - north * (once - south_of(once, lane_ids)))
        return turned, turned_once

    lax.fori_loop(0, cells.shape[0] // 8, strip, (inner, inner_once), unroll=STRIPS)


def reversed_lanes(values, flip):
    width = flip.shape[0]
    high, rest = split(values)
    mid = rest
    low = (values - high.astype(F32) - mid.astype(F32)).astype(BF16)
    pieces = []
    for at in range(values.shape[1] // width - 1, -1, -1):
        cut = slice(at * width, (at + 1) * width)
        pieces.append(dot(high[:, cut], flip) + (dot(mid[:, cut], flip) + dot(low[:, cut], flip)))
    return jnp.concatenate(pieces, axis=1)


def first_field_kernel(cells, edge, lon, lat, courant_edge, target, flip, moved, folded):
    def store(rows, values):
        moved[0, rows, :] = values

    two_steps(
        cells.at[0, 0], edge[0], lon, lat, courant_edge[0:1], courant_edge[1:2], store
    )
    anomaly = target[0] - moved[0]
    half = anomaly.shape[1] // 2
    north = anomaly[:, :half]
    south = reversed_lanes(anomaly[:, half:], flip[...])
    folded[0, :, :half] = north + south
    folded[0, :, half:] = north - south


def other_fields_kernel(cells, edge, lon, lat, courant_edge, moved):
    def store(rows, values):
        moved[0, 0, rows, :] = values

    two_steps(
        cells.at[0, 0], edge[0], lon, lat, courant_edge[0:1], courant_edge[1:2], store
    )


def finish_kernel(flip, moved, mine, theirs, whole, out):
    del whole
    total = mine[0, 0] + theirs[0]
    half = total.shape[1] // 2
    even, odd = total[:, :half], total[:, half:]
    out[0, 0, :, :half] = moved[0, :, :half] + (even + odd)
    out[0, 0, :, half:] = moved[0, :, half:] + reversed_lanes(even - odd, flip[...])


def forward_kernel(cuts, place, table, mine, theirs, quad, *outs):
    del place
    a_high, a_low = split(jnp.concatenate([mine[0], theirs[0]], axis=0))
    waves = table.shape[1] // 2
    wide = dot(table[0], a_high)
    total = (wide[:waves] + (wide[waves:] + dot(table[0, :waves], a_low))) * quad[...]
    for out, (begin, end) in zip(outs, cuts):
        out[0] = total[begin:end]


def inverse_kernel(place, table, *refs):
    del place
    out = refs[-1]
    s_high, s_low = split(jnp.concatenate([ref[0] for ref in refs[:-1]], axis=0))
    lons = table.shape[1] // 2
    wide = dot(table[0], s_high)
    total = wide[:lons] + (wide[lons:] + dot(table[0, :lons], s_low))
    out[0, 0], out[1, 0] = total[: lons // 2], total[lons // 2 :]


def table_block(index, first, local, carry, alpha, start, deficit, mu, scaled, even, odd):
    earlier, latest, owed = carry
    count = len(earlier)
    fresh = first == 1
    rows = pl.ds(pl.multiple_of(local * GROUP, GROUP), GROUP)
    factors = alpha[0, index]
    earlier, latest, owed = list(earlier), list(latest), list(owed)
    for b in range(count):
        lanes = slice(128 * b, 128 * (b + 1))
        earlier[b] = jnp.where(fresh, start[0, rows, lanes], earlier[b])
        latest[b] = jnp.where(fresh, 0.0, latest[b])
        if scaled[b]:
            owed[b] = jnp.where(fresh, deficit[0, rows, lanes], owed[b])
    values = [[None] * ROWS for _ in range(count)]
    for segment in range(0, ROWS, 16):
        for b in range(count):
            if scaled[b]:
                large = jnp.maximum(jnp.abs(earlier[b]), jnp.abs(latest[b])) > 2.0**TOP
                down = jnp.logical_and(large, owed[b] > 0.0)
                factor = jnp.where(down, 2.0**-DROP, 1.0)
                earlier[b] = earlier[b] * factor
                latest[b] = latest[b] * factor
                owed[b] = owed[b] - jnp.where(down, 1.0, 0.0)
        for k in range(segment, segment + 16):
            spread = jnp.broadcast_to(factors[:, k : k + 1], (GROUP, 128))
            for b in range(count):
                fresh_value = (spread * mu[:, 128 * b : 128 * (b + 1)]) * latest[b] - earlier[b]
                earlier[b], latest[b] = latest[b], fresh_value
                values[b][k] = fresh_value
        for b in range(count):
            lanes = slice(128 * b, 128 * (b + 1))
            for k in range(segment, segment + 16, 4):
                for parity, store in ((0, even), (1, odd)):
                    pair = jnp.concatenate(
                        [values[b][k + parity], values[b][k + parity + 2]], axis=0
                    )
                    if scaled[b]:
                        keep = jnp.concatenate([owed[b], owed[b]], axis=0) == 0.0
                        pair = jnp.where(keep, pair, 0.0)
                    high, low = split(pair)
                    at = 4 * k
                    store[at : at + 16, lanes] = high
                    store[4 * ROWS + at : 4 * ROWS + at + 16, lanes] = low
    return tuple(earlier), tuple(latest), tuple(owed)


def own_lane_mask(value):
    wave = lax.broadcasted_iota(jnp.int32, (GROUP, 128), 0)
    lane = lax.broadcasted_iota(jnp.int32, (GROUP, 128), 1)
    return jnp.where(lane % GROUP == wave, value, 0.0)


def run_blocks(count, tables, use, lat_blocks, scaled, buffers):
    firsts, locals_, alpha, start, deficit, mu = tables
    ahead, behind = buffers
    angles = jnp.broadcast_to(mu[...], (GROUP, mu.shape[1]))
    zero = jnp.zeros((GROUP, 128), F32)
    carry = tuple(tuple(zero for _ in range(lat_blocks)) for _ in range(3))

    def stage(base, carry, made, used):
        use([jnp.maximum(base - UNIT + j, j) for j in range(UNIT)], used)
        for j in range(UNIT):
            i = base + j
            carry = table_block(
                i, firsts[i], locals_[i], carry, alpha, start, deficit, angles, scaled, *made[j]
            )
        return carry

    def two(step, carry):
        carry = stage(2 * UNIT * step, carry, ahead, behind)
        return stage(2 * UNIT * step + UNIT, carry, behind, ahead)

    lax.fori_loop(0, count // (2 * UNIT), two, carry)
    use([jnp.int32(count - UNIT + j) for j in range(UNIT)], behind)


def buffer_pairs(refs):
    pairs = [(refs[2 * j], refs[2 * j + 1]) for j in range(2 * UNIT)]
    return pairs[:UNIT], pairs[UNIT:]


def clear(pairs):
    for pair in pairs:
        for ref in pair:
            ref[...] = jnp.zeros_like(ref)


def slot_of(item, count, owned):
    quarter = item // (count // 4)
    return quarter ^ owned, (item - quarter * (count // 4)) * 24 * QUADS


def analysis_kernel(
    count,
    levels,
    scaled,
    where,
    firsts,
    locals_,
    alpha,
    start,
    deficit,
    mu,
    waves,
    out,
    weights,
    *refs,
):
    buffers = buffer_pairs(refs)
    groups = waves.shape[1] // (2 * GROUP)
    half = waves.shape[2] // 2
    columns = levels * 2 * GROUP

    def prepare(group, _):
        rows = pl.ds(pl.multiple_of(group * 2 * GROUP, 2 * GROUP), 2 * GROUP)
        for parity in range(2):
            block = waves[:, rows, parity * half : (parity + 1) * half].reshape(columns, half)
            block = jnp.concatenate([block, jnp.zeros((128 - columns, half), F32)], axis=0)
            high, low = split(block.T)
            weights[group, parity, :, 0:128] = high
            weights[group, parity, :, 128:256] = low
        return 0

    lax.fori_loop(0, groups, prepare, 0)
    clear(buffers[1])
    owned = where[1]
    mask = own_lane_mask(2.0**-SHIFT)
    lane = lax.broadcasted_iota(jnp.int32, (GROUP, 128), 1)
    table = 4 * ROWS

    def use(items, stores):
        products = []
        for item, pair in zip(items, stores):
            group = locals_[item]
            products.append([dot(pair[p][...], weights[group, p]) for p in range(2)])
        for item, pair in zip(items, products):
            sums = []
            for both in pair:
                product = both[:table, 0:128] + (both[:table, 128:256] + both[table:, 0:128])
                picked = product.reshape(table // GROUP, GROUP, 128) * mask[None]
                sums.append(jnp.sum(picked, axis=1))
            slot, at = slot_of(item, count, owned)
            for quad in range(QUADS):
                tiles = []
                for j in range(4 * quad, 4 * quad + 4):
                    parity, row = divmod(8 * j, ROWS // 2)
                    tiles.append(sums[parity][row : row + 8])
                second, third = pltpu.roll(tiles[1], 96, 1), pltpu.roll(tiles[2], 64, 1)
                packed = (
                    jnp.where(lane < 96, tiles[0], second),
                    jnp.where(lane < 64, second, third),
                    jnp.where(lane < 32, third, pltpu.roll(tiles[3], 32, 1)),
                )
                for j in range(3):
                    rows = pl.ds(pl.multiple_of(at + 24 * quad + 8 * j, 8), 8)
                    out[slot, rows, :] = packed[j]

    run_blocks(
        count,
        (firsts, locals_, alpha, start, deficit, mu),
        use,
        half // 128,
        scaled,
        buffers,
    )


def synthesis_kernel(
    count,
    levels,
    scaled,
    where,
    firsts,
    locals_,
    degrees,
    alpha,
    start,
    deficit,
    mu,
    squares,
    rates,
    coeffs,
    out,
    *refs,
):
    buffers = buffer_pairs(refs)
    half = mu.shape[1]
    columns = levels * 2 * GROUP
    clear(buffers[1])
    owned = where[1]
    mask = own_lane_mask(1.0)
    lane = lax.broadcasted_iota(jnp.int32, (GROUP, 128), 1)
    table = 4 * ROWS

    def use(items, stores):
        totals = []
        for item, pair in zip(items, stores):
            slot, at = slot_of(item, count, owned)
            tiles = []
            for quad in range(QUADS):
                packed = []
                for j in range(3):
                    rows = pl.ds(pl.multiple_of(at + 24 * quad + 8 * j, 8), 8)
                    packed.append(coeffs[slot, rows, :])
                tiles += [
                    packed[0],
                    pltpu.roll(jnp.where(lane < 64, packed[1], packed[0]), 32, 1),
                    pltpu.roll(jnp.where(lane < 32, packed[2], packed[1]), 64, 1),
                    pltpu.roll(packed[2], 96, 1),
                ]
            degree_rows = pl.ds(pl.multiple_of(degrees[item], 8), ROWS // 2)
            share = ROWS // 2
            for parity in range(2):
                parts = tiles[parity * 2 * QUADS : (parity + 1) * 2 * QUADS]
                scale = squares[0, item, share * parity : share * (parity + 1)]
                block = jnp.concatenate(parts, axis=0) * (scale * rates[parity, degree_rows])
                wide = jnp.broadcast_to(block[:, None, :], (share, GROUP, 128)) * mask[None]
                high, low = split(wide.reshape(table, 128).T[:columns])
                left = jnp.concatenate(
                    [
                        jnp.concatenate([high, high], axis=1),
                        jnp.concatenate([low, jnp.zeros_like(low)], axis=1),
                    ],
                    axis=0,
                )
                total = dot(left, pair[parity][...])
                totals.append(total[:columns] + total[columns:])
        for j, item in enumerate(items):
            target = pl.ds(pl.multiple_of(locals_[item] * 2 * GROUP, 2 * GROUP), 2 * GROUP)
            for parity in range(2):
                lanes = slice(parity * half, (parity + 1) * half)
                before = jnp.where(firsts[item] == 1, 0.0, out[:, target, lanes])
                total = totals[2 * j + parity].reshape(levels, 2 * GROUP, half)
                out[:, target, lanes] = before + total

    run_blocks(
        count,
        (firsts, locals_, alpha, start, deficit, mu),
        use,
        half // 128,
        scaled,
        buffers,
    )


def chip_sum(slots, band_count):
    chips = band_count // 2
    steps = [1 << b for b in range(chips.bit_length() - 1)]
    part = slots[:2] + (yield slots[2:], steps[0])
    part = part[:1] + (yield part[1:], steps[1])
    for step in steps[2:]:
        part = part + (yield part, step)
    part = jnp.concatenate([part, (yield part, steps[1])], axis=0)
    return jnp.concatenate([part, (yield part, steps[0])], axis=0)


def chip_move(value, step, band_count):
    ends = []
    for c in range(band_count // 2):
        ends += [(2 * c, 2 * (c ^ step)), (2 * c + 1, 2 * (c ^ step) + 1)]
    return lax.ppermute(value, "band", ends)


class Pipeline:
    def __init__(self, band_count):
        self.band_count = band_count
        self.active = {}
        self.done = {}

    def begin(self, key, slots):
        steps = chip_sum(slots, self.band_count)
        self.active[key] = [steps, next(steps)]

    def compute(self, operands, call):
        keys = list(self.active)
        payloads = [self.active[k][1][0] for k in keys]
        operands, payloads = lax.optimization_barrier((tuple(operands), payloads))
        arrived = [
            chip_move(p, self.active[k][1][1], self.band_count) for k, p in zip(keys, payloads)
        ]
        result, arrived = lax.optimization_barrier((call(*operands), arrived))
        for k, value in zip(keys, arrived):
            entry = self.active[k]
            try:
                entry[1] = entry[0].send(value)
            except StopIteration as stop:
                self.done[k] = stop.value
                del self.active[k]
        return result


def full(shape):
    return pl.BlockSpec(shape, lambda *_: (0,) * len(shape))


def cost(micros):
    return pl.CostEstimate(flops=int(micros * 1e9), bytes_accessed=1 << 20, transcendentals=0)


def params(limit=56):
    return pltpu.CompilerParams(vmem_limit_bytes=limit << 20)


def body(state, courant_lon, courant_lat, reference_field, nudge_rate):
    fields, levels, lon_local, lat_total = state.shape
    band_count = lax.axis_size("band")
    place = lax.axis_index("band")
    wave_total = nudge_rate.shape[0]
    lay = Layout(wave_total, lat_total, lon_local * band_count, band_count)
    half = lay.half
    plane = (lon_local, lat_total)
    chip = place // 2
    owned = 2 * (chip % 2) + (chip // 2) % 2
    where = jnp.stack([place % 2, owned, place]).astype(jnp.int32)

    east = [(i, (i + 1) % band_count) for i in range(band_count)]
    peer = [(i, i ^ 1) for i in range(band_count)]
    edge_rows = jnp.concatenate(
        [
            state[0, :, lon_local - STEPS :, :].reshape(levels * STEPS, lat_total),
            courant_lon[lon_local - 1 :],
            courant_lat[lon_local - 1 :],
        ],
        axis=0,
    )
    arrived = lax.ppermute(edge_rows, "band", east)
    first_edge = arrived[: levels * STEPS].reshape(levels, STEPS, lat_total)
    courant_edge = arrived[levels * STEPS :]
    flip_width = min(256, half)
    flip = jnp.asarray(np.eye(flip_width)[::-1].astype(ml_dtypes.bfloat16))

    moved, folded = pl.pallas_call(
        first_field_kernel,
        grid=(levels,),
        in_specs=[
            pl.BlockSpec((1, 1) + plane, lambda l: (0, l, 0, 0)),
            pl.BlockSpec((1, STEPS, lat_total), lambda l: (l, 0, 0)),
            full(plane),
            full(plane),
            full((2, lat_total)),
            pl.BlockSpec((1,) + plane, lambda l: (l, 0, 0)),
            full((flip_width, flip_width)),
        ],
        out_specs=[pl.BlockSpec((1,) + plane, lambda l: (l, 0, 0))] * 2,
        out_shape=[jax.ShapeDtypeStruct((levels,) + plane, F32)] * 2,
        compiler_params=params(),
        name="first_field",
    )(state, first_edge, courant_lon, courant_lat, courant_edge, reference_field, flip)
    peer_folded = lax.ppermute(folded, "band", peer)

    other_rows = state[1:, :, lon_local - STEPS :, :].reshape((fields - 1) * levels, STEPS, lat_total)
    other_edge = lax.ppermute(other_rows, "band", east)

    def others_call(state, other_edge, courant_lon, courant_lat, courant_edge):
        return pl.pallas_call(
            other_fields_kernel,
            grid=((fields - 1) * levels,),
            in_specs=[
                pl.BlockSpec((1, 1) + plane, lambda i: (1 + i // levels, i % levels, 0, 0)),
                pl.BlockSpec((1, STEPS, lat_total), lambda i: (i, 0, 0)),
                full(plane),
                full(plane),
                full((2, lat_total)),
            ],
            out_specs=pl.BlockSpec((1, 1) + plane, lambda i: (1 + i // levels, i % levels, 0, 0)),
            out_shape=jax.ShapeDtypeStruct(state.shape, F32),
            compiler_params=params(),
            cost_estimate=cost(14.0),
            name="other_fields",
        )(state, other_edge, courant_lon, courant_lat, courant_edge)

    forward, inverse = [jnp.asarray(t) for t in lay.fourier_tables()]
    quad = (math.pi / lat_total) * np.sin(lay.angles)
    quad = jnp.asarray(np.concatenate([quad, quad])[None].astype(np.float32))
    mu = jnp.asarray(np.cos(lay.angles)[None].astype(np.float32))
    cuts = lay.cuts
    pair_lon = 2 * lon_local
    spectra = pl.pallas_call(
        functools.partial(forward_kernel, cuts),
        grid_spec=pltpu.PrefetchScalarGridSpec(
            num_scalar_prefetch=1,
            grid=(levels,),
            in_specs=[
                pl.BlockSpec((1, 2 * wave_total, pair_lon), lambda l, w: (w[2], 0, 0)),
                pl.BlockSpec((1,) + plane, lambda l, w: (l, 0, 0)),
                pl.BlockSpec((1,) + plane, lambda l, w: (l, 0, 0)),
                full((1, lat_total)),
            ],
            out_specs=[pl.BlockSpec((1, e - b, lat_total), lambda l, w: (l, 0, 0)) for b, e in cuts],
        ),
        out_shape=[jax.ShapeDtypeStruct((levels, e - b, lat_total), F32) for b, e in cuts],
        compiler_params=params(),
        name="forward_fourier",
    )(where, forward, folded, peer_folded, quad)

    reach = wave_total + 2 * GROUP + 2 * ROWS
    padded = jnp.concatenate([nudge_rate, jnp.zeros((2 * reach,), F32)])
    padded = lax.dynamic_slice(padded, ((place % 2) * GROUP,), (reach + GROUP,))
    by_wave = jnp.stack([padded[w : w + reach] for w in range(GROUP)], axis=1)
    rates = jnp.tile(by_wave, (1, 128 // GROUP)).reshape(reach // 2, 2, 128).transpose(1, 0, 2)

    deficits = lay.starts[1]
    scaled = tuple(
        bool(np.any(deficits[:, 128 * b : 128 * (b + 1)] > 0)) for b in range(half // 128)
    )
    buffers = [pltpu.VMEM((8 * ROWS, half), BF16)] * (4 * UNIT)
    smem = pl.BlockSpec(memory_space=pltpu.SMEM)
    plans = []
    pipeline = Pipeline(band_count)
    for q, chunk in enumerate(lay.chunks):
        items = lay.items(chunk)
        count = len(items)
        firsts = jnp.asarray(np.array([b == 0 for _, b in items], np.int32))
        locals_ = jnp.asarray(np.array([g for g, _ in items], np.int32))
        degrees = jnp.asarray(
            np.array([(2 * GROUP * chunk[g] + ROWS * max(b, 0)) // 2 for g, b in items], np.int32)
        )
        alpha, start, deficit, squares = [jnp.asarray(t) for t in lay.tables(chunk)]
        table_specs = [
            pl.BlockSpec((1, count, GROUP, 128), lambda i, w: (w[0], 0, 0, 0)),
            pl.BlockSpec((1, GROUP * len(chunk), half), lambda i, w: (w[0], 0, 0)),
            pl.BlockSpec((1, GROUP * len(chunk), half), lambda i, w: (w[0], 0, 0)),
            full((1, half)),
        ]
        rows = count // 4 * 24 * QUADS
        call = pl.pallas_call(
            functools.partial(analysis_kernel, count, levels, scaled),
            grid_spec=pltpu.PrefetchScalarGridSpec(
                num_scalar_prefetch=1,
                grid=(1,),
                in_specs=[smem, smem] + table_specs + [full(spectra[q].shape)],
                out_specs=full((4, rows, 128)),
                scratch_shapes=[pltpu.VMEM((len(chunk), 2, half, 256), BF16)] + buffers,
            ),
            out_shape=jax.ShapeDtypeStruct((4, rows, 128), F32),
            compiler_params=params(),
            cost_estimate=cost(0.5 * count),
            name="analysis",
        )
        slots = pipeline.compute(
            [spectra[q]],
            lambda spectrum: call(where, firsts, locals_, alpha, start, deficit, mu, spectrum),
        )
        pipeline.begin(q, slots)
        plans.append((count, firsts, locals_, degrees, alpha, start, deficit, squares, table_specs, rows))

    others = pipeline.compute([other_edge], lambda edge: others_call(state, edge, courant_lon, courant_lat, courant_edge))
    synths = []
    for q, plan in enumerate(plans):
        count, firsts, locals_, degrees, alpha, start, deficit, squares, table_specs, rows = plan
        while q not in pipeline.done:
            pipeline.compute([], lambda: ())
        shape = spectra[q].shape
        call = pl.pallas_call(
            functools.partial(synthesis_kernel, count, levels, scaled),
            grid_spec=pltpu.PrefetchScalarGridSpec(
                num_scalar_prefetch=1,
                grid=(1,),
                in_specs=[smem, smem, smem]
                + table_specs
                + [
                    pl.BlockSpec((1, count, ROWS, 128), lambda i, w: (w[0], 0, 0, 0)),
                    full(rates.shape),
                    full((4, rows, 128)),
                ],
                out_specs=full(shape),
                scratch_shapes=buffers,
            ),
            out_shape=jax.ShapeDtypeStruct(shape, F32),
            compiler_params=params(),
            cost_estimate=cost(0.5 * count),
            name="synthesis",
        )
        synths.append(
            pipeline.compute(
                [pipeline.done[q]],
                lambda coeffs: call(
                    where, firsts, locals_, degrees, alpha, start, deficit, mu, squares, rates, coeffs
                ),
            )
        )

    def finish(begin, share, both, theirs, whole):
        return pl.pallas_call(
            finish_kernel,
            grid=(share,),
            in_specs=[
                full((flip_width, flip_width)),
                pl.BlockSpec((1,) + plane, lambda l: (l + begin, 0, 0)),
                pl.BlockSpec((1, 1) + plane, lambda l: (0, l, 0, 0)),
                pl.BlockSpec((1,) + plane, lambda l: (l, 0, 0)),
                pl.BlockSpec(memory_space=pl.ANY),
            ],
            out_specs=pl.BlockSpec((1, 1) + plane, lambda l: (0, l + begin, 0, 0)),
            out_shape=jax.ShapeDtypeStruct(state.shape, F32),
            input_output_aliases={4: 0},
            compiler_params=params(),
            cost_estimate=cost(2.0),
            name="finish",
        )(flip, moved, both, theirs, whole)

    parts = []
    share = levels // 2 if levels % 2 == 0 else levels
    for begin in range(0, levels, share):
        both = pl.pallas_call(
            inverse_kernel,
            grid_spec=pltpu.PrefetchScalarGridSpec(
                num_scalar_prefetch=1,
                grid=(share,),
                in_specs=[pl.BlockSpec((1, 2 * pair_lon, wave_total), lambda l, w: (w[2], 0, 0))]
                + [
                    pl.BlockSpec((1, e - b, lat_total), lambda l, w, begin=begin: (l + begin, 0, 0))
                    for b, e in cuts
                ],
                out_specs=pl.BlockSpec((2, 1) + plane, lambda l, w: (0, l, 0, 0)),
            ),
            out_shape=jax.ShapeDtypeStruct((2, share) + plane, F32),
            compiler_params=params(),
            cost_estimate=cost(4.0 * share / levels),
            name="inverse_fourier",
        )(where, inverse, *synths)
        parts.append((begin, both, lax.ppermute(both[1], "band", peer)))
    whole = others
    for begin, both, theirs in parts:
        whole = finish(begin, share, both, theirs, whole)
    return whole


def solution(mesh):
    placed = (
        P("member", None, "band", None),
        P(("member", "band"), None),
        P(("member", "band"), None),
        P("member", "band", None),
        P(),
    )
    return jax.shard_map(
        body, mesh=mesh, in_specs=placed, out_specs=P("member", None, "band", None), check_vma=False
    )
```

time: 936 us -> 366 us (0.39)
  Pallas kernels: 0 us -> 297 us
  other arithmetic: 284 us -> 5.17 us
  local copies, waits for them, and re-layouts: 248 us -> 22.2 us
  matrix products: 220 us -> 0 us
  waiting for transfers between devices: 144 us -> 6.01 us
    pallas_call x0 -> x15, Pallas kernels: none -> 297 us  [the longest x4 106 us: body(): call(where, firsts, locals_, alpha, start, deficit, mu, spectrum)]
    dot_general x3 -> x0, matrix products: 207 us -> none  [the longest x1 107 us: body(): jnp.einsum('skj,cslj->skcl', legendre, weighted, precision=highest)]
    all_to_all x4 -> x0, waiting for transfers between devices: 144 us -> none  [the longest x1 70.2 us: body(): lax.all_to_all(anomaly, 'band', split_axis=2, concat_axis=1, tiled=True)]
    while x480 -> x0, other arithmetic: 101 us -> none
    sub x3 -> x0, other arithmetic: 75.7 us -> none  [the longest x2 73.5 us: advect(): cells - lon_courant * (cells - west_cells)]
    unnamed x26 -> x20, local copies, waits for them, and re-layouts: 66.9 us -> 3.99 us
    dynamic_update_slice x32 -> x0, local copies, waits for them, and re-layouts: 47.4 us -> none  [legendre_table(): lax.scan(advance, (zero_row, zero_row, zero_row), (wave_rows.T, offset_ro...]
    slice x5 -> x14, local copies, waits for them, and re-layouts: 46 us -> 8.79 us  [the longest x4 4.17 us: chip_sum(): part = slots[:2] + (yield (slots[2:], steps[0]))]
  transfers between devices with their start and end apart: 6 -> 25, of which waited for: 3 -> 4; matrix products, arithmetic and copies ran while one was open for 28% -> 4% of each run, Pallas kernels for 0% -> 67%
where the time goes in v1:
time: 366 us; the launch traced here: 361 us
  Pallas kernels  297 us (81%)
  starting transfers between devices  30.9 us (8%)
  local copies, waits for them, and re-layouts  22.2 us (6%)
  waiting for transfers between devices  6.01 us (2%)
  other arithmetic  5.17 us (1%)
    pallas_call x4, Pallas kernels, body(): call(where, firsts, locals_, alpha, start, deficit, mu, spectrum)  106 us
    pallas_call x4, Pallas kernels, body(): call(where, firsts, locals_, degrees, alpha, start, deficit, mu, squares,...  105 us
    pallas_call x1, Pallas kernels, others_call(): pl.pallas_call(other_fields_kernel, grid=((fields - 1) * levels,), in_spe...  41.3 us
    ppermute x20, starting transfers between devices, chip_move(): return lax.ppermute(value, 'band', ends)  19.5 us
    pallas_call x2, Pallas kernels, body(): pl.pallas_call(inverse_kernel, grid_spec=pltpu.PrefetchScalarGridSpec(num...  15.1 us
    pallas_call x1, Pallas kernels, body(): pl.pallas_call(functools.partial(forward_kernel, cuts), grid_spec=pltpu.P...  11.3 us
    pallas_call x2, Pallas kernels, finish(): pl.pallas_call(finish_kernel, grid=(share,), in_specs=[full((flip_width,...  9.56 us
    pallas_call x1, Pallas kernels, body(): pl.pallas_call(first_field_kernel, grid=(levels,), in_specs=[pl.BlockSpec...  8.44 us
  transfers between devices with their start and end apart: 25, of which 4 were waited for; matrix products, arithmetic and copies ran while one was open for 4% of the time, Pallas kernels for 67%

profile of v1, /device:TPU:15, one launch (start us, length us, event | category | flops | bytes accessed | tf_op | source)
XLA Modules:
  0.0 361.2 jit_solution(1009621516227634452)
XLA Ops:
  2.5 1.9 collective-permute-start
  4.4 1.3 collective-permute-done
  7.0 8.4 %first_field.1 = (f32[6,128,1024]{2,1,0:T(8,128)}, f32[6,128,1024]{2,1,0:T(8,128)}) custom-call(f32[7,6,128,1024]{3,2,1,0:T(8,128)} %cells.3, f32[6,2,1024]{2,1,0:T(2,128)} %reshape.10.edge, f32[128,1024]{1,0:T(8,128)} %lon.3, f32[128,1024]{1,0:T(8,128)} %lat.3, f32[2,1024]{1,0:T(2,128)} %slice.129.courant_edge, f32[6,128,1024]{2,1,0:T(8,128)} %target.1, ...), custom_call_target="tpu_custom_call" | custom-call | tf_op jit(solution)/shard_map/first_field/pallas_call | solution.py:565
  16.7 1.4 slice.117
  18.1 2.1 collective-permute-start.8
  20.8 1.4 collective-permute-done.1.theirs
  22.2 1.6 copy-done.2
  23.8 11.3 %forward_fourier.1 = (f32[6,128,1024]{2,1,0:T(8,128)}, f32[6,128,1024]{2,1,0:T(8,128)}, f32[6,128,1024]{2,1,0:T(8,128)}, f32[6,128,1024]{2,1,0:T(8,128)}) custom-call(s32[3]{0:T(128)} %pad_add_fusion.place.where, bf16[16,1024,256]{2,1,0:T(8,128)(2,1)} %constant.107.clone.table, f32[6,128,1024]{2,1,0:T(8,128)} %get-tuple-element.66.mine, ...), custom_call_target="tpu_custom_call" | custom-call | tf_op jit(solution)/shard_map/forward_fourier/pallas_call | solution.py:611
  35.1 26.3 %analysis.4 = f32[4,432,128]{2,1,0:T(8,128)} custom-call(s32[3]{0:T(128)} %pad_add_fusion.place.where, s32[36]{0:T(128)} %constant.111.clone.firsts, s32[36]{0:T(128)} %constant.112.clone.locals_, f32[2,36,8,128]{3,2,1,0:T(8,128)} %constant.114.clone.alpha, f32[2,64,512]{2,1,0:T(8,128)} %constant.115.clone.start, f32[2,64,512]{2,1,0:T(8,128)} %constant.116.clone.deficit, ...), custom_call_target="tpu_custom_call" | custom-call | flops 17999998976 | bytes 1048576 | tf_op jit(solution)/shard_map/analysis/pallas_call | solution.py:675
  63.7 26.4 %analysis.5 = f32[4,432,128]{2,1,0:T(8,128)} custom-call(s32[3]{0:T(128)} %pad_add_fusion.place.where, s32[36]{0:T(128)} %constant.111.clone.firsts, s32[36]{0:T(128)} %constant.112.clone.locals_, f32[2,36,8,128]{3,2,1,0:T(8,128)} %constant.119.clone.alpha, f32[2,64,512]{2,1,0:T(8,128)} %constant.120.clone.start, f32[2,64,512]{2,1,0:T(8,128)} %constant.121.clone.deficit, ...), custom_call_target="tpu_custom_call" | custom-call | flops 17999998976 | bytes 1048576 | tf_op jit(solution)/shard_map/analysis/pallas_call | solution.py:675
  91.2 2.0 collective-permute-start.3
  93.3 26.3 %analysis.6 = f32[4,432,128]{2,1,0:T(8,128)} custom-call(s32[3]{0:T(128)} %pad_add_fusion.place.where, s32[36]{0:T(128)} %constant.111.clone.firsts, s32[36]{0:T(128)} %constant.112.clone.locals_, f32[2,36,8,128]{3,2,1,0:T(8,128)} %constant.124.clone.alpha, f32[2,64,512]{2,1,0:T(8,128)} %constant.125.clone.start, f32[2,64,512]{2,1,0:T(8,128)} %constant.126.clone.deficit, ...), custom_call_target="tpu_custom_call" | custom-call | flops 17999998976 | bytes 1048576 | tf_op jit(solution)/shard_map/analysis/pallas_call | solution.py:675
  124.1 26.5 %analysis.7 = f32[4,432,128]{2,1,0:T(8,128)} custom-call(s32[3]{0:T(128)} %pad_add_fusion.place.where, s32[36]{0:T(128)} %constant.111.clone.firsts, s32[36]{0:T(128)} %constant.112.clone.locals_, f32[2,36,8,128]{3,2,1,0:T(8,128)} %constant.129.clone.alpha, f32[2,64,512]{2,1,0:T(8,128)} %constant.130.clone.start, f32[2,64,512]{2,1,0:T(8,128)} %constant.131.clone.deficit, ...), custom_call_target="tpu_custom_call" | custom-call | flops 17999998976 | bytes 1048576 | tf_op jit(solution)/shard_map/analysis/pallas_call | solution.py:675
  152.1 1.8 collective-permute-start.10
  154.1 41.3 %other_fields.1.whole = f32[7,6,128,1024]{3,2,1,0:T(8,128)} custom-call(f32[7,6,128,1024]{3,2,1,0:T(8,128)} %cells.3, f32[36,2,1024]{2,1,0:T(2,128)} %collective-permute-done.8.edge, f32[128,1024]{1,0:T(8,128)} %lon.3, f32[128,1024]{1,0:T(8,128)} %lat.3, f32[2,1024]{1,0:T(2,128)} %slice.129.courant_edge), custom_call_target="tpu_custom_call" | custom-call | flops 14000000000 | bytes 1048576 | tf_op jit(solution)/shard_map/other_fields/pallas_call | solution.py:588
  195.7 1.4 collective-permute-start.13
  197.2 1.4 collective-permute-start.14
  200.8 2.7 tile.8
  203.5 4.7 %tile.9 = f32[328,2,128]{2,1,0:T(2,128)S(1)} reshape(f32[656,16,8]{2,1,0:T(8,128)} %tile.8) | data formatting | bytes 671744 | tf_op jit(solution)/shard_map/tile | solution.py:633
  209.0 2.1 collective-permute-done.16
  212.1 2.3 collective-permute-start.18
  215.1 26.2 %synthesis.4.refs_0_ = f32[6,128,1024]{2,1,0:T(8,128)} custom-call(s32[3]{0:T(128)} %pad_add_fusion.place.where, s32[36]{0:T(128)} %constant.111.clone.firsts, s32[36]{0:T(128)} %constant.112.clone.locals_, s32[36]{0:T(128)} %constant.113.clone.degrees, f32[2,36,8,128]{3,2,1,0:T(8,128)} %constant.114.clone.alpha, f32[2,64,512]{2,1,0:T(8,128)} %constant.115.clone.start, ...), custom_call_target="tpu_custom_call" | custom-call | flops 17999998976 | bytes 1048576 | tf_op jit(solution)/shard_map/synthesis/pallas_call | solution.py:710
  242.4 1.5 collective-permute-start.21
  245.0 26.5 %synthesis.5.refs_1_ = f32[6,128,1024]{2,1,0:T(8,128)} custom-call(s32[3]{0:T(128)} %pad_add_fusion.place.where, s32[36]{0:T(128)} %constant.111.clone.firsts, s32[36]{0:T(128)} %constant.112.clone.locals_, s32[36]{0:T(128)} %constant.118.clone.degrees, f32[2,36,8,128]{3,2,1,0:T(8,128)} %constant.119.clone.alpha, f32[2,64,512]{2,1,0:T(8,128)} %constant.120.clone.start, ...), custom_call_target="tpu_custom_call" | custom-call | flops 17999998976 | bytes 1048576 | tf_op jit(solution)/shard_map/synthesis/pallas_call | solution.py:710
  273.0 26.3 %synthesis.6.refs_2_ = f32[6,128,1024]{2,1,0:T(8,128)} custom-call(s32[3]{0:T(128)} %pad_add_fusion.place.where, s32[36]{0:T(128)} %constant.111.clone.firsts, s32[36]{0:T(128)} %constant.112.clone.locals_, s32[36]{0:T(128)} %constant.123.clone.degrees, f32[2,36,8,128]{3,2,1,0:T(8,128)} %constant.124.clone.alpha, f32[2,64,512]{2,1,0:T(8,128)} %constant.125.clone.start, ...), custom_call_target="tpu_custom_call" | custom-call | flops 17999998976 | bytes 1048576 | tf_op jit(solution)/shard_map/synthesis/pallas_call | solution.py:710
  300.4 26.2 %synthesis.7.refs_3_ = f32[6,128,1024]{2,1,0:T(8,128)} custom-call(s32[3]{0:T(128)} %pad_add_fusion.place.where, s32[36]{0:T(128)} %constant.111.clone.firsts, s32[36]{0:T(128)} %constant.112.clone.locals_, s32[36]{0:T(128)} %constant.128.clone.degrees, f32[2,36,8,128]{3,2,1,0:T(8,128)} %constant.129.clone.alpha, f32[2,64,512]{2,1,0:T(8,128)} %constant.130.clone.start, ...), custom_call_target="tpu_custom_call" | custom-call | flops 17999998976 | bytes 1048576 | tf_op jit(solution)/shard_map/synthesis/pallas_call | solution.py:710
  326.6 7.4 %inverse_fourier.3.mine = f32[2,3,128,1024]{3,2,1,0:T(8,128)} custom-call(s32[3]{0:T(128)} %pad_add_fusion.place.where, bf16[16,512,512]{2,1,0:T(8,128)(2,1)} %constant.108.clone.table, f32[6,128,1024]{2,1,0:T(8,128)} %synthesis.4.refs_0_, f32[6,128,1024]{2,1,0:T(8,128)} %synthesis.5.refs_1_, f32[6,128,1024]{2,1,0:T(8,128)} %synthesis.6.refs_2_, ...), custom_call_target="tpu_custom_call" | custom-call | flops 2000000000 | bytes 1048576 | tf_op jit(solution)/shard_map/inverse_fourier/pallas_call | solution.py:738
  334.0 7.7 %inverse_fourier.2.mine = f32[2,3,128,1024]{3,2,1,0:T(8,128)} custom-call(s32[3]{0:T(128)} %pad_add_fusion.place.where, bf16[16,512,512]{2,1,0:T(8,128)(2,1)} %constant.108.clone.table, f32[6,128,1024]{2,1,0:T(8,128)} %synthesis.4.refs_0_, f32[6,128,1024]{2,1,0:T(8,128)} %synthesis.5.refs_1_, f32[6,128,1024]{2,1,0:T(8,128)} %synthesis.6.refs_2_, ...), custom_call_target="tpu_custom_call" | custom-call | flops 2000000000 | bytes 1048576 | tf_op jit(solution)/shard_map/inverse_fourier/pallas_call | solution.py:738
  341.8 4.5 %collective-permute-start.24 = (f32[3,128,1024]{2,1,0:T(8,128)S(1)}, f32[3,128,1024]{2,1,0:T(8,128)S(1)}, u32[]{:S(2)}, u32[]{:S(2)}) collective-permute-start(f32[3,128,1024]{2,1,0:T(8,128)S(1)} %slice_bitcast_fusion), channel_id=1, source_target_pairs={{0,1},{1,0},{2,3},{3,2},{4,5},{5,4},{6,7},{7,6},{8,9},{9,8},{10,11... | collective-permute-start | bytes 4718600 | tf_op jit(solution)/shard_map/ppermute | solution.py:755
  346.4 1.8 collective-permute-start.23
  350.5 4.9 %finish.2.whole = f32[7,6,128,1024]{3,2,1,0:T(8,128)} custom-call(bf16[256,256]{1,0:T(8,128)(2,1)} %constant.106.clone.flip, f32[6,128,1024]{2,1,0:T(8,128)} %get-tuple-element.65.moved, f32[2,3,128,1024]{3,2,1,0:T(8,128)} %inverse_fourier.3.mine, f32[3,128,1024]{2,1,0:T(8,128)} %copy-done.4, ...), custom_call_target="tpu_custom_call", output_to_operand_aliasing={{}: (4, {})} | custom-call | flops 2000000000 | bytes 1048576 | tf_op jit(solution)/shard_map/finish/pallas_call | solution.py:717
  356.5 4.7 %finish.3 = f32[7,6,128,1024]{3,2,1,0:T(8,128)} custom-call(bf16[256,256]{1,0:T(8,128)(2,1)} %constant.106.clone.flip, f32[6,128,1024]{2,1,0:T(8,128)} %get-tuple-element.65.moved, f32[2,3,128,1024]{3,2,1,0:T(8,128)} %inverse_fourier.2.mine, f32[3,128,1024]{2,1,0:T(8,128)} %copy-done.3, f32[7,6,128,1024]{3,2,1,0:T(8,128)} %finish.2.whole), custom_call_target="tpu_custom_call", output_to_operand_aliasing={{}: (4, {})} | custom-call | flops 2000000000 | bytes 1048576 | tf_op jit(solution)/shard_map/finish/pallas_call | solution.py:717
  (106 shorter events, 28.5 us)
Async XLA Ops:
  2.5 3.2 collective-permute-start
  15.4 6.8 %collective-permute-start.1 = (f32[6,128,1024]{2,1,0:T(8,128)}, f32[6,128,1024]{2,1,0:T(8,128)S(1)}, u32[]{:S(2)}, u32[]{:S(2)}) collective-permute-start(f32[6,128,1024]{2,1,0:T(8,128)} %get-tuple-element.66.mine), channel_id=1, source_target_pairs={{0,1},{1,0},{2,3},{3,2},{4,5},{5,4},{6,7},{7,6},{8,9},{9,8},{10,11... | collective-permute-start | bytes 9437192 | tf_op jit(solution)/shard_map/ppermute | solution.py:582
  18.1 133.8 %collective-permute-start.8 = (f32[36,2,1024]{2,1,0:T(2,128)S(1)}, f32[36,2,1024]{2,1,0:T(2,128)}, u32[]{:S(2)}, u32[]{:S(2)}) collective-permute-start(f32[36,2,1024]{2,1,0:T(2,128)S(1)} %bitcast.16), channel_id=1, source_target_pairs={{0,1},{1,2},{2,3},{3,4},{4,5},{5,6},{6,7},{7,8},{8,9},{9,10},{10,1... | collective-permute-start | bytes 884744 | tf_op jit(solution)/shard_map/ppermute | solution.py:585
  22.2 1.6 copy-start.2
  62.5 27.6 %copy-start.7 = (f32[4,432,128]{2,1,0:T(8,128)S(1)}, f32[4,432,128]{2,1,0:T(8,128)}, u32[]{:S(2)}) copy-start(f32[4,432,128]{2,1,0:T(8,128)} %analysis.4) | copy-start | bytes 2654212
  62.5 27.6 %collective-permute-start.2 = (f32[2,432,128]{2,1,0:T(8,128)S(1)}, f32[2,432,128]{2,1,0:T(8,128)S(1)}, u32[]{:S(2)}, u32[]{:S(2)}) collective-permute-start(f32[2,432,128]{2,1,0:T(8,128)S(1)} %slice.131), channel_id=1, source_target_pairs={{0,2},{1,3},{2,0},{3,1},{4,6},{5,7},{6,4},{7,5},{8,10},{9,11},{10,... | collective-permute-start | bytes 1327112 | tf_op jit(solution)/shard_map/ppermute | solution.py:494
  91.2 28.5 %copy-start.6 = (f32[4,432,128]{2,1,0:T(8,128)S(1)}, f32[4,432,128]{2,1,0:T(8,128)}, u32[]{:S(2)}) copy-start(f32[4,432,128]{2,1,0:T(8,128)} %analysis.5) | copy-start | bytes 2654212
  91.2 28.5 %collective-permute-start.3 = (f32[1,432,128]{2,1,0:T(8,128)S(1)}, f32[1,432,128]{2,1,0:T(8,128)S(1)}, u32[]{:S(2)}, u32[]{:S(2)}) collective-permute-start(f32[1,432,128]{2,1,0:T(8,128)S(1)} %slice.133), channel_id=1, source_target_pairs={{0,4},{1,5},{2,6},{3,7},{4,0},{5,1},{6,2},{7,3},{8,12},{9,13},{10,... | collective-permute-start | bytes 663560 | tf_op jit(solution)/shard_map/ppermute | solution.py:494
  93.2 26.5 %collective-permute-start.4 = (f32[2,432,128]{2,1,0:T(8,128)S(1)}, f32[2,432,128]{2,1,0:T(8,128)S(1)}, u32[]{:S(2)}, u32[]{:S(2)}) collective-permute-start(f32[2,432,128]{2,1,0:T(8,128)S(1)} %slice.113), channel_id=1, source_target_pairs={{0,2},{1,3},{2,0},{3,1},{4,6},{5,7},{6,4},{7,5},{8,10},{9,11},{10,... | collective-permute-start | bytes 1327112 | tf_op jit(solution)/shard_map/ppermute | solution.py:494
  120.9 29.8 %copy-start.5 = (f32[4,432,128]{2,1,0:T(8,128)S(1)}, f32[4,432,128]{2,1,0:T(8,128)}, u32[]{:S(2)}) copy-start(f32[4,432,128]{2,1,0:T(8,128)} %analysis.6) | copy-start | bytes 2654212
  120.9 29.7 %collective-permute-start.5 = (f32[1,432,128]{2,1,0:T(8,128)S(1)}, f32[1,432,128]{2,1,0:T(8,128)S(1)}, u32[]{:S(2)}, u32[]{:S(2)}) collective-permute-start(f32[1,432,128]{2,1,0:T(8,128)S(1)} %slice_add_fusion.7), channel_id=1, source_target_pairs={{0,8},{1,9},{2,10},{3,11},{4,12},{5,13},{6,14},{7,15},{8,0},{9,1},... | collective-permute-start | bytes 663560 | tf_op jit(solution)/shard_map/ppermute | solution.py:494
  121.7 28.9 %collective-permute-start.6 = (f32[1,432,128]{2,1,0:T(8,128)S(1)}, f32[1,432,128]{2,1,0:T(8,128)S(1)}, u32[]{:S(2)}, u32[]{:S(2)}) collective-permute-start(f32[1,432,128]{2,1,0:T(8,128)S(1)} %slice.134), channel_id=1, source_target_pairs={{0,4},{1,5},{2,6},{3,7},{4,0},{5,1},{6,2},{7,3},{8,12},{9,13},{10,... | collective-permute-start | bytes 663560 | tf_op jit(solution)/shard_map/ppermute | solution.py:494
  122.9 27.7 %collective-permute-start.7 = (f32[2,432,128]{2,1,0:T(8,128)S(1)}, f32[2,432,128]{2,1,0:T(8,128)S(1)}, u32[]{:S(2)}, u32[]{:S(2)}) collective-permute-start(f32[2,432,128]{2,1,0:T(8,128)S(1)} %slice.116), channel_id=1, source_target_pairs={{0,2},{1,3},{2,0},{3,1},{4,6},{5,7},{6,4},{7,5},{8,10},{9,11},{10,... | collective-permute-start | bytes 1327112 | tf_op jit(solution)/shard_map/ppermute | solution.py:494
  151.8 43.8 %copy-start.8 = (f32[4,432,128]{2,1,0:T(8,128)S(1)}, f32[4,432,128]{2,1,0:T(8,128)}, u32[]{:S(2)}) copy-start(f32[4,432,128]{2,1,0:T(8,128)} %analysis.7) | copy-start | bytes 2654212
  151.8 43.6 %collective-permute-start.9 = (f32[1,432,128]{2,1,0:T(8,128)S(1)}, f32[1,432,128]{2,1,0:T(8,128)S(1)}, u32[]{:S(2)}, u32[]{:S(2)}) collective-permute-start(f32[1,432,128]{2,1,0:T(8,128)S(1)} %add.65), channel_id=1, source_target_pairs={{0,4},{1,5},{2,6},{3,7},{4,0},{5,1},{6,2},{7,3},{8,12},{9,13},{10,... | collective-permute-start | bytes 663560 | tf_op jit(solution)/shard_map/ppermute | solution.py:494
  152.1 43.4 %collective-permute-start.10 = (f32[1,432,128]{2,1,0:T(8,128)S(1)}, f32[1,432,128]{2,1,0:T(8,128)S(1)}, u32[]{:S(2)}, u32[]{:S(2)}) collective-permute-start(f32[1,432,128]{2,1,0:T(8,128)S(1)} %slice_add_fusion.6), channel_id=1, source_target_pairs={{0,8},{1,9},{2,10},{3,11},{4,12},{5,13},{6,14},{7,15},{8,0},{9,1},... | collective-permute-start | bytes 663560 | tf_op jit(solution)/shard_map/ppermute | solution.py:494
  153.9 41.6 %collective-permute-start.11 = (f32[1,432,128]{2,1,0:T(8,128)S(1)}, f32[1,432,128]{2,1,0:T(8,128)S(1)}, u32[]{:S(2)}, u32[]{:S(2)}) collective-permute-start(f32[1,432,128]{2,1,0:T(8,128)S(1)} %slice.136), channel_id=1, source_target_pairs={{0,4},{1,5},{2,6},{3,7},{4,0},{5,1},{6,2},{7,3},{8,12},{9,13},{10,... | collective-permute-start | bytes 663560 | tf_op jit(solution)/shard_map/ppermute | solution.py:494
  154.0 41.5 %collective-permute-start.12 = (f32[2,432,128]{2,1,0:T(8,128)S(1)}, f32[2,432,128]{2,1,0:T(8,128)S(1)}, u32[]{:S(2)}, u32[]{:S(2)}) collective-permute-start(f32[2,432,128]{2,1,0:T(8,128)S(1)} %slice.121), channel_id=1, source_target_pairs={{0,2},{1,3},{2,0},{3,1},{4,6},{5,7},{6,4},{7,5},{8,10},{9,11},{10,... | collective-permute-start | bytes 1327112 | tf_op jit(solution)/shard_map/ppermute | solution.py:494
  195.7 15.3 %collective-permute-start.13 = (f32[2,432,128]{2,1,0:T(8,128)S(1)}, f32[2,432,128]{2,1,0:T(8,128)S(1)}, u32[]{:S(2)}, u32[]{:S(2)}) collective-permute-start(f32[2,432,128]{2,1,0:T(8,128)S(1)} %get-tuple-element.98), channel_id=1, source_target_pairs={{0,2},{1,3},{2,0},{3,1},{4,6},{5,7},{6,4},{7,5},{8,10},{9,11},{10,... | collective-permute-start | bytes 1327112 | tf_op jit(solution)/shard_map/ppermute | solution.py:494
  197.2 11.8 %collective-permute-start.14 = (f32[1,432,128]{2,1,0:T(8,128)S(1)}, f32[1,432,128]{2,1,0:T(8,128)S(1)}, u32[]{:S(2)}, u32[]{:S(2)}) collective-permute-start(f32[1,432,128]{2,1,0:T(8,128)S(1)} %add.68), channel_id=1, source_target_pairs={{0,4},{1,5},{2,6},{3,7},{4,0},{5,1},{6,2},{7,3},{8,12},{9,13},{10,... | collective-permute-start | bytes 663560 | tf_op jit(solution)/shard_map/ppermute | solution.py:494
  198.5 10.4 %collective-permute-start.15 = (f32[1,432,128]{2,1,0:T(8,128)S(1)}, f32[1,432,128]{2,1,0:T(8,128)S(1)}, u32[]{:S(2)}, u32[]{:S(2)}) collective-permute-start(f32[1,432,128]{2,1,0:T(8,128)S(1)} %slice_add_fusion.5), channel_id=1, source_target_pairs={{0,8},{1,9},{2,10},{3,11},{4,12},{5,13},{6,14},{7,15},{8,0},{9,1},... | collective-permute-start | bytes 663560 | tf_op jit(solution)/shard_map/ppermute | solution.py:494
  199.1 11.9 %collective-permute-start.16 = (f32[1,432,128]{2,1,0:T(8,128)S(1)}, f32[1,432,128]{2,1,0:T(8,128)S(1)}, u32[]{:S(2)}, u32[]{:S(2)}) collective-permute-start(f32[1,432,128]{2,1,0:T(8,128)S(1)} %slice.138), channel_id=1, source_target_pairs={{0,4},{1,5},{2,6},{3,7},{4,0},{5,1},{6,2},{7,3},{8,12},{9,13},{10,... | collective-permute-start | bytes 663560 | tf_op jit(solution)/shard_map/ppermute | solution.py:494
  212.1 29.3 %collective-permute-start.18 = (f32[1,432,128]{2,1,0:T(8,128)S(1)}, f32[1,432,128]{2,1,0:T(8,128)S(1)}, u32[]{:S(2)}, u32[]{:S(2)}) collective-permute-start(f32[1,432,128]{2,1,0:T(8,128)S(1)} %add.71), channel_id=1, source_target_pairs={{0,4},{1,5},{2,6},{3,7},{4,0},{5,1},{6,2},{7,3},{8,12},{9,13},{10,... | collective-permute-start | bytes 663560 | tf_op jit(solution)/shard_map/ppermute | solution.py:494
  214.4 27.0 %collective-permute-start.19 = (f32[1,432,128]{2,1,0:T(8,128)S(1)}, f32[1,432,128]{2,1,0:T(8,128)S(1)}, u32[]{:S(2)}, u32[]{:S(2)}) collective-permute-start(f32[1,432,128]{2,1,0:T(8,128)S(1)} %slice_add_fusion.4), channel_id=1, source_target_pairs={{0,8},{1,9},{2,10},{3,11},{4,12},{5,13},{6,14},{7,15},{8,0},{9,1},... | collective-permute-start | bytes 663560 | tf_op jit(solution)/shard_map/ppermute | solution.py:494
  214.7 26.7 %collective-permute-start.17 = (f32[2,432,128]{2,1,0:T(8,128)S(1)}, f32[2,432,128]{2,1,0:T(8,128)S(1)}, u32[]{:S(2)}, u32[]{:S(2)}) collective-permute-start(f32[2,432,128]{2,1,0:T(8,128)S(1)} %pad_maximum_fusion.5), channel_id=1, source_target_pairs={{0,2},{1,3},{2,0},{3,1},{4,6},{5,7},{6,4},{7,5},{8,10},{9,11},{10,... | collective-permute-start | bytes 1327112 | tf_op jit(solution)/shard_map/ppermute | solution.py:494
  242.4 29.0 %collective-permute-start.21 = (f32[1,432,128]{2,1,0:T(8,128)S(1)}, f32[1,432,128]{2,1,0:T(8,128)S(1)}, u32[]{:S(2)}, u32[]{:S(2)}) collective-permute-start(f32[1,432,128]{2,1,0:T(8,128)S(1)} %add.73), channel_id=1, source_target_pairs={{0,4},{1,5},{2,6},{3,7},{4,0},{5,1},{6,2},{7,3},{8,12},{9,13},{10,... | collective-permute-start | bytes 663560 | tf_op jit(solution)/shard_map/ppermute | solution.py:494
  243.9 27.5 %collective-permute-start.20 = (f32[2,432,128]{2,1,0:T(8,128)S(1)}, f32[2,432,128]{2,1,0:T(8,128)S(1)}, u32[]{:S(2)}, u32[]{:S(2)}) collective-permute-start(f32[2,432,128]{2,1,0:T(8,128)S(1)} %pad_maximum_fusion.6), channel_id=1, source_target_pairs={{0,2},{1,3},{2,0},{3,1},{4,6},{5,7},{6,4},{7,5},{8,10},{9,11},{10,... | collective-permute-start | bytes 1327112 | tf_op jit(solution)/shard_map/ppermute | solution.py:494
  272.5 26.9 %collective-permute-start.22 = (f32[2,432,128]{2,1,0:T(8,128)S(1)}, f32[2,432,128]{2,1,0:T(8,128)S(1)}, u32[]{:S(2)}, u32[]{:S(2)}) collective-permute-start(f32[2,432,128]{2,1,0:T(8,128)S(1)} %pad_maximum_fusion.7), channel_id=1, source_target_pairs={{0,2},{1,3},{2,0},{3,1},{4,6},{5,7},{6,4},{7,5},{8,10},{9,11},{10,... | collective-permute-start | bytes 1327112 | tf_op jit(solution)/shard_map/ppermute | solution.py:494
  334.0 7.7 %copy-start.1 = (f32[2,3,128,1024]{3,2,1,0:T(8,128)S(1)}, f32[2,3,128,1024]{3,2,1,0:T(8,128)}, u32[]{:S(2)}) copy-start(f32[2,3,128,1024]{3,2,1,0:T(8,128)} %inverse_fourier.3.mine) | copy-start | bytes 9437188
  341.7 4.6 %copy-start = (f32[2,3,128,1024]{3,2,1,0:T(8,128)S(1)}, f32[2,3,128,1024]{3,2,1,0:T(8,128)}, u32[]{:S(2)}) copy-start(f32[2,3,128,1024]{3,2,1,0:T(8,128)} %inverse_fourier.2.mine) | copy-start | bytes 9437188
  341.8 7.5 %collective-permute-start.24 = (f32[3,128,1024]{2,1,0:T(8,128)S(1)}, f32[3,128,1024]{2,1,0:T(8,128)S(1)}, u32[]{:S(2)}, u32[]{:S(2)}) collective-permute-start(f32[3,128,1024]{2,1,0:T(8,128)S(1)} %slice_bitcast_fusion), channel_id=1, source_target_pairs={{0,1},{1,0},{2,3},{3,2},{4,5},{5,4},{6,7},{7,6},{8,9},{9,8},{10,11... | collective-permute-start | bytes 4718600 | tf_op jit(solution)/shard_map/ppermute | solution.py:755
  346.4 9.0 %collective-permute-start.23 = (f32[3,128,1024]{2,1,0:T(8,128)S(1)}, f32[3,128,1024]{2,1,0:T(8,128)S(1)}, u32[]{:S(2)}, u32[]{:S(2)}) collective-permute-start(f32[3,128,1024]{2,1,0:T(8,128)S(1)} %slice_bitcast_fusion.1), channel_id=1, source_target_pairs={{0,1},{1,0},{2,3},{3,2},{4,5},{5,4},{6,7},{7,6},{8,9},{9,8},{10,11... | collective-permute-start | bytes 4718600 | tf_op jit(solution)/shard_map/ppermute | solution.py:755
  (3 other events, 3.9 us)

commit v2 on v1

--- a/solution.py
+++ b/solution.py
@@ -12,13 +12,13 @@
 
 STEPS = 2
 GROUP = 8
-STRIPS = 16
+STRIPS = 8
 UNIT = 2
 ROWS = 64
 QUADS = ROWS // 32
 SHIFT = 100
-DROP = 120
-TOP = 20
+DROP = 88
+TOP = -12
 CHUNKS = 4
 F32 = jnp.float32
 BF16 = jnp.bfloat16
@@ -117,19 +117,26 @@
                     continue
                 waves = GROUP * (2 * chunk[local] + core) + np.arange(GROUP)
                 out_alpha[core, i, :, :ROWS] = alpha[waves, ROWS * b : ROWS * (b + 1)]
-                squares = c[waves][:, ROWS * b + rows] ** 2 * 2.0**-SHIFT
-                out_c[core, i] = np.tile(squares.T, (1, 128 // GROUP))
+                squares = (c[waves][:, ROWS * b + rows] ** 2 * 2.0**-SHIFT).T
+                squares = squares.reshape(ROWS // GROUP, GROUP, GROUP)
+                for w in range(GROUP):
+                    squares[:, :, w] = np.roll(squares[:, :, w], w, axis=1)
+                out_c[core, i] = np.tile(squares.reshape(ROWS, GROUP), (1, 128 // GROUP))
+        out_start, out_deficit = [
+            t.reshape(2, -1, 2, self.half // 2).transpose(0, 2, 1, 3).reshape(4, -1, self.half // 2)
+            for t in (out_start, out_deficit)
+        ]
         return out_alpha, out_start, out_deficit, out_c
 
     def fourier_tables(self):
         local = self.lons // self.band
-        forward = np.zeros((self.band, self.waves, 2 * local))
-        inverse = np.zeros((self.band, 2 * local, self.waves))
+        forward = np.zeros((self.band, self.waves, 4 * local))
+        inverse = np.zeros((self.band, 4 * local, self.waves))
         for place in range(self.band):
             waves = self.wave_ids(place % 2)
-            lons = np.concatenate([local * place + np.arange(local), local * (place ^ 1) + np.arange(local)])
+            lons = np.concatenate([local * (place ^ i) + np.arange(local) for i in (0, 2, 1, 3)])
             phase = (waves[:, :, None] * lons % self.lons) * (2 * math.pi / self.lons)
-            both = np.stack([np.cos(phase), -np.sin(phase)], axis=1).reshape(self.waves, 2 * local)
+            both = np.stack([np.cos(phase), -np.sin(phase)], axis=1).reshape(self.waves, 4 * local)
             double = np.where(waves == 0, 1.0, 2.0)
             double = np.stack([double, double], axis=1).reshape(self.waves)
             forward[place] = both / self.lons
@@ -155,12 +162,13 @@
         before, before_once = carry
         rows = pl.ds(pl.multiple_of(8 * i, 8), 8)
         now, east, north = cells[rows, :], lon[rows, :], lat[rows, :]
+        stay = 1.0 - east - north
         turned = pltpu.roll(now, 1, 0)
         west = jnp.where(row_ids == 0, before, turned)
-        once = now - east * (now - west) - north * (now - south_of(now, lane_ids))
+        once = stay * now + east * west + north * south_of(now, lane_ids)
         turned_once = pltpu.roll(once, 1, 0)
         west = jnp.where(row_ids == 0, before_once, turned_once)
-        store(rows, once - east * (once - west) - north * (once - south_of(once, lane_ids)))
+        store(rows, stay * once + east * west + north * south_of(once, lane_ids))
         return turned, turned_once
 
     lax.fori_loop(0, cells.shape[0] // 8, strip, (inner, inner_once), unroll=STRIPS)
@@ -178,7 +186,7 @@
     return jnp.concatenate(pieces, axis=1)
 
 
-def first_field_kernel(cells, edge, lon, lat, courant_edge, target, flip, moved, folded):
+def first_field_kernel(where, cells, edge, lon, lat, courant_edge, target, flip, moved, keep, send):
     def store(rows, values):
         moved[0, rows, :] = values
 
@@ -189,31 +197,45 @@
     half = anomaly.shape[1] // 2
     north = anomaly[:, :half]
     south = reversed_lanes(anomaly[:, half:], flip[...])
-    folded[0, :, :half] = north + south
-    folded[0, :, half:] = north - south
+    second = where[3] == 1
+    for part, values in enumerate((north + south, north - south)):
+        lanes = slice(part * half // 2, (part + 1) * half // 2)
+        one, two = values[:, : half // 2], values[:, half // 2 :]
+        keep[0, :, lanes] = jnp.where(second, two, one)
+        send[0, :, lanes] = jnp.where(second, one, two)
 
 
 def other_fields_kernel(cells, edge, lon, lat, courant_edge, moved):
-    def store(rows, values):
-        moved[0, 0, rows, :] = values
-
-    two_steps(
-        cells.at[0, 0], edge[0], lon, lat, courant_edge[0:1], courant_edge[1:2], store
-    )
-
-
-def finish_kernel(flip, moved, mine, theirs, whole, out):
+    for p in range(cells.shape[1]):
+
+        def store(rows, values):
+            moved[0, p, rows, :] = values
+
+        two_steps(
+            cells.at[0, p], edge[p], lon, lat, courant_edge[0:1], courant_edge[1:2], store
+        )
+
+
+def finish_kernel(where, flip, moved, mine, theirs, far, whole, out):
     del whole
-    total = mine[0, 0] + theirs[0]
-    half = total.shape[1] // 2
-    even, odd = total[:, :half], total[:, half:]
+    near, far = mine[0, 0] + theirs[0], far[0]
+    part = near.shape[1] // 2
+    second = where[3] == 1
+    ends = []
+    for lanes in (slice(0, part), slice(part, 2 * part)):
+        one, two = near[:, lanes], far[:, lanes]
+        ends.append(
+            jnp.concatenate([jnp.where(second, two, one), jnp.where(second, one, two)], axis=1)
+        )
+    even, odd = ends
+    half = 2 * part
     out[0, 0, :, :half] = moved[0, :, :half] + (even + odd)
     out[0, 0, :, half:] = moved[0, :, half:] + reversed_lanes(even - odd, flip[...])
 
 
-def forward_kernel(cuts, place, table, mine, theirs, quad, *outs):
+def forward_kernel(cuts, place, table, one, two, three, four, quad, *outs):
     del place
-    a_high, a_low = split(jnp.concatenate([mine[0], theirs[0]], axis=0))
+    a_high, a_low = split(jnp.concatenate([one[0], two[0], three[0], four[0]], axis=0))
     waves = table.shape[1] // 2
     wide = dot(table[0], a_high)
     total = (wide[:waves] + (wide[waves:] + dot(table[0, :waves], a_low))) * quad[...]
@@ -228,7 +250,8 @@
     lons = table.shape[1] // 2
     wide = dot(table[0], s_high)
     total = wide[:lons] + (wide[lons:] + dot(table[0, :lons], s_low))
-    out[0, 0], out[1, 0] = total[: lons // 2], total[lons // 2 :]
+    for i in range(4):
+        out[i, 0] = total[i * lons // 4 : (i + 1) * lons // 4]
 
 
 def table_block(index, first, local, carry, alpha, start, deficit, mu, scaled, even, odd):
@@ -248,7 +271,7 @@
     for segment in range(0, ROWS, 16):
         for b in range(count):
             if scaled[b]:
-                large = jnp.maximum(jnp.abs(earlier[b]), jnp.abs(latest[b])) > 2.0**TOP
+                large = jnp.abs(latest[b]) > 2.0**TOP
                 down = jnp.logical_and(large, owed[b] > 0.0)
                 factor = jnp.where(down, 2.0**-DROP, 1.0)
                 earlier[b] = earlier[b] * factor
@@ -267,55 +290,78 @@
                     pair = jnp.concatenate(
                         [values[b][k + parity], values[b][k + parity + 2]], axis=0
                     )
-                    if scaled[b]:
-                        keep = jnp.concatenate([owed[b], owed[b]], axis=0) == 0.0
-                        pair = jnp.where(keep, pair, 0.0)
                     high, low = split(pair)
                     at = 4 * k
                     store[at : at + 16, lanes] = high
                     store[4 * ROWS + at : 4 * ROWS + at + 16, lanes] = low
+        yield
     return tuple(earlier), tuple(latest), tuple(owed)
 
 
-def own_lane_mask(value):
-    wave = lax.broadcasted_iota(jnp.int32, (GROUP, 128), 0)
+def lane_lag():
+    row = lax.broadcasted_iota(jnp.int32, (GROUP, 128), 0)
     lane = lax.broadcasted_iota(jnp.int32, (GROUP, 128), 1)
-    return jnp.where(lane % GROUP == wave, value, 0.0)
-
-
-def run_blocks(count, tables, use, lat_blocks, scaled, buffers):
+    return (row + 128 - lane) % GROUP
+
+
+def skewed(rows, lag):
+    tile = rows[:GROUP]
+    for k in range(1, GROUP):
+        tile = jnp.where(lag == k, pltpu.roll(rows[GROUP * k : GROUP * (k + 1)], k, 0), tile)
+    return tile
+
+
+def unskewed(tile, own):
+    rows = [jnp.where(own, tile, 0.0)]
+    for k in range(1, GROUP):
+        rows.append(jnp.where(own, pltpu.roll(tile, GROUP - k, 0), 0.0))
+    return jnp.concatenate(rows, axis=0)
+
+
+def run_blocks(count, tables, use, lat_blocks, scaled, sets):
     firsts, locals_, alpha, start, deficit, mu = tables
-    ahead, behind = buffers
+    sets = [as_pairs(ref) for ref in sets]
     angles = jnp.broadcast_to(mu[...], (GROUP, mu.shape[1]))
     zero = jnp.zeros((GROUP, 128), F32)
     carry = tuple(tuple(zero for _ in range(lat_blocks)) for _ in range(3))
 
     def stage(base, carry, made, used):
-        use([jnp.maximum(base - UNIT + j, j) for j in range(UNIT)], used)
-        for j in range(UNIT):
-            i = base + j
-            carry = table_block(
-                i, firsts[i], locals_[i], carry, alpha, start, deficit, angles, scaled, *made[j]
-            )
+        using = use([jnp.maximum(base - UNIT + j, j) for j in range(UNIT)], used)
+
+        def making(carry):
+            for j in range(UNIT):
+                i = base + j
+                carry = yield from table_block(
+                    i, firsts[i], locals_[i], carry, alpha, start, deficit, angles, scaled, *made[j]
+                )
+            return carry
+
+        making = making(carry)
+        pieces, segments = 2 * UNIT, UNIT * ROWS // 16
+        for piece in range(pieces):
+            next(using)
+            for _ in range(segments // pieces):
+                next(making)
+        for _ in using:
+            pass
+        try:
+            next(making)
+        except StopIteration as stop:
+            return stop.value
+
+    def two(step, carry):
+        for turn in range(2):
+            made, used = sets[turn], sets[1 - turn]
+            carry = stage(UNIT * (2 * step + turn), carry, made, used)
         return carry
 
-    def two(step, carry):
-        carry = stage(2 * UNIT * step, carry, ahead, behind)
-        return stage(2 * UNIT * step + UNIT, carry, behind, ahead)
-
     lax.fori_loop(0, count // (2 * UNIT), two, carry)
-    use([jnp.int32(count - UNIT + j) for j in range(UNIT)], behind)
-
-
-def buffer_pairs(refs):
-    pairs = [(refs[2 * j], refs[2 * j + 1]) for j in range(2 * UNIT)]
-    return pairs[:UNIT], pairs[UNIT:]
-
-
-def clear(pairs):
-    for pair in pairs:
-        for ref in pair:
-            ref[...] = jnp.zeros_like(ref)
+    for _ in use([jnp.int32(count - UNIT + j) for j in range(UNIT)], sets[1]):
+        pass
+
+
+def as_pairs(ref):
+    return [(ref.at[2 * j], ref.at[2 * j + 1]) for j in range(UNIT)]
 
 
 def slot_of(item, count, owned):
@@ -335,11 +381,13 @@
     deficit,
     mu,
     waves,
-    out,
+    keep,
+    send,
+    slots,
     weights,
-    *refs,
+    set_a,
+    set_b,
 ):
-    buffers = buffer_pairs(refs)
     groups = waves.shape[1] // (2 * GROUP)
     half = waves.shape[2] // 2
     columns = levels * 2 * GROUP
@@ -355,29 +403,23 @@
         return 0
 
     lax.fori_loop(0, groups, prepare, 0)
-    clear(buffers[1])
+    set_b[...] = jnp.zeros_like(set_b)
     owned = where[1]
-    mask = own_lane_mask(2.0**-SHIFT)
+    lag = lane_lag()
     lane = lax.broadcasted_iota(jnp.int32, (GROUP, 128), 1)
     table = 4 * ROWS
 
     def use(items, stores):
-        products = []
         for item, pair in zip(items, stores):
-            group = locals_[item]
-            products.append([dot(pair[p][...], weights[group, p]) for p in range(2)])
-        for item, pair in zip(items, products):
             sums = []
-            for both in pair:
+            for parity in range(2):
+                both = dot(pair[parity][...], weights[locals_[item], parity])
+                yield
                 product = both[:table, 0:128] + (both[:table, 128:256] + both[table:, 0:128])
-                picked = product.reshape(table // GROUP, GROUP, 128) * mask[None]
-                sums.append(jnp.sum(picked, axis=1))
+                sums += [skewed(product[64 * j : 64 * (j + 1)], lag) for j in range(ROWS // 16)]
             slot, at = slot_of(item, count, owned)
             for quad in range(QUADS):
-                tiles = []
-                for j in range(4 * quad, 4 * quad + 4):
-                    parity, row = divmod(8 * j, ROWS // 2)
-                    tiles.append(sums[parity][row : row + 8])
+                tiles = sums[4 * quad : 4 * quad + 4]
                 second, third = pltpu.roll(tiles[1], 96, 1), pltpu.roll(tiles[2], 64, 1)
                 packed = (
                     jnp.where(lane < 96, tiles[0], second),
@@ -386,7 +428,7 @@
                 )
                 for j in range(3):
                     rows = pl.ds(pl.multiple_of(at + 24 * quad + 8 * j, 8), 8)
-                    out[slot, rows, :] = packed[j]
+                    slots[slot, rows, :] = packed[j] * 2.0**-SHIFT
 
     run_blocks(
         count,
@@ -394,39 +436,24 @@
         use,
         half // 128,
         scaled,
-        buffers,
+        (set_a, set_b),
     )
-
-
-def synthesis_kernel(
-    count,
-    levels,
-    scaled,
-    where,
-    firsts,
-    locals_,
-    degrees,
-    alpha,
-    start,
-    deficit,
-    mu,
-    squares,
-    rates,
-    coeffs,
-    out,
-    *refs,
+    keep[...], send[...] = slots[0:2], slots[2:4]
+
+
+def synthesis_use(
+    count, levels, half, where, locals_, degrees, squares, rates, own_quarter, next_quarter,
+    other_half, out, coeffs,
 ):
-    buffers = buffer_pairs(refs)
-    half = mu.shape[1]
     columns = levels * 2 * GROUP
-    clear(buffers[1])
     owned = where[1]
-    mask = own_lane_mask(1.0)
     lane = lax.broadcasted_iota(jnp.int32, (GROUP, 128), 1)
+    own = jnp.logical_and(lane_lag() == 0, lane < columns)
+    out[...] = jnp.zeros_like(out)
+    coeffs[0:1], coeffs[1:2], coeffs[2:4] = own_quarter[...], next_quarter[...], other_half[...]
     table = 4 * ROWS
 
     def use(items, stores):
-        totals = []
         for item, pair in zip(items, stores):
             slot, at = slot_of(item, count, owned)
             tiles = []
@@ -447,8 +474,8 @@
                 parts = tiles[parity * 2 * QUADS : (parity + 1) * 2 * QUADS]
                 scale = squares[0, item, share * parity : share * (parity + 1)]
                 block = jnp.concatenate(parts, axis=0) * (scale * rates[parity, degree_rows])
-                wide = jnp.broadcast_to(block[:, None, :], (share, GROUP, 128)) * mask[None]
-                high, low = split(wide.reshape(table, 128).T[:columns])
+                wide = [unskewed(block[8 * j : 8 * j + 8], own) for j in range(share // 8)]
+                high, low = split(jnp.concatenate(wide, axis=0).T[:columns])
                 left = jnp.concatenate(
                     [
                         jnp.concatenate([high, high], axis=1),
@@ -457,34 +484,63 @@
                     axis=0,
                 )
                 total = dot(left, pair[parity][...])
-                totals.append(total[:columns] + total[columns:])
-        for j, item in enumerate(items):
-            target = pl.ds(pl.multiple_of(locals_[item] * 2 * GROUP, 2 * GROUP), 2 * GROUP)
-            for parity in range(2):
+                yield
+                total = (total[:columns] + total[columns:]).reshape(levels, 2 * GROUP, half)
+                target = pl.ds(pl.multiple_of(locals_[item] * 2 * GROUP, 2 * GROUP), 2 * GROUP)
                 lanes = slice(parity * half, (parity + 1) * half)
-                before = jnp.where(firsts[item] == 1, 0.0, out[:, target, lanes])
-                total = totals[2 * j + parity].reshape(levels, 2 * GROUP, half)
-                out[:, target, lanes] = before + total
-
+                out[:, target, lanes] = out[:, target, lanes] + total
+
+    return use
+
+
+def synthesis_kernel(
+    count,
+    levels,
+    scaled,
+    where,
+    firsts,
+    locals_,
+    degrees,
+    alpha,
+    start,
+    deficit,
+    mu,
+    squares,
+    rates,
+    own_quarter,
+    next_quarter,
+    other_half,
+    out,
+    coeffs,
+    set_a,
+    set_b,
+):
+    half = mu.shape[1]
+    set_b[...] = jnp.zeros_like(set_b)
+    use = synthesis_use(
+        count, levels, half, where, locals_, degrees, squares, rates, own_quarter, next_quarter,
+        other_half, out, coeffs,
+    )
     run_blocks(
         count,
         (firsts, locals_, alpha, start, deficit, mu),
         use,
         half // 128,
         scaled,
-        buffers,
+        (set_a, set_b),
     )
 
 
 def chip_sum(slots, band_count):
     chips = band_count // 2
     steps = [1 << b for b in range(chips.bit_length() - 1)]
-    part = slots[:2] + (yield slots[2:], steps[0])
-    part = part[:1] + (yield part[1:], steps[1])
+    keep, send = slots
+    keep = keep + (yield send, steps[0])
+    part = keep[:1] + (yield keep[1:], steps[1])
     for step in steps[2:]:
         part = part + (yield part, step)
-    part = jnp.concatenate([part, (yield part, steps[1])], axis=0)
-    return jnp.concatenate([part, (yield part, steps[0])], axis=0)
+    near = yield part, steps[1]
+    return part, near, (yield jnp.concatenate([part, near], axis=0), steps[0])
 
 
 def chip_move(value, step, band_count):
@@ -544,7 +600,8 @@
     plane = (lon_local, lat_total)
     chip = place // 2
     owned = 2 * (chip % 2) + (chip // 2) % 2
-    where = jnp.stack([place % 2, owned, place]).astype(jnp.int32)
+    second = chip % 2
+    where = jnp.stack([place % 2, owned, place, second, 2 * (place % 2) + second]).astype(jnp.int32)
 
     east = [(i, (i + 1) % band_count) for i in range(band_count)]
     peer = [(i, i ^ 1) for i in range(band_count)]
@@ -562,81 +619,102 @@
     flip_width = min(256, half)
     flip = jnp.asarray(np.eye(flip_width)[::-1].astype(ml_dtypes.bfloat16))
 
-    moved, folded = pl.pallas_call(
+    share_lat = lat_total // 2
+    strip = (lon_local, share_lat)
+    moved, keep, send = pl.pallas_call(
         first_field_kernel,
-        grid=(levels,),
-        in_specs=[
-            pl.BlockSpec((1, 1) + plane, lambda l: (0, l, 0, 0)),
-            pl.BlockSpec((1, STEPS, lat_total), lambda l: (l, 0, 0)),
-            full(plane),
-            full(plane),
-            full((2, lat_total)),
-            pl.BlockSpec((1,) + plane, lambda l: (l, 0, 0)),
-            full((flip_width, flip_width)),
-        ],
-        out_specs=[pl.BlockSpec((1,) + plane, lambda l: (l, 0, 0))] * 2,
-        out_shape=[jax.ShapeDtypeStruct((levels,) + plane, F32)] * 2,
+        grid_spec=pltpu.PrefetchScalarGridSpec(
+            num_scalar_prefetch=1,
+            grid=(levels,),
+            in_specs=[
+                pl.BlockSpec((1, 1) + plane, lambda l, w: (0, l, 0, 0)),
+                pl.BlockSpec((1, STEPS, lat_total), lambda l, w: (l, 0, 0)),
+                full(plane),
+                full(plane),
+                full((2, lat_total)),
+                pl.BlockSpec((1,) + plane, lambda l, w: (l, 0, 0)),
+                full((flip_width, flip_width)),
+            ],
+            out_specs=[pl.BlockSpec((1,) + plane, lambda l, w: (l, 0, 0))]
+            + [pl.BlockSpec((1,) + strip, lambda l, w: (l, 0, 0))] * 2,
+        ),
+        out_shape=[jax.ShapeDtypeStruct((levels,) + plane, F32)]
+        + [jax.ShapeDtypeStruct((levels,) + strip, F32)] * 2,
         compiler_params=params(),
         name="first_field",
-    )(state, first_edge, courant_lon, courant_lat, courant_edge, reference_field, flip)
-    peer_folded = lax.ppermute(folded, "band", peer)
+    )(where, state, first_edge, courant_lon, courant_lat, courant_edge, reference_field, flip)
+    across = [(i, i ^ 2) for i in range(band_count)]
+    peer_keep = lax.ppermute(keep, "band", peer)
 
     other_rows = state[1:, :, lon_local - STEPS :, :].reshape((fields - 1) * levels, STEPS, lat_total)
     other_edge = lax.ppermute(other_rows, "band", east)
 
-    def others_call(state, other_edge, courant_lon, courant_lat, courant_edge):
+    def others_call(first, last, *operands):
+        def at(i):
+            return (1 + first + i, 0, 0, 0)
+
         return pl.pallas_call(
             other_fields_kernel,
-            grid=((fields - 1) * levels,),
+            grid=(last - first,),
             in_specs=[
-                pl.BlockSpec((1, 1) + plane, lambda i: (1 + i // levels, i % levels, 0, 0)),
-                pl.BlockSpec((1, STEPS, lat_total), lambda i: (i, 0, 0)),
+                pl.BlockSpec((1, levels) + plane, at),
+                pl.BlockSpec((levels, STEPS, lat_total), lambda i: (first + i, 0, 0)),
                 full(plane),
                 full(plane),
                 full((2, lat_total)),
             ],
-            out_specs=pl.BlockSpec((1, 1) + plane, lambda i: (1 + i // levels, i % levels, 0, 0)),
+            out_specs=pl.BlockSpec((1, levels) + plane, at),
             out_shape=jax.ShapeDtypeStruct(state.shape, F32),
             compiler_params=params(),
-            cost_estimate=cost(14.0),
+            cost_estimate=cost(28.0),
             name="other_fields",
-        )(state, other_edge, courant_lon, courant_lat, courant_edge)
+        )(*operands)
+
+    reach = wave_total + 2 * GROUP + 2 * ROWS
+    padded = jnp.concatenate([nudge_rate, jnp.zeros((2 * reach,), F32)])
+    padded = lax.dynamic_slice(padded, ((place % 2) * GROUP,), (reach + GROUP,))
+    by_wave = [
+        jnp.roll(padded[w : w + reach].reshape(reach // 16, GROUP, 2), w, axis=1)
+        for w in range(GROUP)
+    ]
+    by_wave = jnp.stack(by_wave, axis=-1).reshape(reach // 2, 2, GROUP).transpose(1, 0, 2)
+    rates = jnp.broadcast_to(by_wave[:, :, None, :], (2, reach // 2, 128 // GROUP, GROUP))
+    rates = rates.reshape(2, reach // 2, 128)
+
+    send, other_edge = lax.optimization_barrier((send, other_edge))
+    far_keep = lax.ppermute(send, "band", across)
+    others = others_call(0, fields - 1, state, other_edge, courant_lon, courant_lat, courant_edge)
+    others, rates, far_keep = lax.optimization_barrier((others, rates, far_keep))
+    peer_far = lax.ppermute(far_keep, "band", peer)
 
     forward, inverse = [jnp.asarray(t) for t in lay.fourier_tables()]
     quad = (math.pi / lat_total) * np.sin(lay.angles)
-    quad = jnp.asarray(np.concatenate([quad, quad])[None].astype(np.float32))
-    mu = jnp.asarray(np.cos(lay.angles)[None].astype(np.float32))
+    quad = np.tile(quad.reshape(2, 1, half // 2), (1, 1, 2))
+    quad = jnp.asarray(quad.astype(np.float32))
+    mu = jnp.asarray(np.cos(lay.angles).reshape(2, 1, half // 2).astype(np.float32))
+    half = half // 2
     cuts = lay.cuts
-    pair_lon = 2 * lon_local
+    near_lon = 4 * lon_local
     spectra = pl.pallas_call(
         functools.partial(forward_kernel, cuts),
         grid_spec=pltpu.PrefetchScalarGridSpec(
             num_scalar_prefetch=1,
             grid=(levels,),
-            in_specs=[
-                pl.BlockSpec((1, 2 * wave_total, pair_lon), lambda l, w: (w[2], 0, 0)),
-                pl.BlockSpec((1,) + plane, lambda l, w: (l, 0, 0)),
-                pl.BlockSpec((1,) + plane, lambda l, w: (l, 0, 0)),
-                full((1, lat_total)),
-            ],
-            out_specs=[pl.BlockSpec((1, e - b, lat_total), lambda l, w: (l, 0, 0)) for b, e in cuts],
+            in_specs=[pl.BlockSpec((1, 2 * wave_total, near_lon), lambda l, w: (w[2], 0, 0))]
+            + [pl.BlockSpec((1,) + strip, lambda l, w: (l, 0, 0))] * 4
+            + [pl.BlockSpec((None, 1, share_lat), lambda l, w: (w[3], 0, 0))],
+            out_specs=[pl.BlockSpec((1, e - b, share_lat), lambda l, w: (l, 0, 0)) for b, e in cuts],
         ),
-        out_shape=[jax.ShapeDtypeStruct((levels, e - b, lat_total), F32) for b, e in cuts],
+        out_shape=[jax.ShapeDtypeStruct((levels, e - b, share_lat), F32) for b, e in cuts],
         compiler_params=params(),
+        cost_estimate=cost(8.0),
         name="forward_fourier",
-    )(where, forward, folded, peer_folded, quad)
-
-    reach = wave_total + 2 * GROUP + 2 * ROWS
-    padded = jnp.concatenate([nudge_rate, jnp.zeros((2 * reach,), F32)])
-    padded = lax.dynamic_slice(padded, ((place % 2) * GROUP,), (reach + GROUP,))
-    by_wave = jnp.stack([padded[w : w + reach] for w in range(GROUP)], axis=1)
-    rates = jnp.tile(by_wave, (1, 128 // GROUP)).reshape(reach // 2, 2, 128).transpose(1, 0, 2)
+    )(where, forward, keep, far_keep, peer_keep, peer_far, quad)
 
     deficits = lay.starts[1]
-    scaled = tuple(
-        bool(np.any(deficits[:, 128 * b : 128 * (b + 1)] > 0)) for b in range(half // 128)
-    )
-    buffers = [pltpu.VMEM((8 * ROWS, half), BF16)] * (4 * UNIT)
+    wanted = np.any(deficits > 0, axis=0).reshape(2, half // 128, 128)
+    scaled = tuple(bool(w) for w in np.any(wanted, axis=(0, 2)))
+    buffers = [pltpu.VMEM((2 * UNIT, 8 * ROWS, half), BF16)] * 2
     smem = pl.BlockSpec(memory_space=pltpu.SMEM)
     plans = []
     pipeline = Pipeline(band_count)
@@ -651,9 +729,9 @@
         alpha, start, deficit, squares = [jnp.asarray(t) for t in lay.tables(chunk)]
         table_specs = [
             pl.BlockSpec((1, count, GROUP, 128), lambda i, w: (w[0], 0, 0, 0)),
-            pl.BlockSpec((1, GROUP * len(chunk), half), lambda i, w: (w[0], 0, 0)),
-            pl.BlockSpec((1, GROUP * len(chunk), half), lambda i, w: (w[0], 0, 0)),
-            full((1, half)),
+            pl.BlockSpec((1, GROUP * len(chunk), half), lambda i, w: (w[4], 0, 0)),
+            pl.BlockSpec((1, GROUP * len(chunk), half), lambda i, w: (w[4], 0, 0)),
+            pl.BlockSpec((None, 1, half), lambda i, w: (w[3], 0, 0)),
         ]
         rows = count // 4 * 24 * QUADS
         call = pl.pallas_call(
@@ -662,10 +740,14 @@
                 num_scalar_prefetch=1,
                 grid=(1,),
                 in_specs=[smem, smem] + table_specs + [full(spectra[q].shape)],
-                out_specs=full((4, rows, 128)),
-                scratch_shapes=[pltpu.VMEM((len(chunk), 2, half, 256), BF16)] + buffers,
+                out_specs=[full((2, rows, 128))] * 2,
+                scratch_shapes=[
+                    pltpu.VMEM((4, rows, 128), F32),
+                    pltpu.VMEM((len(chunk), 2, half, 256), BF16),
+                ]
+                + buffers,
             ),
-            out_shape=jax.ShapeDtypeStruct((4, rows, 128), F32),
+            out_shape=[jax.ShapeDtypeStruct((2, rows, 128), F32)] * 2,
             compiler_params=params(),
             cost_estimate=cost(0.5 * count),
             name="analysis",
@@ -677,27 +759,28 @@
         pipeline.begin(q, slots)
         plans.append((count, firsts, locals_, degrees, alpha, start, deficit, squares, table_specs, rows))
 
-    others = pipeline.compute([other_edge], lambda edge: others_call(state, edge, courant_lon, courant_lat, courant_edge))
     synths = []
     for q, plan in enumerate(plans):
         count, firsts, locals_, degrees, alpha, start, deficit, squares, table_specs, rows = plan
         while q not in pipeline.done:
             pipeline.compute([], lambda: ())
         shape = spectra[q].shape
+        sum_specs = [
+            pl.BlockSpec((1, count, ROWS, 128), lambda i, w: (w[0], 0, 0, 0)),
+            full(rates.shape),
+            full((1, rows, 128)),
+            full((1, rows, 128)),
+            full((2, rows, 128)),
+        ]
+        operands = [firsts, locals_, degrees, alpha, start, deficit, mu]
         call = pl.pallas_call(
             functools.partial(synthesis_kernel, count, levels, scaled),
             grid_spec=pltpu.PrefetchScalarGridSpec(
                 num_scalar_prefetch=1,
                 grid=(1,),
-                in_specs=[smem, smem, smem]
-                + table_specs
-                + [
-                    pl.BlockSpec((1, count, ROWS, 128), lambda i, w: (w[0], 0, 0, 0)),
-                    full(rates.shape),
-                    full((4, rows, 128)),
-                ],
+                in_specs=[smem, smem, smem] + table_specs + sum_specs,
                 out_specs=full(shape),
-                scratch_shapes=buffers,
+                scratch_shapes=[pltpu.VMEM((4, rows, 128), F32)] + buffers,
             ),
             out_shape=jax.ShapeDtypeStruct(shape, F32),
             compiler_params=params(),
@@ -706,31 +789,33 @@
         )
         synths.append(
             pipeline.compute(
-                [pipeline.done[q]],
-                lambda coeffs: call(
-                    where, firsts, locals_, degrees, alpha, start, deficit, mu, squares, rates, coeffs
-                ),
+                pipeline.done[q],
+                lambda *sums: call(where, *operands, squares, rates, *sums),
             )
         )
 
-    def finish(begin, share, both, theirs, whole):
+    def finish(begin, share, both, theirs, far, whole):
         return pl.pallas_call(
             finish_kernel,
-            grid=(share,),
-            in_specs=[
-                full((flip_width, flip_width)),
-                pl.BlockSpec((1,) + plane, lambda l: (l + begin, 0, 0)),
-                pl.BlockSpec((1, 1) + plane, lambda l: (0, l, 0, 0)),
-                pl.BlockSpec((1,) + plane, lambda l: (l, 0, 0)),
-                pl.BlockSpec(memory_space=pl.ANY),
-            ],
-            out_specs=pl.BlockSpec((1, 1) + plane, lambda l: (0, l + begin, 0, 0)),
+            grid_spec=pltpu.PrefetchScalarGridSpec(
+                num_scalar_prefetch=1,
+                grid=(share,),
+                in_specs=[
+                    full((flip_width, flip_width)),
+                    pl.BlockSpec((1,) + plane, lambda l, w: (l + begin, 0, 0)),
+                    pl.BlockSpec((1, 1) + strip, lambda l, w: (0, l, 0, 0)),
+                    pl.BlockSpec((1,) + strip, lambda l, w: (l, 0, 0)),
+                    pl.BlockSpec((1,) + strip, lambda l, w: (l, 0, 0)),
+                    pl.BlockSpec(memory_space=pl.ANY),
+                ],
+                out_specs=pl.BlockSpec((1, 1) + plane, lambda l, w: (0, l + begin, 0, 0)),
+            ),
             out_shape=jax.ShapeDtypeStruct(state.shape, F32),
-            input_output_aliases={4: 0},
+            input_output_aliases={6: 0},
             compiler_params=params(),
             cost_estimate=cost(2.0),
             name="finish",
-        )(flip, moved, both, theirs, whole)
+        )(where, flip, moved, both, theirs, far, whole)
 
     parts = []
     share = levels // 2 if levels % 2 == 0 else levels
@@ -740,22 +825,23 @@
             grid_spec=pltpu.PrefetchScalarGridSpec(
                 num_scalar_prefetch=1,
                 grid=(share,),
-                in_specs=[pl.BlockSpec((1, 2 * pair_lon, wave_total), lambda l, w: (w[2], 0, 0))]
+                in_specs=[pl.BlockSpec((1, 2 * near_lon, wave_total), lambda l, w: (w[2], 0, 0))]
                 + [
-                    pl.BlockSpec((1, e - b, lat_total), lambda l, w, begin=begin: (l + begin, 0, 0))
+                    pl.BlockSpec((1, e - b, share_lat), lambda l, w, begin=begin: (l + begin, 0, 0))
                     for b, e in cuts
                 ],
-                out_specs=pl.BlockSpec((2, 1) + plane, lambda l, w: (0, l, 0, 0)),
+                out_specs=pl.BlockSpec((4, 1) + strip, lambda l, w: (0, l, 0, 0)),
             ),
-            out_shape=jax.ShapeDtypeStruct((2, share) + plane, F32),
+            out_shape=jax.ShapeDtypeStruct((4, share) + strip, F32),
             compiler_params=params(),
             cost_estimate=cost(4.0 * share / levels),
             name="inverse_fourier",
         )(where, inverse, *synths)
-        parts.append((begin, both, lax.ppermute(both[1], "band", peer)))
+        far = lax.ppermute(both[1] + lax.ppermute(both[3], "band", peer), "band", across)
+        parts.append((begin, both, lax.ppermute(both[2], "band", peer), far))
     whole = others
-    for begin, both, theirs in parts:
-        whole = finish(begin, share, both, theirs, whole)
+    for begin, both, theirs, far in parts:
+        whole = finish(begin, share, both, theirs, far, whole)
     return whole
 
 

time: 366 us -> 297 us (0.81)
  Pallas kernels: 297 us -> 183 us
  waiting for transfers between devices: 6.01 us -> 63.8 us
  local copies, waits for them, and re-layouts: 22.2 us -> 15.5 us
  other arithmetic: 5.17 us -> 1.19 us
    pallas_call x8, Pallas kernels: 165 us -> 103 us  [the longest x4 57.2 us: body(): call(where, *operands, squares, rates, *sums)]
    pallas_call x4, Pallas kernels: 106 us -> 55.9 us  [body(): call(where, firsts, locals_, alpha, start, deficit, mu, spectrum)]
    ppermute x3 -> x9, waiting for transfers between devices: 2.55 us -> 41.7 us  [the longest x2 26.5 us: body(): lax.ppermute(both[1] + lax.ppermute(both[3], 'band', peer), 'band', across)]
    ppermute x20, waiting for transfers between devices: 2.12 us -> 22.1 us  [chip_move(): return lax.ppermute(value, 'band', ends)]
    another operation x13 -> x11, local copies, waits for them, and re-layouts: 8.42 us -> 1.74 us  [the longest x10 1.11 us: body(): jnp.stack(by_wave, axis=-1).reshape(reach // 2, 2, GROUP).transpose(1, 0, 2)]
    concatenate x8 -> x4, other arithmetic: 4.18 us -> 0.12 us  [chip_sum(): jnp.concatenate([part, near], axis=0)]
    slice x9 -> x15, local copies, waits for them, and re-layouts: 4.32 us -> 0.32 us  [the longest x10 0.18 us: body(): jnp.roll(padded[w:w + reach].reshape(reach // 16, GROUP, 2), w, axis=1)]
    ppermute x3 -> x9, starting transfers between devices: 7.48 us -> 8.01 us  [the longest x2 4.96 us: body(): lax.ppermute(both[3], 'band', peer)]
  transfers between devices with their start and end apart: 25 -> 31, of which waited for: 4 -> 12; matrix products, arithmetic and copies ran while one was open for 4% -> 3% of each run, Pallas kernels for 67% -> 43%
where the time goes in v2:
time: 297 us; the launch traced here: 294 us
  Pallas kernels  183 us (62%)
  waiting for transfers between devices  63.8 us (21%)
  starting transfers between devices  30.1 us (10%)
  local copies, waits for them, and re-layouts  15.5 us (5%)
    pallas_call x4, Pallas kernels, body(): call(where, *operands, squares, rates, *sums)  57.2 us
    pallas_call x4, Pallas kernels, body(): call(where, firsts, locals_, alpha, start, deficit, mu, spectrum)  55.9 us
    ppermute x2, waiting for transfers between devices, body(): lax.ppermute(both[1] + lax.ppermute(both[3], 'band', peer), 'band', across)  26.5 us
    pallas_call x1, Pallas kernels, others_call(): pl.pallas_call(other_fields_kernel, grid=(last - first,), in_specs=[pl.Bl...  25.7 us
    ppermute x20, waiting for transfers between devices, chip_move(): return lax.ppermute(value, 'band', ends)  22.1 us
    ppermute x20, starting transfers between devices, chip_move(): return lax.ppermute(value, 'band', ends)  20.1 us
    pallas_call x2, Pallas kernels, body(): pl.pallas_call(inverse_kernel, grid_spec=pltpu.PrefetchScalarGridSpec(num...  14 us
    pallas_call x2, Pallas kernels, finish(): pl.pallas_call(finish_kernel, grid_spec=pltpu.PrefetchScalarGridSpec(num_...  10.3 us
  transfers between devices with their start and end apart: 31, of which 12 were waited for; matrix products, arithmetic and copies ran while one was open for 3% of the time, Pallas kernels for 43%

profile of v2, /device:TPU:15, one launch (start us, length us, event | category | flops | bytes accessed | tf_op | source)
XLA Modules:
  0.0 294.4 jit_solution(17849558895214109915)
XLA Ops:
  2.5 1.9 collective-permute-start
  11.6 9.9 %first_field.1 = (f32[6,128,1024]{2,1,0:T(8,128)}, f32[6,128,512]{2,1,0:T(8,128)}, f32[6,128,512]{2,1,0:T(8,128)}) custom-call(s32[5]{0:T(128)} %stack.50.where.place, f32[7,6,128,1024]{3,2,1,0:T(8,128)} %cells.3, f32[6,2,1024]{2,1,0:T(2,128)} %reshape.56.edge, f32[128,1024]{1,0:T(8,128)} %lon.3, f32[128,1024]{1,0:T(8,128)} %lat.3, ...), custom_call_target="tpu_custom_call" | custom-call | tf_op jit(solution)/shard_map/first_field/pallas_call | solution.py:624
  22.7 25.7 %other_fields.1.whole = f32[7,6,128,1024]{3,2,1,0:T(8,128)} custom-call(f32[7,6,128,1024]{3,2,1,0:T(8,128)} %cells.3, f32[36,2,1024]{2,1,0:T(2,128)} %copy-done.27, f32[128,1024]{1,0:T(8,128)} %lon.3, f32[128,1024]{1,0:T(8,128)} %lat.3, f32[2,1024]{1,0:T(2,128)} %slice.189.courant_edge), custom_call_target="tpu_custom_call" | custom-call | flops 28000000000 | bytes 1048576 | tf_op jit(solution)/shard_map/other_fields/pallas_call | solution.py:656
  48.4 9.8 %collective-permute-done.2.two = f32[6,128,512]{2,1,0:T(8,128)S(1)} collective-permute-done((f32[6,128,512]{2,1,0:T(8,128)}, f32[6,128,512]{2,1,0:T(8,128)S(1)}, u32[]{:S(2)}, u32[]{:S(2)}) %collective-permute-start.2) | collective-permute-done | bytes 1572896 | tf_op jit(solution)/shard_map/ppermute | solution.py:685
  59.0 3.0 %collective-permute-done.4.four = f32[6,128,512]{2,1,0:T(8,128)S(1)} collective-permute-done((f32[6,128,512]{2,1,0:T(8,128)S(1)}, f32[6,128,512]{2,1,0:T(8,128)S(1)}, u32[]{:S(2)}, u32[]{:S(2)}) %collective-permute-start.4) | collective-permute-done | bytes 1572896 | tf_op jit(solution)/shard_map/ppermute | solution.py:688
  63.2 10.3 %forward_fourier.1 = (f32[6,128,512]{2,1,0:T(8,128)}, f32[6,128,512]{2,1,0:T(8,128)}, f32[6,128,512]{2,1,0:T(8,128)}, f32[6,128,512]{2,1,0:T(8,128)}) custom-call(s32[5]{0:T(128)} %stack.50.where.place, bf16[16,1024,512]{2,1,0:T(8,128)(2,1)} %constant.111.clone.table, f32[6,128,512]{2,1,0:T(8,128)} %get-tuple-element.94.one, f32[6,128,512]{2,1,0:T(8,128)} %copy-done.19, ...), custom_call_target="tpu_custom_call" | custom-call | flops 8000000000 | bytes 1048576 | tf_op jit(solution)/shard_map/forward_fourier/pallas_call | solution.py:698
  73.5 13.9 %analysis.4 = (f32[2,432,128]{2,1,0:T(8,128)}, f32[2,432,128]{2,1,0:T(8,128)}) custom-call(s32[5]{0:T(128)} %stack.50.where.place, s32[36]{0:T(128)} %constant.115.clone.firsts, s32[36]{0:T(128)} %constant.116.clone.locals_, f32[2,36,8,128]{3,2,1,0:T(8,128)} %constant.118.clone.alpha, f32[4,64,256]{2,1,0:T(8,128)} %constant.119.clone.start, ...), custom_call_target="tpu_custom_call" | custom-call | flops 17999998976 | bytes 1048576 | tf_op jit(solution)/shard_map/analysis/pallas_call | solution.py:757
  87.6 14.0 %analysis.5 = (f32[2,432,128]{2,1,0:T(8,128)}, f32[2,432,128]{2,1,0:T(8,128)}) custom-call(s32[5]{0:T(128)} %stack.50.where.place, s32[36]{0:T(128)} %constant.115.clone.firsts, s32[36]{0:T(128)} %constant.116.clone.locals_, f32[2,36,8,128]{3,2,1,0:T(8,128)} %constant.123.clone.alpha, f32[4,64,256]{2,1,0:T(8,128)} %constant.124.clone.start, ...), custom_call_target="tpu_custom_call" | custom-call | flops 17999998976 | bytes 1048576 | tf_op jit(solution)/shard_map/analysis/pallas_call | solution.py:757
  103.2 14.0 %analysis.6 = (f32[2,432,128]{2,1,0:T(8,128)}, f32[2,432,128]{2,1,0:T(8,128)}) custom-call(s32[5]{0:T(128)} %stack.50.where.place, s32[36]{0:T(128)} %constant.115.clone.firsts, s32[36]{0:T(128)} %constant.116.clone.locals_, f32[2,36,8,128]{3,2,1,0:T(8,128)} %constant.128.clone.alpha, f32[4,64,256]{2,1,0:T(8,128)} %constant.129.clone.start, ...), custom_call_target="tpu_custom_call" | custom-call | flops 17999998976 | bytes 1048576 | tf_op jit(solution)/shard_map/analysis/pallas_call | solution.py:757
  117.4 2.4 collective-permute-start.8
  121.3 14.0 %analysis.7 = (f32[2,432,128]{2,1,0:T(8,128)}, f32[2,432,128]{2,1,0:T(8,128)}) custom-call(s32[5]{0:T(128)} %stack.50.where.place, s32[36]{0:T(128)} %constant.115.clone.firsts, s32[36]{0:T(128)} %constant.116.clone.locals_, f32[2,36,8,128]{3,2,1,0:T(8,128)} %constant.133.clone.alpha, f32[4,64,256]{2,1,0:T(8,128)} %constant.134.clone.start, ...), custom_call_target="tpu_custom_call" | custom-call | flops 17999998976 | bytes 1048576 | tf_op jit(solution)/shard_map/analysis/pallas_call | solution.py:757
  139.1 4.0 %collective-permute-done.11.next_quarter = f32[1,432,128]{2,1,0:T(8,128)S(1)} collective-permute-done((f32[1,432,128]{2,1,0:T(8,128)S(1)}, f32[1,432,128]{2,1,0:T(8,128)S(1)}, u32[]{:S(2)}, u32[]{:S(2)}) %collective-permute-start.11) | collective-permute-done | bytes 221216 | tf_op jit(solution)/shard_map/ppermute | solution.py:550
  143.1 2.3 collective-permute-done.12
  145.4 5.3 %collective-permute-done.13 = f32[1,432,128]{2,1,0:T(8,128)S(1)} collective-permute-done((f32[1,432,128]{2,1,0:T(8,128)S(1)}, f32[1,432,128]{2,1,0:T(8,128)S(1)}, u32[]{:S(2)}, u32[]{:S(2)}) %collective-permute-start.13) | collective-permute-done | bytes 221216 | tf_op jit(solution)/shard_map/ppermute | solution.py:550
  156.0 3.0 %collective-permute-done.16.next_quarter = f32[1,432,128]{2,1,0:T(8,128)S(1)} collective-permute-done((f32[1,432,128]{2,1,0:T(8,128)S(1)}, f32[1,432,128]{2,1,0:T(8,128)S(1)}, u32[]{:S(2)}, u32[]{:S(2)}) %collective-permute-start.16) | collective-permute-done | bytes 221216 | tf_op jit(solution)/shard_map/ppermute | solution.py:550
  159.1 1.7 collective-permute-done.17
  160.8 5.7 %collective-permute-done.18 = f32[1,432,128]{2,1,0:T(8,128)S(1)} collective-permute-done((f32[1,432,128]{2,1,0:T(8,128)S(1)}, f32[1,432,128]{2,1,0:T(8,128)S(1)}, u32[]{:S(2)}, u32[]{:S(2)}) %collective-permute-start.18) | collective-permute-done | bytes 221216 | tf_op jit(solution)/shard_map/ppermute | solution.py:550
  166.6 2.3 collective-permute-start.20
  171.2 14.4 %synthesis.4.refs_0_ = f32[6,128,512]{2,1,0:T(8,128)} custom-call(s32[5]{0:T(128)} %stack.50.where.place, s32[36]{0:T(128)} %constant.115.clone.firsts, s32[36]{0:T(128)} %constant.116.clone.locals_, s32[36]{0:T(128)} %constant.117.clone.degrees, f32[2,36,8,128]{3,2,1,0:T(8,128)} %constant.118.clone.alpha, f32[4,64,256]{2,1,0:T(8,128)} %constant.119.clone.start, ...), custom_call_target="tpu_custom_call" | custom-call | flops 17999998976 | bytes 1048576 | tf_op jit(solution)/shard_map/synthesis/pallas_call | solution.py:793
  187.2 14.3 %synthesis.5.refs_1_ = f32[6,128,512]{2,1,0:T(8,128)} custom-call(s32[5]{0:T(128)} %stack.50.where.place, s32[36]{0:T(128)} %constant.115.clone.firsts, s32[36]{0:T(128)} %constant.116.clone.locals_, s32[36]{0:T(128)} %constant.122.clone.degrees, f32[2,36,8,128]{3,2,1,0:T(8,128)} %constant.123.clone.alpha, f32[4,64,256]{2,1,0:T(8,128)} %constant.124.clone.start, ...), custom_call_target="tpu_custom_call" | custom-call | flops 17999998976 | bytes 1048576 | tf_op jit(solution)/shard_map/synthesis/pallas_call | solution.py:793
  201.6 1.5 collective-permute-start.24
  203.1 14.2 %synthesis.6.refs_2_ = f32[6,128,512]{2,1,0:T(8,128)} custom-call(s32[5]{0:T(128)} %stack.50.where.place, s32[36]{0:T(128)} %constant.115.clone.firsts, s32[36]{0:T(128)} %constant.116.clone.locals_, s32[36]{0:T(128)} %constant.127.clone.degrees, f32[2,36,8,128]{3,2,1,0:T(8,128)} %constant.128.clone.alpha, f32[4,64,256]{2,1,0:T(8,128)} %constant.129.clone.start, ...), custom_call_target="tpu_custom_call" | custom-call | flops 17999998976 | bytes 1048576 | tf_op jit(solution)/shard_map/synthesis/pallas_call | solution.py:793
  218.1 14.2 %synthesis.7.refs_3_ = f32[6,128,512]{2,1,0:T(8,128)} custom-call(s32[5]{0:T(128)} %stack.50.where.place, s32[36]{0:T(128)} %constant.115.clone.firsts, s32[36]{0:T(128)} %constant.116.clone.locals_, s32[36]{0:T(128)} %constant.132.clone.degrees, f32[2,36,8,128]{3,2,1,0:T(8,128)} %constant.133.clone.alpha, f32[4,64,256]{2,1,0:T(8,128)} %constant.134.clone.start, ...), custom_call_target="tpu_custom_call" | custom-call | flops 17999998976 | bytes 1048576 | tf_op jit(solution)/shard_map/synthesis/pallas_call | solution.py:793
  232.4 6.8 %inverse_fourier.3.mine = f32[4,3,128,512]{3,2,1,0:T(8,128)} custom-call(s32[5]{0:T(128)} %stack.50.where.place, bf16[16,1024,512]{2,1,0:T(8,128)(2,1)} %constant.112.clone.table, f32[6,128,512]{2,1,0:T(8,128)} %synthesis.4.refs_0_, f32[6,128,512]{2,1,0:T(8,128)} %synthesis.5.refs_1_, f32[6,128,512]{2,1,0:T(8,128)} %synthesis.6.refs_2_, ...), custom_call_target="tpu_custom_call" | custom-call | flops 2000000000 | bytes 1048576 | tf_op jit(solution)/shard_map/inverse_fourier/pallas_call | solution.py:823
  239.2 7.1 %inverse_fourier.2.mine = f32[4,3,128,512]{3,2,1,0:T(8,128)} custom-call(s32[5]{0:T(128)} %stack.50.where.place, bf16[16,1024,512]{2,1,0:T(8,128)(2,1)} %constant.112.clone.table, f32[6,128,512]{2,1,0:T(8,128)} %synthesis.4.refs_0_, f32[6,128,512]{2,1,0:T(8,128)} %synthesis.5.refs_1_, f32[6,128,512]{2,1,0:T(8,128)} %synthesis.6.refs_2_, ...), custom_call_target="tpu_custom_call" | custom-call | flops 2000000000 | bytes 1048576 | tf_op jit(solution)/shard_map/inverse_fourier/pallas_call | solution.py:823
  246.5 3.2 %collective-permute-start.29 = (f32[3,128,512]{2,1,0:T(8,128)S(1)}, f32[3,128,512]{2,1,0:T(8,128)S(1)}, u32[]{:S(2)}, u32[]{:S(2)}) collective-permute-start(f32[3,128,512]{2,1,0:T(8,128)S(1)} %get-tuple-element.173), channel_id=1, source_target_pairs={{0,1},{1,0},{2,3},{3,2},{4,5},{5,4},{6,7},{7,6},{8,9},{9,8},{10,11... | collective-permute-start | bytes 2359304 | tf_op jit(solution)/shard_map/ppermute | solution.py:840
  249.9 1.8 collective-permute-start.26
  254.1 1.6 collective-permute-done.28.theirs
  255.8 15.7 %collective-permute-done.30.far = f32[3,128,512]{2,1,0:T(8,128)S(1)} collective-permute-done((f32[3,128,512]{2,1,0:T(8,128)S(1)}, f32[3,128,512]{2,1,0:T(8,128)S(1)}, u32[]{:S(2)}, u32[]{:S(2)}) %collective-permute-start.30) | collective-permute-done | bytes 786464 | tf_op jit(solution)/shard_map/ppermute | solution.py:840
  272.3 5.1 %finish.2.whole = f32[7,6,128,1024]{3,2,1,0:T(8,128)} custom-call(s32[5]{0:T(128)} %stack.50.where.place, bf16[256,256]{1,0:T(8,128)(2,1)} %constant.110.clone.flip, f32[6,128,1024]{2,1,0:T(8,128)} %get-tuple-element.89.moved, f32[4,3,128,512]{3,2,1,0:T(8,128)} %inverse_fourier.3.mine, f32[3,128,512]{2,1,0:T(8,128)} %copy-done.7, ...), custom_call_target="tpu_custom_call", output_to_operand_aliasing={{}: (6, {})} | custom-call | flops 2000000000 | bytes 1048576 | tf_op jit(solution)/shard_map/finish/pallas_call | solution.py:798
  277.5 10.8 %collective-permute-done.27.far = f32[3,128,512]{2,1,0:T(8,128)S(1)} collective-permute-done((f32[3,128,512]{2,1,0:T(8,128)S(1)}, f32[3,128,512]{2,1,0:T(8,128)S(1)}, u32[]{:S(2)}, u32[]{:S(2)}) %collective-permute-start.27) | collective-permute-done | bytes 786464 | tf_op jit(solution)/shard_map/ppermute | solution.py:840
  289.3 5.2 %finish.3 = f32[7,6,128,1024]{3,2,1,0:T(8,128)} custom-call(s32[5]{0:T(128)} %stack.50.where.place, bf16[256,256]{1,0:T(8,128)(2,1)} %constant.110.clone.flip, f32[6,128,1024]{2,1,0:T(8,128)} %get-tuple-element.89.moved, f32[4,3,128,512]{3,2,1,0:T(8,128)} %inverse_fourier.2.mine, f32[3,128,512]{2,1,0:T(8,128)} %copy-done.6, ...), custom_call_target="tpu_custom_call", output_to_operand_aliasing={{}: (6, {})} | custom-call | flops 2000000000 | bytes 1048576 | tf_op jit(solution)/shard_map/finish/pallas_call | solution.py:798
  (172 shorter events, 34.5 us)
Async XLA Ops:
  2.5 7.8 %collective-permute-start = (f32[14,1024]{1,0:T(8,128)S(1)}, f32[14,1024]{1,0:T(8,128)S(1)}, u32[]{:S(2)}, u32[]{:S(2)}) collective-permute-start(f32[14,1024]{1,0:T(8,128)S(1)} %pad_maximum_fusion.4), channel_id=1, source_target_pairs={{0,1},{1,2},{2,3},{3,4},{4,5},{5,6},{6,7},{7,8},{8,9},{9,10},{10,1... | collective-permute-start | bytes 172040 | tf_op jit(solution)/shard_map/ppermute | solution.py:616
  5.8 16.1 %collective-permute-start.1 = (f32[36,2,1024]{2,1,0:T(2,128)S(1)}, f32[36,2,1024]{2,1,0:T(2,128)S(1)}, u32[]{:S(2)}, u32[]{:S(2)}) collective-permute-start(f32[36,2,1024]{2,1,0:T(2,128)S(1)} %bitcast.46), channel_id=1, source_target_pairs={{0,1},{1,2},{2,3},{3,4},{4,5},{5,6},{6,7},{7,8},{8,9},{9,10},{10,1... | collective-permute-start | bytes 884744 | tf_op jit(solution)/shard_map/ppermute | solution.py:650
  21.5 37.5 %collective-permute-start.3 = (f32[6,128,512]{2,1,0:T(8,128)}, f32[6,128,512]{2,1,0:T(8,128)S(1)}, u32[]{:S(2)}, u32[]{:S(2)}) collective-permute-start(f32[6,128,512]{2,1,0:T(8,128)} %get-tuple-element.94.one), channel_id=1, source_target_pairs={{0,1},{1,0},{2,3},{3,2},{4,5},{5,4},{6,7},{7,6},{8,9},{9,8},{10,11... | collective-permute-start | bytes 4718600 | tf_op jit(solution)/shard_map/ppermute | solution.py:647
  22.0 36.2 %collective-permute-start.2 = (f32[6,128,512]{2,1,0:T(8,128)}, f32[6,128,512]{2,1,0:T(8,128)S(1)}, u32[]{:S(2)}, u32[]{:S(2)}) collective-permute-start(f32[6,128,512]{2,1,0:T(8,128)} %get-tuple-element.92), channel_id=1, source_target_pairs={{0,2},{1,3},{2,0},{3,1},{4,6},{5,7},{6,4},{7,5},{8,10},{9,11},{10,... | collective-permute-start | bytes 4718600 | tf_op jit(solution)/shard_map/ppermute | solution.py:685
  58.1 3.9 %collective-permute-start.4 = (f32[6,128,512]{2,1,0:T(8,128)S(1)}, f32[6,128,512]{2,1,0:T(8,128)S(1)}, u32[]{:S(2)}, u32[]{:S(2)}) collective-permute-start(f32[6,128,512]{2,1,0:T(8,128)S(1)} %collective-permute-done.2.two), channel_id=1, source_target_pairs={{0,1},{1,0},{2,3},{3,2},{4,5},{5,4},{6,7},{7,6},{8,9},{9,8},{10,11... | collective-permute-start | bytes 4718600 | tf_op jit(solution)/shard_map/ppermute | solution.py:688
  87.4 14.3 %collective-permute-start.5 = (f32[2,432,128]{2,1,0:T(8,128)}, f32[2,432,128]{2,1,0:T(8,128)S(1)}, u32[]{:S(2)}, u32[]{:S(2)}) collective-permute-start(f32[2,432,128]{2,1,0:T(8,128)} %get-tuple-element.103), channel_id=1, source_target_pairs={{0,2},{1,3},{2,0},{3,1},{4,6},{5,7},{6,4},{7,5},{8,10},{9,11},{10,... | collective-permute-start | bytes 1327112 | tf_op jit(solution)/shard_map/ppermute | solution.py:550
  101.8 15.4 %collective-permute-start.6 = (f32[1,432,128]{2,1,0:T(8,128)S(1)}, f32[1,432,128]{2,1,0:T(8,128)S(1)}, u32[]{:S(2)}, u32[]{:S(2)}) collective-permute-start(f32[1,432,128]{2,1,0:T(8,128)S(1)} %slice.205), channel_id=1, source_target_pairs={{0,4},{1,5},{2,6},{3,7},{4,0},{5,1},{6,2},{7,3},{8,12},{9,13},{10,... | collective-permute-start | bytes 663560 | tf_op jit(solution)/shard_map/ppermute | solution.py:550
  102.0 15.2 %collective-permute-start.7 = (f32[2,432,128]{2,1,0:T(8,128)}, f32[2,432,128]{2,1,0:T(8,128)S(1)}, u32[]{:S(2)}, u32[]{:S(2)}) collective-permute-start(f32[2,432,128]{2,1,0:T(8,128)} %get-tuple-element.111), channel_id=1, source_target_pairs={{0,2},{1,3},{2,0},{3,1},{4,6},{5,7},{6,4},{7,5},{8,10},{9,11},{10,... | collective-permute-start | bytes 1327112 | tf_op jit(solution)/shard_map/ppermute | solution.py:550
  117.4 17.9 %collective-permute-start.8 = (f32[1,432,128]{2,1,0:T(8,128)S(1)}, f32[1,432,128]{2,1,0:T(8,128)S(1)}, u32[]{:S(2)}, u32[]{:S(2)}) collective-permute-start(f32[1,432,128]{2,1,0:T(8,128)S(1)} %slice_add_fusion.3), channel_id=1, source_target_pairs={{0,8},{1,9},{2,10},{3,11},{4,12},{5,13},{6,14},{7,15},{8,0},{9,1},... | collective-permute-start | bytes 663560 | tf_op jit(solution)/shard_map/ppermute | solution.py:550
  119.7 15.5 %collective-permute-start.9 = (f32[1,432,128]{2,1,0:T(8,128)S(1)}, f32[1,432,128]{2,1,0:T(8,128)S(1)}, u32[]{:S(2)}, u32[]{:S(2)}) collective-permute-start(f32[1,432,128]{2,1,0:T(8,128)S(1)} %slice.206), channel_id=1, source_target_pairs={{0,4},{1,5},{2,6},{3,7},{4,0},{5,1},{6,2},{7,3},{8,12},{9,13},{10,... | collective-permute-start | bytes 663560 | tf_op jit(solution)/shard_map/ppermute | solution.py:550
  119.9 15.3 %collective-permute-start.10 = (f32[2,432,128]{2,1,0:T(8,128)S(1)}, f32[2,432,128]{2,1,0:T(8,128)S(1)}, u32[]{:S(2)}, u32[]{:S(2)}) collective-permute-start(f32[2,432,128]{2,1,0:T(8,128)S(1)} %copy-done.23), channel_id=1, source_target_pairs={{0,2},{1,3},{2,0},{3,1},{4,6},{5,7},{6,4},{7,5},{8,10},{9,11},{10,... | collective-permute-start | bytes 1327112 | tf_op jit(solution)/shard_map/ppermute | solution.py:550
  136.3 14.4 %collective-permute-start.14 = (f32[2,432,128]{2,1,0:T(8,128)S(1)}, f32[2,432,128]{2,1,0:T(8,128)S(1)}, u32[]{:S(2)}, u32[]{:S(2)}) collective-permute-start(f32[2,432,128]{2,1,0:T(8,128)S(1)} %copy-done.22), channel_id=1, source_target_pairs={{0,2},{1,3},{2,0},{3,1},{4,6},{5,7},{6,4},{7,5},{8,10},{9,11},{10,... | collective-permute-start | bytes 1327112 | tf_op jit(solution)/shard_map/ppermute | solution.py:550
  136.5 6.7 %collective-permute-start.11 = (f32[1,432,128]{2,1,0:T(8,128)S(1)}, f32[1,432,128]{2,1,0:T(8,128)S(1)}, u32[]{:S(2)}, u32[]{:S(2)}) collective-permute-start(f32[1,432,128]{2,1,0:T(8,128)S(1)} %add.77.own_quarter), channel_id=1, source_target_pairs={{0,4},{1,5},{2,6},{3,7},{4,0},{5,1},{6,2},{7,3},{8,12},{9,13},{10,... | collective-permute-start | bytes 663560 | tf_op jit(solution)/shard_map/ppermute | solution.py:550
  137.7 7.7 %collective-permute-start.12 = (f32[1,432,128]{2,1,0:T(8,128)S(1)}, f32[1,432,128]{2,1,0:T(8,128)S(1)}, u32[]{:S(2)}, u32[]{:S(2)}) collective-permute-start(f32[1,432,128]{2,1,0:T(8,128)S(1)} %slice_add_fusion.2), channel_id=1, source_target_pairs={{0,8},{1,9},{2,10},{3,11},{4,12},{5,13},{6,14},{7,15},{8,0},{9,1},... | collective-permute-start | bytes 663560 | tf_op jit(solution)/shard_map/ppermute | solution.py:550
  137.8 12.9 %collective-permute-start.13 = (f32[1,432,128]{2,1,0:T(8,128)S(1)}, f32[1,432,128]{2,1,0:T(8,128)S(1)}, u32[]{:S(2)}, u32[]{:S(2)}) collective-permute-start(f32[1,432,128]{2,1,0:T(8,128)S(1)} %slice.208), channel_id=1, source_target_pairs={{0,4},{1,5},{2,6},{3,7},{4,0},{5,1},{6,2},{7,3},{8,12},{9,13},{10,... | collective-permute-start | bytes 663560 | tf_op jit(solution)/shard_map/ppermute | solution.py:550
  150.9 15.5 %collective-permute-start.15 = (f32[2,432,128]{2,1,0:T(8,128)S(1)}, f32[2,432,128]{2,1,0:T(8,128)S(1)}, u32[]{:S(2)}, u32[]{:S(2)}) collective-permute-start(f32[2,432,128]{2,1,0:T(8,128)S(1)} %pad_maximum_fusion), channel_id=1, source_target_pairs={{0,2},{1,3},{2,0},{3,1},{4,6},{5,7},{6,4},{7,5},{8,10},{9,11},{10,... | collective-permute-start | bytes 1327112 | tf_op jit(solution)/shard_map/ppermute | solution.py:550
  151.9 7.2 %collective-permute-start.16 = (f32[1,432,128]{2,1,0:T(8,128)S(1)}, f32[1,432,128]{2,1,0:T(8,128)S(1)}, u32[]{:S(2)}, u32[]{:S(2)}) collective-permute-start(f32[1,432,128]{2,1,0:T(8,128)S(1)} %add.80.own_quarter), channel_id=1, source_target_pairs={{0,4},{1,5},{2,6},{3,7},{4,0},{5,1},{6,2},{7,3},{8,12},{9,13},{10,... | collective-permute-start | bytes 663560 | tf_op jit(solution)/shard_map/ppermute | solution.py:550
  153.3 7.5 %collective-permute-start.17 = (f32[1,432,128]{2,1,0:T(8,128)S(1)}, f32[1,432,128]{2,1,0:T(8,128)S(1)}, u32[]{:S(2)}, u32[]{:S(2)}) collective-permute-start(f32[1,432,128]{2,1,0:T(8,128)S(1)} %slice_add_fusion.1), channel_id=1, source_target_pairs={{0,8},{1,9},{2,10},{3,11},{4,12},{5,13},{6,14},{7,15},{8,0},{9,1},... | collective-permute-start | bytes 663560 | tf_op jit(solution)/shard_map/ppermute | solution.py:550
  153.7 12.7 %collective-permute-start.18 = (f32[1,432,128]{2,1,0:T(8,128)S(1)}, f32[1,432,128]{2,1,0:T(8,128)S(1)}, u32[]{:S(2)}, u32[]{:S(2)}) collective-permute-start(f32[1,432,128]{2,1,0:T(8,128)S(1)} %slice.210), channel_id=1, source_target_pairs={{0,4},{1,5},{2,6},{3,7},{4,0},{5,1},{6,2},{7,3},{8,12},{9,13},{10,... | collective-permute-start | bytes 663560 | tf_op jit(solution)/shard_map/ppermute | solution.py:550
  159.1 26.5 %copy-start.15 = (f32[1,432,128]{2,1,0:T(8,128)}, f32[1,432,128]{2,1,0:T(8,128)S(1)}, u32[]{:S(2)}) copy-start(f32[1,432,128]{2,1,0:T(8,128)S(1)} %collective-permute-done.16.next_quarter) | copy-start | bytes 663556
  166.6 19.0 %collective-permute-start.20 = (f32[1,432,128]{2,1,0:T(8,128)S(1)}, f32[1,432,128]{2,1,0:T(8,128)S(1)}, u32[]{:S(2)}, u32[]{:S(2)}) collective-permute-start(f32[1,432,128]{2,1,0:T(8,128)S(1)} %add.83.own_quarter), channel_id=1, source_target_pairs={{0,4},{1,5},{2,6},{3,7},{4,0},{5,1},{6,2},{7,3},{8,12},{9,13},{10,... | collective-permute-start | bytes 663560 | tf_op jit(solution)/shard_map/ppermute | solution.py:550
  168.8 16.8 %collective-permute-start.21 = (f32[1,432,128]{2,1,0:T(8,128)S(1)}, f32[1,432,128]{2,1,0:T(8,128)S(1)}, u32[]{:S(2)}, u32[]{:S(2)}) collective-permute-start(f32[1,432,128]{2,1,0:T(8,128)S(1)} %slice_add_fusion), channel_id=1, source_target_pairs={{0,8},{1,9},{2,10},{3,11},{4,12},{5,13},{6,14},{7,15},{8,0},{9,1},... | collective-permute-start | bytes 663560 | tf_op jit(solution)/shard_map/ppermute | solution.py:550
  169.7 15.9 %collective-permute-start.19 = (f32[2,432,128]{2,1,0:T(8,128)S(1)}, f32[2,432,128]{2,1,0:T(8,128)S(1)}, u32[]{:S(2)}, u32[]{:S(2)}) collective-permute-start(f32[2,432,128]{2,1,0:T(8,128)S(1)} %pad_maximum_fusion.1), channel_id=1, source_target_pairs={{0,2},{1,3},{2,0},{3,1},{4,6},{5,7},{6,4},{7,5},{8,10},{9,11},{10,... | collective-permute-start | bytes 1327112 | tf_op jit(solution)/shard_map/ppermute | solution.py:550
  185.7 15.8 %collective-permute-start.23 = (f32[1,432,128]{2,1,0:T(8,128)S(1)}, f32[1,432,128]{2,1,0:T(8,128)S(1)}, u32[]{:S(2)}, u32[]{:S(2)}) collective-permute-start(f32[1,432,128]{2,1,0:T(8,128)S(1)} %add.85.own_quarter), channel_id=1, source_target_pairs={{0,4},{1,5},{2,6},{3,7},{4,0},{5,1},{6,2},{7,3},{8,12},{9,13},{10,... | collective-permute-start | bytes 663560 | tf_op jit(solution)/shard_map/ppermute | solution.py:550
  187.2 14.3 %collective-permute-start.22 = (f32[2,432,128]{2,1,0:T(8,128)S(1)}, f32[2,432,128]{2,1,0:T(8,128)S(1)}, u32[]{:S(2)}, u32[]{:S(2)}) collective-permute-start(f32[2,432,128]{2,1,0:T(8,128)S(1)} %pad_maximum_fusion.2), channel_id=1, source_target_pairs={{0,2},{1,3},{2,0},{3,1},{4,6},{5,7},{6,4},{7,5},{8,10},{9,11},{10,... | collective-permute-start | bytes 1327112 | tf_op jit(solution)/shard_map/ppermute | solution.py:550
  201.6 15.8 %collective-permute-start.24 = (f32[2,432,128]{2,1,0:T(8,128)S(1)}, f32[2,432,128]{2,1,0:T(8,128)S(1)}, u32[]{:S(2)}, u32[]{:S(2)}) collective-permute-start(f32[2,432,128]{2,1,0:T(8,128)S(1)} %pad_maximum_fusion.3), channel_id=1, source_target_pairs={{0,2},{1,3},{2,0},{3,1},{4,6},{5,7},{6,4},{7,5},{8,10},{9,11},{10,... | collective-permute-start | bytes 1327112 | tf_op jit(solution)/shard_map/ppermute | solution.py:550
  246.5 5.6 %collective-permute-start.29 = (f32[3,128,512]{2,1,0:T(8,128)S(1)}, f32[3,128,512]{2,1,0:T(8,128)S(1)}, u32[]{:S(2)}, u32[]{:S(2)}) collective-permute-start(f32[3,128,512]{2,1,0:T(8,128)S(1)} %get-tuple-element.173), channel_id=1, source_target_pairs={{0,1},{1,0},{2,3},{3,2},{4,5},{5,4},{6,7},{7,6},{8,9},{9,8},{10,11... | collective-permute-start | bytes 2359304 | tf_op jit(solution)/shard_map/ppermute | solution.py:840
  249.9 3.7 %collective-permute-start.26 = (f32[3,128,512]{2,1,0:T(8,128)S(1)}, f32[3,128,512]{2,1,0:T(8,128)S(1)}, u32[]{:S(2)}, u32[]{:S(2)}) collective-permute-start(f32[3,128,512]{2,1,0:T(8,128)S(1)} %get-tuple-element.175), channel_id=1, source_target_pairs={{0,1},{1,0},{2,3},{3,2},{4,5},{5,4},{6,7},{7,6},{8,9},{9,8},{10,11... | collective-permute-start | bytes 2359304 | tf_op jit(solution)/shard_map/ppermute | solution.py:840
  251.6 25.9 %collective-permute-start.25 = (f32[3,128,512]{2,1,0:T(8,128)S(1)}, f32[3,128,512]{2,1,0:T(8,128)S(1)}, u32[]{:S(2)}, u32[]{:S(2)}) collective-permute-start(f32[3,128,512]{2,1,0:T(8,128)S(1)} %get-tuple-element.176), channel_id=1, source_target_pairs={{0,1},{1,0},{2,3},{3,2},{4,5},{5,4},{6,7},{7,6},{8,9},{9,8},{10,11... | collective-permute-start | bytes 2359304 | tf_op jit(solution)/shard_map/ppermute | solution.py:841
  251.7 4.1 %collective-permute-start.28 = (f32[3,128,512]{2,1,0:T(8,128)S(1)}, f32[3,128,512]{2,1,0:T(8,128)S(1)}, u32[]{:S(2)}, u32[]{:S(2)}) collective-permute-start(f32[3,128,512]{2,1,0:T(8,128)S(1)} %get-tuple-element.174), channel_id=1, source_target_pairs={{0,1},{1,0},{2,3},{3,2},{4,5},{5,4},{6,7},{7,6},{8,9},{9,8},{10,11... | collective-permute-start | bytes 2359304 | tf_op jit(solution)/shard_map/ppermute | solution.py:841
  252.3 19.2 %collective-permute-start.30 = (f32[3,128,512]{2,1,0:T(8,128)S(1)}, f32[3,128,512]{2,1,0:T(8,128)S(1)}, u32[]{:S(2)}, u32[]{:S(2)}) collective-permute-start(f32[3,128,512]{2,1,0:T(8,128)S(1)} %fusion), channel_id=1, source_target_pairs={{0,2},{1,3},{2,0},{3,1},{4,6},{5,7},{6,4},{7,5},{8,10},{9,11},{10,... | collective-permute-start | bytes 2359304 | tf_op jit(solution)/shard_map/ppermute | solution.py:840
  253.7 34.6 %collective-permute-start.27 = (f32[3,128,512]{2,1,0:T(8,128)S(1)}, f32[3,128,512]{2,1,0:T(8,128)S(1)}, u32[]{:S(2)}, u32[]{:S(2)}) collective-permute-start(f32[3,128,512]{2,1,0:T(8,128)S(1)} %fusion.1), channel_id=1, source_target_pairs={{0,2},{1,3},{2,0},{3,1},{4,6},{5,7},{6,4},{7,5},{8,10},{9,11},{10,... | collective-permute-start | bytes 2359304 | tf_op jit(solution)/shard_map/ppermute | solution.py:840
  (27 other events, 244.9 us)

commit v3 on v2

--- a/solution.py
+++ b/solution.py
@@ -586,7 +586,7 @@
     return pl.CostEstimate(flops=int(micros * 1e9), bytes_accessed=1 << 20, transcendentals=0)
 
 
-def params(limit=56):
+def params(limit):
     return pltpu.CompilerParams(vmem_limit_bytes=limit << 20)
 
 
@@ -640,7 +640,7 @@
         ),
         out_shape=[jax.ShapeDtypeStruct((levels,) + plane, F32)]
         + [jax.ShapeDtypeStruct((levels,) + strip, F32)] * 2,
-        compiler_params=params(),
+        compiler_params=params(56),
         name="first_field",
     )(where, state, first_edge, courant_lon, courant_lat, courant_edge, reference_field, flip)
     across = [(i, i ^ 2) for i in range(band_count)]
@@ -665,7 +665,7 @@
             ],
             out_specs=pl.BlockSpec((1, levels) + plane, at),
             out_shape=jax.ShapeDtypeStruct(state.shape, F32),
-            compiler_params=params(),
+            compiler_params=params(56),
             cost_estimate=cost(28.0),
             name="other_fields",
         )(*operands)
@@ -706,7 +706,7 @@
             out_specs=[pl.BlockSpec((1, e - b, share_lat), lambda l, w: (l, 0, 0)) for b, e in cuts],
         ),
         out_shape=[jax.ShapeDtypeStruct((levels, e - b, share_lat), F32) for b, e in cuts],
-        compiler_params=params(),
+        compiler_params=params(20),
         cost_estimate=cost(8.0),
         name="forward_fourier",
     )(where, forward, keep, far_keep, peer_keep, peer_far, quad)
@@ -748,7 +748,7 @@
                 + buffers,
             ),
             out_shape=[jax.ShapeDtypeStruct((2, rows, 128), F32)] * 2,
-            compiler_params=params(),
+            compiler_params=params(20),
             cost_estimate=cost(0.5 * count),
             name="analysis",
         )
@@ -783,7 +783,7 @@
                 scratch_shapes=[pltpu.VMEM((4, rows, 128), F32)] + buffers,
             ),
             out_shape=jax.ShapeDtypeStruct(shape, F32),
-            compiler_params=params(),
+            compiler_params=params(20),
             cost_estimate=cost(0.5 * count),
             name="synthesis",
         )
@@ -812,7 +812,7 @@
             ),
             out_shape=jax.ShapeDtypeStruct(state.shape, F32),
             input_output_aliases={6: 0},
-            compiler_params=params(),
+            compiler_params=params(20),
             cost_estimate=cost(2.0),
             name="finish",
         )(where, flip, moved, both, theirs, far, whole)
@@ -833,7 +833,7 @@
                 out_specs=pl.BlockSpec((4, 1) + strip, lambda l, w: (0, l, 0, 0)),
             ),
             out_shape=jax.ShapeDtypeStruct((4, share) + strip, F32),
-            compiler_params=params(),
+            compiler_params=params(20),
             cost_estimate=cost(4.0 * share / levels),
             name="inverse_fourier",
         )(where, inverse, *synths)

time: 297 us -> 275 us (0.926)
  Pallas kernels: 183 us -> 149 us
  local copies, waits for them, and re-layouts: 15.5 us -> 21.9 us
  waiting for transfers between devices: 63.8 us -> 67.4 us
  other arithmetic: 1.19 us -> 4.75 us
    pallas_call x4, Pallas kernels: 57.2 us -> 46.7 us  [body(): call(where, *operands, squares, rates, *sums)]
    pallas_call x4, Pallas kernels: 55.9 us -> 47.5 us  [body(): call(where, firsts, locals_, alpha, start, deficit, mu, spectrum)]
    pallas_call x2, Pallas kernels: 14 us -> 7.36 us  [body(): pl.pallas_call(inverse_kernel, grid_spec=pltpu.PrefetchScalarGridSpec(num...]
    unnamed x56 -> x82, local copies, waits for them, and re-layouts: 5.19 us -> 9.96 us
    pallas_call x2, Pallas kernels: 10.3 us -> 5.56 us  [finish(): pl.pallas_call(finish_kernel, grid_spec=pltpu.PrefetchScalarGridSpec(num_...]
    pallas_call x1, Pallas kernels: 10.3 us -> 6.46 us  [body(): pl.pallas_call(functools.partial(forward_kernel, cuts), grid_spec=pltpu.P...]
    ppermute x2, waiting for transfers between devices: 26.5 us -> 29.7 us  [body(): lax.ppermute(both[1] + lax.ppermute(both[3], 'band', peer), 'band', across)]
  transfers between devices with their start and end apart: 31 -> 31, of which waited for: 12 -> 13; matrix products, arithmetic and copies ran while one was open for 3% -> 3% of each run, Pallas kernels for 43% -> 40%
where the time goes in v3:
time: 275 us; the launch traced here: 273 us
  Pallas kernels  149 us (54%)
  waiting for transfers between devices  67.4 us (25%)
  starting transfers between devices  28.7 us (10%)
  local copies, waits for them, and re-layouts  21.9 us (8%)
  other arithmetic  4.75 us (2%)
    pallas_call x4, Pallas kernels, body(): call(where, firsts, locals_, alpha, start, deficit, mu, spectrum)  47.5 us
    pallas_call x4, Pallas kernels, body(): call(where, *operands, squares, rates, *sums)  46.7 us
    ppermute x2, waiting for transfers between devices, body(): lax.ppermute(both[1] + lax.ppermute(both[3], 'band', peer), 'band', across)  29.7 us
    pallas_call x1, Pallas kernels, others_call(): pl.pallas_call(other_fields_kernel, grid=(last - first,), in_specs=[pl.Bl...  25.8 us
    ppermute x20, waiting for transfers between devices, chip_move(): return lax.ppermute(value, 'band', ends)  21.8 us
    ppermute x20, starting transfers between devices, chip_move(): return lax.ppermute(value, 'band', ends)  20.1 us
    unnamed x82, local copies, waits for them, and re-layouts  9.96 us
    pallas_call x1, Pallas kernels, body(): pl.pallas_call(first_field_kernel, grid_spec=pltpu.PrefetchScalarGridSpec...  9.88 us
  transfers between devices with their start and end apart: 31, of which 13 were waited for; matrix products, arithmetic and copies ran while one was open for 3% of the time, Pallas kernels for 40%

profile of v3, /device:TPU:15, one launch (start us, length us, event | category | flops | bytes accessed | tf_op | source)
XLA Modules:
  0.0 272.9 jit_solution(16623203912783929688)
XLA Ops:
  2.5 1.9 collective-permute-start
  12.3 9.9 %first_field.1 = (f32[6,128,1024]{2,1,0:T(8,128)}, f32[6,128,512]{2,1,0:T(8,128)}, f32[6,128,512]{2,1,0:T(8,128)}) custom-call(s32[5]{0:T(128)} %stack.50.where.place, f32[7,6,128,1024]{3,2,1,0:T(8,128)} %cells.3, f32[6,2,1024]{2,1,0:T(2,128)} %reshape.56.edge, f32[128,1024]{1,0:T(8,128)} %lon.3, f32[128,1024]{1,0:T(8,128)} %lat.3, ...), custom_call_target="tpu_custom_call" | custom-call | tf_op jit(solution)/shard_map/first_field/pallas_call | solution.py:624
  23.4 25.8 %other_fields.1.whole = f32[7,6,128,1024]{3,2,1,0:T(8,128)} custom-call(f32[7,6,128,1024]{3,2,1,0:T(8,128)} %cells.3, f32[36,2,1024]{2,1,0:T(2,128)} %copy-done.36, f32[128,1024]{1,0:T(8,128)} %lon.3, f32[128,1024]{1,0:T(8,128)} %lat.3, f32[2,1024]{1,0:T(2,128)} %slice.189.courant_edge), custom_call_target="tpu_custom_call" | custom-call | flops 28000000000 | bytes 1048576 | tf_op jit(solution)/shard_map/other_fields/pallas_call | solution.py:656
  49.2 9.7 %collective-permute-done.2.two = f32[6,128,512]{2,1,0:T(8,128)S(1)} collective-permute-done((f32[6,128,512]{2,1,0:T(8,128)}, f32[6,128,512]{2,1,0:T(8,128)S(1)}, u32[]{:S(2)}, u32[]{:S(2)}) %collective-permute-start.2) | collective-permute-done | bytes 1572896 | tf_op jit(solution)/shard_map/ppermute | solution.py:685
  59.7 3.0 %collective-permute-done.4.four = f32[6,128,512]{2,1,0:T(8,128)S(1)} collective-permute-done((f32[6,128,512]{2,1,0:T(8,128)S(1)}, f32[6,128,512]{2,1,0:T(8,128)S(1)}, u32[]{:S(2)}, u32[]{:S(2)}) %collective-permute-start.4) | collective-permute-done | bytes 1572896 | tf_op jit(solution)/shard_map/ppermute | solution.py:688
  62.8 5.8 %copy-done.4 = bf16[16,1024,512]{2,1,0:T(8,128)(2,1)S(1)} copy-done((bf16[16,1024,512]{2,1,0:T(8,128)(2,1)S(1)}, bf16[16,1024,512]{2,1,0:T(8,128)(2,1)}, u32[]{:S(2)}) %copy-start.4) | copy-done | bytes 16777240
  68.5 6.5 %forward_fourier.1 = (f32[6,128,512]{2,1,0:T(8,128)S(1)}, f32[6,128,512]{2,1,0:T(8,128)S(1)}, f32[6,128,512]{2,1,0:T(8,128)S(1)}, f32[6,128,512]{2,1,0:T(8,128)S(1)}) custom-call(s32[5]{0:T(128)S(1)} %copy-done.2, bf16[16,1024,512]{2,1,0:T(8,128)(2,1)S(1)} %copy-done.4, f32[6,128,512]{2,1,0:T(8,128)S(1)} %copy-done.3, ...), custom_call_target="tpu_custom_call" | custom-call | flops 8000000000 | bytes 1048576 | tf_op jit(solution)/shard_map/forward_fourier/pallas_call | solution.py:698
  75.1 11.9 %analysis.4 = (f32[2,432,128]{2,1,0:T(8,128)S(1)}, f32[2,432,128]{2,1,0:T(8,128)S(1)}) custom-call(s32[5]{0:T(128)S(1)} %copy-done.2, s32[36]{0:T(128)S(1)} %copy-done.30, s32[36]{0:T(128)S(1)} %copy-done.29, f32[2,36,8,128]{3,2,1,0:T(8,128)S(1)} %copy-done.12, f32[4,64,256]{2,1,0:T(8,128)S(1)} %copy-done.25, f32[4,64,256]{2,1,0:T(8,128)S(1)} %copy-done.23, ...), custom_call_target="tpu_custom_call" | custom-call | flops 17999998976 | bytes 1048576 | tf_op jit(solution)/shard_map/analysis/pallas_call | solution.py:757
  87.3 11.9 %analysis.5 = (f32[2,432,128]{2,1,0:T(8,128)S(1)}, f32[2,432,128]{2,1,0:T(8,128)S(1)}) custom-call(s32[5]{0:T(128)S(1)} %copy-done.2, s32[36]{0:T(128)S(1)} %copy-done.30, s32[36]{0:T(128)S(1)} %copy-done.29, f32[2,36,8,128]{3,2,1,0:T(8,128)S(1)} %copy-done.11, f32[4,64,256]{2,1,0:T(8,128)S(1)} %copy-done.21, f32[4,64,256]{2,1,0:T(8,128)S(1)} %copy-done.19, ...), custom_call_target="tpu_custom_call" | custom-call | flops 17999998976 | bytes 1048576 | tf_op jit(solution)/shard_map/analysis/pallas_call | solution.py:757
  100.8 11.9 %analysis.6 = (f32[2,432,128]{2,1,0:T(8,128)S(1)}, f32[2,432,128]{2,1,0:T(8,128)S(1)}) custom-call(s32[5]{0:T(128)S(1)} %copy-done.2, s32[36]{0:T(128)S(1)} %copy-done.30, s32[36]{0:T(128)S(1)} %copy-done.29, f32[2,36,8,128]{3,2,1,0:T(8,128)S(1)} %copy-done.10, f32[4,64,256]{2,1,0:T(8,128)S(1)} %copy-done.17, f32[4,64,256]{2,1,0:T(8,128)S(1)} %copy-done.15, ...), custom_call_target="tpu_custom_call" | custom-call | flops 17999998976 | bytes 1048576 | tf_op jit(solution)/shard_map/analysis/pallas_call | solution.py:757
  112.9 2.4 collective-permute-start.8
  116.8 11.9 %analysis.7 = (f32[2,432,128]{2,1,0:T(8,128)S(1)}, f32[2,432,128]{2,1,0:T(8,128)S(1)}) custom-call(s32[5]{0:T(128)S(1)} %copy-done.2, s32[36]{0:T(128)S(1)} %copy-done.30, s32[36]{0:T(128)S(1)} %copy-done.29, f32[2,36,8,128]{3,2,1,0:T(8,128)S(1)} %copy-done.9, f32[4,64,256]{2,1,0:T(8,128)S(1)} %copy-done.14, f32[4,64,256]{2,1,0:T(8,128)S(1)} %copy-done.13, ...), custom_call_target="tpu_custom_call" | custom-call | flops 17999998976 | bytes 1048576 | tf_op jit(solution)/shard_map/analysis/pallas_call | solution.py:757
  131.7 4.3 %collective-permute-done.11.next_quarter = f32[1,432,128]{2,1,0:T(8,128)S(1)} collective-permute-done((f32[1,432,128]{2,1,0:T(8,128)S(1)}, f32[1,432,128]{2,1,0:T(8,128)S(1)}, u32[]{:S(2)}, u32[]{:S(2)}) %collective-permute-start.11) | collective-permute-done | bytes 221216 | tf_op jit(solution)/shard_map/ppermute | solution.py:550
  136.0 2.0 collective-permute-done.12
  138.0 5.4 %collective-permute-done.13 = f32[1,432,128]{2,1,0:T(8,128)S(1)} collective-permute-done((f32[1,432,128]{2,1,0:T(8,128)S(1)}, f32[1,432,128]{2,1,0:T(8,128)S(1)}, u32[]{:S(2)}, u32[]{:S(2)}) %collective-permute-start.13) | collective-permute-done | bytes 221216 | tf_op jit(solution)/shard_map/ppermute | solution.py:550
  151.1 2.7 collective-permute-done.16.next_quarter
  153.8 2.6 collective-permute-done.17
  156.4 4.8 %collective-permute-done.18 = f32[1,432,128]{2,1,0:T(8,128)} collective-permute-done((f32[1,432,128]{2,1,0:T(8,128)}, f32[1,432,128]{2,1,0:T(8,128)}, u32[]{:S(2)}, u32[]{:S(2)}) %collective-permute-start.18) | collective-permute-done | bytes 221216 | tf_op jit(solution)/shard_map/ppermute | solution.py:550
  163.4 2.3 collective-permute-start.20
  167.8 1.7 copy-done.8
  171.4 11.8 %synthesis.4.refs_0_ = f32[6,128,512]{2,1,0:T(8,128)S(1)} custom-call(s32[5]{0:T(128)S(1)} %copy-done.2, s32[36]{0:T(128)S(1)} %copy-done.30, s32[36]{0:T(128)S(1)} %copy-done.29, s32[36]{0:T(128)S(1)} %copy-done.34, f32[2,36,8,128]{3,2,1,0:T(8,128)S(1)} %copy-done.12, f32[4,64,256]{2,1,0:T(8,128)S(1)} %copy-done.26, f32[4,64,256]{2,1,0:T(8,128)S(1)} %copy-done.24, ...), custom_call_target="tpu_custom_call" | custom-call | flops 17999998976 | bytes 1048576 | tf_op jit(solution)/shard_map/synthesis/pallas_call | solution.py:793
  185.1 11.6 %synthesis.5.refs_1_ = f32[6,128,512]{2,1,0:T(8,128)S(1)} custom-call(s32[5]{0:T(128)S(1)} %copy-done.2, s32[36]{0:T(128)S(1)} %copy-done.30, s32[36]{0:T(128)S(1)} %copy-done.29, s32[36]{0:T(128)S(1)} %copy-done.33, f32[2,36,8,128]{3,2,1,0:T(8,128)S(1)} %copy-done.11, f32[4,64,256]{2,1,0:T(8,128)S(1)} %copy-done.22, f32[4,64,256]{2,1,0:T(8,128)S(1)} %copy-done.20, ...), custom_call_target="tpu_custom_call" | custom-call | flops 17999998976 | bytes 1048576 | tf_op jit(solution)/shard_map/synthesis/pallas_call | solution.py:793
  198.2 11.6 %synthesis.6.refs_2_ = f32[6,128,512]{2,1,0:T(8,128)S(1)} custom-call(s32[5]{0:T(128)S(1)} %copy-done.2, s32[36]{0:T(128)S(1)} %copy-done.30, s32[36]{0:T(128)S(1)} %copy-done.29, s32[36]{0:T(128)S(1)} %copy-done.32, f32[2,36,8,128]{3,2,1,0:T(8,128)S(1)} %copy-done.10, f32[4,64,256]{2,1,0:T(8,128)S(1)} %copy-done.18, f32[4,64,256]{2,1,0:T(8,128)S(1)} %copy-done.16, ...), custom_call_target="tpu_custom_call" | custom-call | flops 17999998976 | bytes 1048576 | tf_op jit(solution)/shard_map/synthesis/pallas_call | solution.py:793
  209.8 11.6 %synthesis.7.refs_3_ = f32[6,128,512]{2,1,0:T(8,128)S(1)} custom-call(s32[5]{0:T(128)S(1)} %copy-done.2, s32[36]{0:T(128)S(1)} %copy-done.30, s32[36]{0:T(128)S(1)} %copy-done.29, s32[36]{0:T(128)S(1)} %copy-done.31, f32[2,36,8,128]{3,2,1,0:T(8,128)S(1)} %copy-done.9, f32[4,64,256]{2,1,0:T(8,128)S(1)} %copy-done.14, f32[4,64,256]{2,1,0:T(8,128)S(1)} %copy-done.13, ...), custom_call_target="tpu_custom_call" | custom-call | flops 17999998976 | bytes 1048576 | tf_op jit(solution)/shard_map/synthesis/pallas_call | solution.py:793
  221.5 3.7 %inverse_fourier.3.mine = f32[4,3,128,512]{3,2,1,0:T(8,128)S(1)} custom-call(s32[5]{0:T(128)S(1)} %copy-done.2, bf16[16,1024,512]{2,1,0:T(8,128)(2,1)S(1)} %bitcast.44, f32[6,128,512]{2,1,0:T(8,128)S(1)} %synthesis.4.refs_0_, f32[6,128,512]{2,1,0:T(8,128)S(1)} %synthesis.5.refs_1_, f32[6,128,512]{2,1,0:T(8,128)S(1)} %synthesis.6.refs_2_, ...), custom_call_target="tpu_custom_call" | custom-call | flops 2000000000 | bytes 1048576 | tf_op jit(solution)/shard_map/inverse_fourier/pallas_call | solution.py:823
  225.2 3.7 %inverse_fourier.2.mine = f32[4,3,128,512]{3,2,1,0:T(8,128)S(1)} custom-call(s32[5]{0:T(128)S(1)} %copy-done.2, bf16[16,1024,512]{2,1,0:T(8,128)(2,1)S(1)} %bitcast.44, f32[6,128,512]{2,1,0:T(8,128)S(1)} %synthesis.4.refs_0_, f32[6,128,512]{2,1,0:T(8,128)S(1)} %synthesis.5.refs_1_, f32[6,128,512]{2,1,0:T(8,128)S(1)} %synthesis.6.refs_2_, ...), custom_call_target="tpu_custom_call" | custom-call | flops 2000000000 | bytes 1048576 | tf_op jit(solution)/shard_map/inverse_fourier/pallas_call | solution.py:823
  229.0 3.4 %collective-permute-start.29 = (f32[3,128,512]{2,1,0:T(8,128)S(1)}, f32[3,128,512]{2,1,0:T(8,128)S(1)}, u32[]{:S(2)}, u32[]{:S(2)}) collective-permute-start(f32[3,128,512]{2,1,0:T(8,128)S(1)} %get-tuple-element.173), channel_id=1, source_target_pairs={{0,1},{1,0},{2,3},{3,2},{4,5},{5,4},{6,7},{7,6},{8,9},{9,8},{10,11... | collective-permute-start | bytes 2359304 | tf_op jit(solution)/shard_map/ppermute | solution.py:840
  236.2 1.5 collective-permute-done.28.theirs
  237.7 15.6 %collective-permute-done.30.far = f32[3,128,512]{2,1,0:T(8,128)S(1)} collective-permute-done((f32[3,128,512]{2,1,0:T(8,128)S(1)}, f32[3,128,512]{2,1,0:T(8,128)S(1)}, u32[]{:S(2)}, u32[]{:S(2)}) %collective-permute-start.30) | collective-permute-done | bytes 786464 | tf_op jit(solution)/shard_map/ppermute | solution.py:840
  253.3 2.8 %finish.2.whole = f32[7,6,128,1024]{3,2,1,0:T(8,128)} custom-call(s32[5]{0:T(128)S(1)} %copy-done.2, bf16[256,256]{1,0:T(8,128)(2,1)S(1)} %copy-done.1, f32[6,128,1024]{2,1,0:T(8,128)S(1)} %copy-done, f32[4,3,128,512]{3,2,1,0:T(8,128)S(1)} %inverse_fourier.3.mine, f32[3,128,512]{2,1,0:T(8,128)S(1)} %collective-permute-done.28.theirs, ...), custom_call_target="tpu_custom_call", output_to_operand_aliasing={{}: (6, {})} | custom-call | flops 2000000000 | bytes 1048576 | tf_op jit(solution)/shard_map/finish/pallas_call | solution.py:798
  256.1 14.1 %collective-permute-done.27.far = f32[3,128,512]{2,1,0:T(8,128)S(1)} collective-permute-done((f32[3,128,512]{2,1,0:T(8,128)S(1)}, f32[3,128,512]{2,1,0:T(8,128)S(1)}, u32[]{:S(2)}, u32[]{:S(2)}) %collective-permute-start.27) | collective-permute-done | bytes 786464 | tf_op jit(solution)/shard_map/ppermute | solution.py:840
  270.1 2.8 %finish.3 = f32[7,6,128,1024]{3,2,1,0:T(8,128)} custom-call(s32[5]{0:T(128)S(1)} %copy-done.2, bf16[256,256]{1,0:T(8,128)(2,1)S(1)} %copy-done.1, f32[6,128,1024]{2,1,0:T(8,128)S(1)} %copy-done, f32[4,3,128,512]{3,2,1,0:T(8,128)S(1)} %inverse_fourier.2.mine, f32[3,128,512]{2,1,0:T(8,128)S(1)} %collective-permute-done.25.theirs, ...), custom_call_target="tpu_custom_call", output_to_operand_aliasing={{}: (6, {})} | custom-call | flops 2000000000 | bytes 1048576 | tf_op jit(solution)/shard_map/finish/pallas_call | solution.py:798
  (199 shorter events, 39.7 us)
Async XLA Ops:
  2.5 8.5 %collective-permute-start = (f32[14,1024]{1,0:T(8,128)S(1)}, f32[14,1024]{1,0:T(8,128)S(1)}, u32[]{:S(2)}, u32[]{:S(2)}) collective-permute-start(f32[14,1024]{1,0:T(8,128)S(1)} %pad_maximum_fusion.4), channel_id=1, source_target_pairs={{0,1},{1,2},{2,3},{3,4},{4,5},{5,6},{6,7},{7,8},{8,9},{9,10},{10,1... | collective-permute-start | bytes 172040 | tf_op jit(solution)/shard_map/ppermute | solution.py:616
  5.8 16.8 %collective-permute-start.1 = (f32[36,2,1024]{2,1,0:T(2,128)S(1)}, f32[36,2,1024]{2,1,0:T(2,128)S(1)}, u32[]{:S(2)}, u32[]{:S(2)}) collective-permute-start(f32[36,2,1024]{2,1,0:T(2,128)S(1)} %bitcast.48), channel_id=1, source_target_pairs={{0,1},{1,2},{2,3},{3,4},{4,5},{5,6},{6,7},{7,8},{8,9},{9,10},{10,1... | collective-permute-start | bytes 884744 | tf_op jit(solution)/shard_map/ppermute | solution.py:650
  22.1 37.6 %collective-permute-start.3 = (f32[6,128,512]{2,1,0:T(8,128)}, f32[6,128,512]{2,1,0:T(8,128)S(1)}, u32[]{:S(2)}, u32[]{:S(2)}) collective-permute-start(f32[6,128,512]{2,1,0:T(8,128)} %get-tuple-element.94.one), channel_id=1, source_target_pairs={{0,1},{1,0},{2,3},{3,2},{4,5},{5,4},{6,7},{7,6},{8,9},{9,8},{10,11... | collective-permute-start | bytes 4718600 | tf_op jit(solution)/shard_map/ppermute | solution.py:647
  22.6 36.3 %collective-permute-start.2 = (f32[6,128,512]{2,1,0:T(8,128)}, f32[6,128,512]{2,1,0:T(8,128)S(1)}, u32[]{:S(2)}, u32[]{:S(2)}) collective-permute-start(f32[6,128,512]{2,1,0:T(8,128)} %get-tuple-element.92), channel_id=1, source_target_pairs={{0,2},{1,3},{2,0},{3,1},{4,6},{5,7},{6,4},{7,5},{8,10},{9,11},{10,... | collective-permute-start | bytes 4718600 | tf_op jit(solution)/shard_map/ppermute | solution.py:685
  23.3 51.7 %copy-start.29 = (s32[36]{0:T(128)S(1)}, s32[36]{0:T(128)}, u32[]{:S(2)}) copy-start(s32[36]{0:T(128)} %constant.116.clone.locals_) | copy-start | bytes 436
  58.9 3.9 %collective-permute-start.4 = (f32[6,128,512]{2,1,0:T(8,128)S(1)}, f32[6,128,512]{2,1,0:T(8,128)S(1)}, u32[]{:S(2)}, u32[]{:S(2)}) collective-permute-start(f32[6,128,512]{2,1,0:T(8,128)S(1)} %collective-permute-done.2.two), channel_id=1, source_target_pairs={{0,1},{1,0},{2,3},{3,2},{4,5},{5,4},{6,7},{7,6},{8,9},{9,8},{10,11... | collective-permute-start | bytes 4718600 | tf_op jit(solution)/shard_map/ppermute | solution.py:688
  87.0 12.2 %collective-permute-start.5 = (f32[2,432,128]{2,1,0:T(8,128)S(1)}, f32[2,432,128]{2,1,0:T(8,128)S(1)}, u32[]{:S(2)}, u32[]{:S(2)}) collective-permute-start(f32[2,432,128]{2,1,0:T(8,128)S(1)} %get-tuple-element.103), channel_id=1, source_target_pairs={{0,2},{1,3},{2,0},{3,1},{4,6},{5,7},{6,4},{7,5},{8,10},{9,11},{10,... | collective-permute-start | bytes 1327112 | tf_op jit(solution)/shard_map/ppermute | solution.py:550
  99.3 13.4 %collective-permute-start.6 = (f32[1,432,128]{2,1,0:T(8,128)S(1)}, f32[1,432,128]{2,1,0:T(8,128)S(1)}, u32[]{:S(2)}, u32[]{:S(2)}) collective-permute-start(f32[1,432,128]{2,1,0:T(8,128)S(1)} %slice.205), channel_id=1, source_target_pairs={{0,4},{1,5},{2,6},{3,7},{4,0},{5,1},{6,2},{7,3},{8,12},{9,13},{10,... | collective-permute-start | bytes 663560 | tf_op jit(solution)/shard_map/ppermute | solution.py:550
  99.5 13.2 %collective-permute-start.7 = (f32[2,432,128]{2,1,0:T(8,128)S(1)}, f32[2,432,128]{2,1,0:T(8,128)S(1)}, u32[]{:S(2)}, u32[]{:S(2)}) collective-permute-start(f32[2,432,128]{2,1,0:T(8,128)S(1)} %get-tuple-element.111), channel_id=1, source_target_pairs={{0,2},{1,3},{2,0},{3,1},{4,6},{5,7},{6,4},{7,5},{8,10},{9,11},{10,... | collective-permute-start | bytes 1327112 | tf_op jit(solution)/shard_map/ppermute | solution.py:550
  112.9 15.8 %collective-permute-start.8 = (f32[1,432,128]{2,1,0:T(8,128)S(1)}, f32[1,432,128]{2,1,0:T(8,128)S(1)}, u32[]{:S(2)}, u32[]{:S(2)}) collective-permute-start(f32[1,432,128]{2,1,0:T(8,128)S(1)} %slice_add_fusion.3), channel_id=1, source_target_pairs={{0,8},{1,9},{2,10},{3,11},{4,12},{5,13},{6,14},{7,15},{8,0},{9,1},... | collective-permute-start | bytes 663560 | tf_op jit(solution)/shard_map/ppermute | solution.py:550
  115.2 13.4 %collective-permute-start.9 = (f32[1,432,128]{2,1,0:T(8,128)S(1)}, f32[1,432,128]{2,1,0:T(8,128)S(1)}, u32[]{:S(2)}, u32[]{:S(2)}) collective-permute-start(f32[1,432,128]{2,1,0:T(8,128)S(1)} %slice.206), channel_id=1, source_target_pairs={{0,4},{1,5},{2,6},{3,7},{4,0},{5,1},{6,2},{7,3},{8,12},{9,13},{10,... | collective-permute-start | bytes 663560 | tf_op jit(solution)/shard_map/ppermute | solution.py:550
  115.3 13.4 %collective-permute-start.10 = (f32[2,432,128]{2,1,0:T(8,128)S(1)}, f32[2,432,128]{2,1,0:T(8,128)S(1)}, u32[]{:S(2)}, u32[]{:S(2)}) collective-permute-start(f32[2,432,128]{2,1,0:T(8,128)S(1)} %get-tuple-element.122), channel_id=1, source_target_pairs={{0,2},{1,3},{2,0},{3,1},{4,6},{5,7},{6,4},{7,5},{8,10},{9,11},{10,... | collective-permute-start | bytes 1327112 | tf_op jit(solution)/shard_map/ppermute | solution.py:550
  128.9 14.5 %collective-permute-start.14 = (f32[2,432,128]{2,1,0:T(8,128)S(1)}, f32[2,432,128]{2,1,0:T(8,128)S(1)}, u32[]{:S(2)}, u32[]{:S(2)}) collective-permute-start(f32[2,432,128]{2,1,0:T(8,128)S(1)} %get-tuple-element.131), channel_id=1, source_target_pairs={{0,2},{1,3},{2,0},{3,1},{4,6},{5,7},{6,4},{7,5},{8,10},{9,11},{10,... | collective-permute-start | bytes 1327112 | tf_op jit(solution)/shard_map/ppermute | solution.py:550
  129.0 7.0 %collective-permute-start.11 = (f32[1,432,128]{2,1,0:T(8,128)S(1)}, f32[1,432,128]{2,1,0:T(8,128)S(1)}, u32[]{:S(2)}, u32[]{:S(2)}) collective-permute-start(f32[1,432,128]{2,1,0:T(8,128)S(1)} %add.77.own_quarter), channel_id=1, source_target_pairs={{0,4},{1,5},{2,6},{3,7},{4,0},{5,1},{6,2},{7,3},{8,12},{9,13},{10,... | collective-permute-start | bytes 663560 | tf_op jit(solution)/shard_map/ppermute | solution.py:550
  130.3 7.7 %collective-permute-start.12 = (f32[1,432,128]{2,1,0:T(8,128)S(1)}, f32[1,432,128]{2,1,0:T(8,128)S(1)}, u32[]{:S(2)}, u32[]{:S(2)}) collective-permute-start(f32[1,432,128]{2,1,0:T(8,128)S(1)} %slice_add_fusion.2), channel_id=1, source_target_pairs={{0,8},{1,9},{2,10},{3,11},{4,12},{5,13},{6,14},{7,15},{8,0},{9,1},... | collective-permute-start | bytes 663560 | tf_op jit(solution)/shard_map/ppermute | solution.py:550
  130.4 13.0 %collective-permute-start.13 = (f32[1,432,128]{2,1,0:T(8,128)S(1)}, f32[1,432,128]{2,1,0:T(8,128)S(1)}, u32[]{:S(2)}, u32[]{:S(2)}) collective-permute-start(f32[1,432,128]{2,1,0:T(8,128)S(1)} %slice.208), channel_id=1, source_target_pairs={{0,4},{1,5},{2,6},{3,7},{4,0},{5,1},{6,2},{7,3},{8,12},{9,13},{10,... | collective-permute-start | bytes 663560 | tf_op jit(solution)/shard_map/ppermute | solution.py:550
  145.7 15.5 %collective-permute-start.15 = (f32[2,432,128]{2,1,0:T(8,128)}, f32[2,432,128]{2,1,0:T(8,128)S(1)}, u32[]{:S(2)}, u32[]{:S(2)}) collective-permute-start(f32[2,432,128]{2,1,0:T(8,128)} %pad_maximum_fusion), channel_id=1, source_target_pairs={{0,2},{1,3},{2,0},{3,1},{4,6},{5,7},{6,4},{7,5},{8,10},{9,11},{10,... | collective-permute-start | bytes 1327112 | tf_op jit(solution)/shard_map/ppermute | solution.py:550
  146.5 7.3 %collective-permute-start.16 = (f32[1,432,128]{2,1,0:T(8,128)S(1)}, f32[1,432,128]{2,1,0:T(8,128)S(1)}, u32[]{:S(2)}, u32[]{:S(2)}) collective-permute-start(f32[1,432,128]{2,1,0:T(8,128)S(1)} %add.80.own_quarter), channel_id=1, source_target_pairs={{0,4},{1,5},{2,6},{3,7},{4,0},{5,1},{6,2},{7,3},{8,12},{9,13},{10,... | collective-permute-start | bytes 663560 | tf_op jit(solution)/shard_map/ppermute | solution.py:550
  147.9 8.5 %collective-permute-start.17 = (f32[1,432,128]{2,1,0:T(8,128)}, f32[1,432,128]{2,1,0:T(8,128)}, u32[]{:S(2)}, u32[]{:S(2)}) collective-permute-start(f32[1,432,128]{2,1,0:T(8,128)} %slice_add_fusion.1), channel_id=1, source_target_pairs={{0,8},{1,9},{2,10},{3,11},{4,12},{5,13},{6,14},{7,15},{8,0},{9,1},... | collective-permute-start | bytes 663560 | tf_op jit(solution)/shard_map/ppermute | solution.py:550
  148.5 12.7 %collective-permute-start.18 = (f32[1,432,128]{2,1,0:T(8,128)}, f32[1,432,128]{2,1,0:T(8,128)}, u32[]{:S(2)}, u32[]{:S(2)}) collective-permute-start(f32[1,432,128]{2,1,0:T(8,128)} %slice.210), channel_id=1, source_target_pairs={{0,4},{1,5},{2,6},{3,7},{4,0},{5,1},{6,2},{7,3},{8,12},{9,13},{10,... | collective-permute-start | bytes 663560 | tf_op jit(solution)/shard_map/ppermute | solution.py:550
  163.4 19.8 %collective-permute-start.20 = (f32[1,432,128]{2,1,0:T(8,128)S(1)}, f32[1,432,128]{2,1,0:T(8,128)S(1)}, u32[]{:S(2)}, u32[]{:S(2)}) collective-permute-start(f32[1,432,128]{2,1,0:T(8,128)S(1)} %add.83.own_quarter), channel_id=1, source_target_pairs={{0,4},{1,5},{2,6},{3,7},{4,0},{5,1},{6,2},{7,3},{8,12},{9,13},{10,... | collective-permute-start | bytes 663560 | tf_op jit(solution)/shard_map/ppermute | solution.py:550
  165.7 17.6 %collective-permute-start.21 = (f32[1,432,128]{2,1,0:T(8,128)S(1)}, f32[1,432,128]{2,1,0:T(8,128)S(1)}, u32[]{:S(2)}, u32[]{:S(2)}) collective-permute-start(f32[1,432,128]{2,1,0:T(8,128)S(1)} %slice_add_fusion), channel_id=1, source_target_pairs={{0,8},{1,9},{2,10},{3,11},{4,12},{5,13},{6,14},{7,15},{8,0},{9,1},... | collective-permute-start | bytes 663560 | tf_op jit(solution)/shard_map/ppermute | solution.py:550
  166.6 16.6 %collective-permute-start.19 = (f32[2,432,128]{2,1,0:T(8,128)S(1)}, f32[2,432,128]{2,1,0:T(8,128)S(1)}, u32[]{:S(2)}, u32[]{:S(2)}) collective-permute-start(f32[2,432,128]{2,1,0:T(8,128)S(1)} %pad_maximum_fusion.1), channel_id=1, source_target_pairs={{0,2},{1,3},{2,0},{3,1},{4,6},{5,7},{6,4},{7,5},{8,10},{9,11},{10,... | collective-permute-start | bytes 1327112 | tf_op jit(solution)/shard_map/ppermute | solution.py:550
  183.4 13.4 %collective-permute-start.23 = (f32[1,432,128]{2,1,0:T(8,128)S(1)}, f32[1,432,128]{2,1,0:T(8,128)S(1)}, u32[]{:S(2)}, u32[]{:S(2)}) collective-permute-start(f32[1,432,128]{2,1,0:T(8,128)S(1)} %add.85.own_quarter), channel_id=1, source_target_pairs={{0,4},{1,5},{2,6},{3,7},{4,0},{5,1},{6,2},{7,3},{8,12},{9,13},{10,... | collective-permute-start | bytes 663560 | tf_op jit(solution)/shard_map/ppermute | solution.py:550
  184.9 11.9 %collective-permute-start.22 = (f32[2,432,128]{2,1,0:T(8,128)S(1)}, f32[2,432,128]{2,1,0:T(8,128)S(1)}, u32[]{:S(2)}, u32[]{:S(2)}) collective-permute-start(f32[2,432,128]{2,1,0:T(8,128)S(1)} %pad_maximum_fusion.2), channel_id=1, source_target_pairs={{0,2},{1,3},{2,0},{3,1},{4,6},{5,7},{6,4},{7,5},{8,10},{9,11},{10,... | collective-permute-start | bytes 1327112 | tf_op jit(solution)/shard_map/ppermute | solution.py:550
  196.9 12.9 %collective-permute-start.24 = (f32[2,432,128]{2,1,0:T(8,128)S(1)}, f32[2,432,128]{2,1,0:T(8,128)S(1)}, u32[]{:S(2)}, u32[]{:S(2)}) collective-permute-start(f32[2,432,128]{2,1,0:T(8,128)S(1)} %pad_maximum_fusion.3), channel_id=1, source_target_pairs={{0,2},{1,3},{2,0},{3,1},{4,6},{5,7},{6,4},{7,5},{8,10},{9,11},{10,... | collective-permute-start | bytes 1327112 | tf_op jit(solution)/shard_map/ppermute | solution.py:550
  229.0 5.3 %collective-permute-start.29 = (f32[3,128,512]{2,1,0:T(8,128)S(1)}, f32[3,128,512]{2,1,0:T(8,128)S(1)}, u32[]{:S(2)}, u32[]{:S(2)}) collective-permute-start(f32[3,128,512]{2,1,0:T(8,128)S(1)} %get-tuple-element.173), channel_id=1, source_target_pairs={{0,1},{1,0},{2,3},{3,2},{4,5},{5,4},{6,7},{7,6},{8,9},{9,8},{10,11... | collective-permute-start | bytes 2359304 | tf_op jit(solution)/shard_map/ppermute | solution.py:840
  232.6 2.9 %collective-permute-start.26 = (f32[3,128,512]{2,1,0:T(8,128)S(1)}, f32[3,128,512]{2,1,0:T(8,128)S(1)}, u32[]{:S(2)}, u32[]{:S(2)}) collective-permute-start(f32[3,128,512]{2,1,0:T(8,128)S(1)} %get-tuple-element.175), channel_id=1, source_target_pairs={{0,1},{1,0},{2,3},{3,2},{4,5},{5,4},{6,7},{7,6},{8,9},{9,8},{10,11... | collective-permute-start | bytes 2359304 | tf_op jit(solution)/shard_map/ppermute | solution.py:840
  232.7 23.4 %collective-permute-start.25 = (f32[3,128,512]{2,1,0:T(8,128)S(1)}, f32[3,128,512]{2,1,0:T(8,128)S(1)}, u32[]{:S(2)}, u32[]{:S(2)}) collective-permute-start(f32[3,128,512]{2,1,0:T(8,128)S(1)} %get-tuple-element.176), channel_id=1, source_target_pairs={{0,1},{1,0},{2,3},{3,2},{4,5},{5,4},{6,7},{7,6},{8,9},{9,8},{10,11... | collective-permute-start | bytes 2359304 | tf_op jit(solution)/shard_map/ppermute | solution.py:841
  233.2 4.5 %collective-permute-start.28 = (f32[3,128,512]{2,1,0:T(8,128)S(1)}, f32[3,128,512]{2,1,0:T(8,128)S(1)}, u32[]{:S(2)}, u32[]{:S(2)}) collective-permute-start(f32[3,128,512]{2,1,0:T(8,128)S(1)} %get-tuple-element.174), channel_id=1, source_target_pairs={{0,1},{1,0},{2,3},{3,2},{4,5},{5,4},{6,7},{7,6},{8,9},{9,8},{10,11... | collective-permute-start | bytes 2359304 | tf_op jit(solution)/shard_map/ppermute | solution.py:841
  234.5 18.8 %collective-permute-start.30 = (f32[3,128,512]{2,1,0:T(8,128)S(1)}, f32[3,128,512]{2,1,0:T(8,128)S(1)}, u32[]{:S(2)}, u32[]{:S(2)}) collective-permute-start(f32[3,128,512]{2,1,0:T(8,128)S(1)} %fusion), channel_id=1, source_target_pairs={{0,2},{1,3},{2,0},{3,1},{4,6},{5,7},{6,4},{7,5},{8,10},{9,11},{10,... | collective-permute-start | bytes 2359304 | tf_op jit(solution)/shard_map/ppermute | solution.py:840
  235.6 34.6 %collective-permute-start.27 = (f32[3,128,512]{2,1,0:T(8,128)S(1)}, f32[3,128,512]{2,1,0:T(8,128)S(1)}, u32[]{:S(2)}, u32[]{:S(2)}) collective-permute-start(f32[3,128,512]{2,1,0:T(8,128)S(1)} %fusion.1), channel_id=1, source_target_pairs={{0,2},{1,3},{2,0},{3,1},{4,6},{5,7},{6,4},{7,5},{8,10},{9,11},{10,... | collective-permute-start | bytes 2359304 | tf_op jit(solution)/shard_map/ppermute | solution.py:840
  (40 other events, 786.7 us)
